TPU v7x, 32 devices: a whole 2x2x4 slice. The times are simulated.
32 devices in a mesh: seq: 16 (over z, y, core), head: 2 (over x).
Axes of the slice: x: 2, y: 2, z: 4, core: 2. Of those that a mesh axis runs over, the one named last changes fastest.
Arguments:
- hidden_in: bfloat16 [2048, 2048], P('seq'), may hold values from -6 to 6
- attn_gain: float32 [2048], replicated, may hold values from 0.25 to 1.75
- w_query: bfloat16 [2048, 1024], P(None, 'head'), may hold values from -0.125 to 0.125
- w_key: bfloat16 [2048, 256], P(None, 'head'), may hold values from -0.125 to 0.125
- w_value: bfloat16 [2048, 256], P(None, 'head'), may hold values from -0.125 to 0.125
- query_gain: float32 [64], replicated, may hold values from 1 to 12, as said below
- key_gain: float32 [64], replicated, may hold values from 1 to 12, as said below
- w_output: bfloat16 [1024, 2048], P('head'), may hold values from -0.1875 to 0.1875
- prior_keys: bfloat16 [32, 128, 256], P('seq', None, 'head')
- prior_values: bfloat16 [32, 128, 256], P('seq', None, 'head'), may hold values from -6 to 6
- span_order: int32 [32], replicated, may hold values from 0 to 31, as said below
- key_live: int32 [32], replicated, may hold values 0 or 1
- page_table: int32 [16], replicated, may hold values from 0 to 31, as said below
- page_dest: int32 [16], replicated, may hold values from 0 to 15, as said below
Outputs:
- attn_out: float32 [2048, 2048], P('seq', 'head')
- new_keys: bfloat16 [16, 128, 256], P('seq', None, 'head')
- new_values: bfloat16 [16, 128, 256], P('seq', None, 'head')
Inputs may be any that keep to these rules, and one draw needn't show every extreme that they name: span_order holds each block number once. `page_table`: distinct slots; of the 2 slots held by each index of seq (slots i * 2 to i * 2 + 1), exactly 1 are named. `page_dest`: each slot once. `query_gain`: positive. `key_gain`: positive.
All inputs are finite; a program needn't handle non-finite values.
Results may differ from a plain program's by a relative error of at most 0.009.
The roundings to bfloat16 on the way count: a program that leaves them out, or rounds other values in their place, can miss the bound.
Values may be sent and summed in bfloat16 or wider, within the bound.
No kernel may reach another device: no remote copies, remote signals or barrier semaphores. Data moves between devices by JAX's collectives and lax.ppermute only.
A program may use at most 128 MiB of HBM per device.

v0:
```python
import jax
import jax.numpy as jnp
from jax import lax
from jax.sharding import PartitionSpec as P

PAGE = 128
BLOCK = 64


epsilon = 1e-06
masked_score = -1e30


def head_norm(vectors, channel_gain):
    mean_square = jnp.mean(vectors * vectors, axis=-1, keepdims=True)
    return vectors * lax.rsqrt(mean_square + epsilon) * channel_gain


def rotary(vectors, positions):
    half_dim = vectors.shape[-1] // 2
    lanes = jnp.arange(half_dim, dtype=jnp.float32)
    inverse_freq = jnp.power(10000.0, -lanes / half_dim)
    angles = positions.astype(jnp.float32)[:, None] * inverse_freq[None, :]
    cosine = jnp.cos(angles)[:, None, :]
    sine_part = jnp.sin(angles)[:, None, :]
    first_half = vectors[..., :half_dim]
    second_half = vectors[..., half_dim:]
    return jnp.concatenate(
        [
            first_half * cosine - second_half * sine_part,
            second_half * cosine + first_half * sine_part,
        ],
        axis=-1,
    )


def lookup(table, indices):
    entries = jnp.arange(table.shape[0], dtype=jnp.int32)
    match_grid = indices[:, None] == entries[None, :]
    return jnp.sum(jnp.where(match_grid, table[None, :], 0), axis=1)


def locate(table, wanted):
    entries = jnp.arange(table.shape[0], dtype=jnp.int32)
    match_grid = table[None, :] == wanted[:, None]
    return jnp.sum(jnp.where(match_grid, entries[None, :], 0), axis=1)


def attend_block(carried, query_heads, query_pos, key_block, value_block, key_pos, key_ok):
    high_score, weight_sum, accum = carried
    kv_count = query_heads.shape[0]
    head_dim = query_heads.shape[-1]
    key_float = key_block.astype(jnp.float32).reshape(-1, kv_count, head_dim)
    value_float = value_block.astype(jnp.float32).reshape(-1, kv_count, head_dim)
    allowed = key_ok[None, :] & (key_pos[None, :] <= query_pos[:, None])
    scores = jnp.einsum("hgqd,khd->hgqk", query_heads, key_float, precision=lax.Precision.HIGHEST)
    scores = jnp.where(allowed, scores, masked_score)
    new_high = jnp.maximum(high_score, jnp.max(scores, axis=-1))
    weights = jnp.where(allowed, jnp.exp(scores - new_high[..., None]), 0.0)
    factor = jnp.exp(high_score - new_high)
    weight_sum = weight_sum * factor + jnp.sum(weights, axis=-1)
    accum = accum * factor[..., None] + jnp.einsum(
        "hgqk,khd->hgqd", weights, value_float, precision=lax.Precision.HIGHEST
    )
    return (new_high, weight_sum, accum)


def fold_keys(carried, query_heads, query_pos, key_rows, value_rows, key_pos, key_ok):
    total_rows = key_rows.shape[0]
    block_rows = total_rows
    while block_rows > 1024 and block_rows % 2 == 0:
        block_rows = block_rows // 2
    block_count = total_rows // block_rows
    latest = jnp.max(query_pos)

    def visit(state, blocks):
        key_block, value_block, pos_block, ok_block = blocks
        needed = jnp.any(ok_block & (pos_block <= latest))
        updated = lax.cond(
            needed,
            lambda inner: attend_block(
                inner, query_heads, query_pos, key_block, value_block, pos_block, ok_block
            ),
            lambda inner: inner,
            state,
        )
        return (updated, None)

    stacked = (
        key_rows.reshape(block_count, block_rows, -1),
        value_rows.reshape(block_count, block_rows, -1),
        key_pos.reshape(block_count, block_rows),
        key_ok.reshape(block_count, block_rows),
    )
    carried, _ = lax.scan(visit, carried, stacked)
    return carried


def body(
    hidden_in,
    attn_gain,
    w_query,
    w_key,
    w_value,
    query_gain,
    key_gain,
    w_output,
    prior_keys,
    prior_values,
    span_order,
    key_live,
    page_table,
    page_dest,
):
    tok_count = hidden_in.shape[0]
    head_dim = query_gain.shape[0]
    q_local = w_query.shape[1] // head_dim
    kv_local = w_key.shape[1] // head_dim
    group = q_local // kv_local
    lane_width = kv_local * head_dim
    prior_len = page_table.shape[0] * PAGE
    seq_rank = lax.axis_index("seq")
    row_ids = seq_rank * tok_count + jnp.arange(tok_count, dtype=jnp.int32)
    positions = prior_len + lookup(span_order, row_ids // BLOCK) * BLOCK + row_ids % BLOCK
    widened = hidden_in.astype(jnp.float32)
    normed = (
        widened
        * lax.rsqrt(jnp.mean(widened * widened, axis=-1, keepdims=True) + epsilon)
        * attn_gain
    ).astype(jnp.bfloat16)
    queries = jnp.dot(normed, w_query, preferred_element_type=jnp.float32)
    keys_raw = jnp.dot(normed, w_key, preferred_element_type=jnp.float32)
    v_cache = jnp.dot(normed, w_value, preferred_element_type=jnp.float32).astype(jnp.bfloat16)
    q_rotated = rotary(
        head_norm(queries.reshape(tok_count, q_local, head_dim), query_gain), positions
    ) * head_dim ** (-0.5)
    query_heads = q_rotated.reshape(tok_count, kv_local, group, head_dim).transpose(1, 2, 0, 3)
    k_cache = (
        rotary(head_norm(keys_raw.reshape(tok_count, kv_local, head_dim), key_gain), positions)
        .astype(jnp.bfloat16)
        .reshape(tok_count, lane_width)
    )
    start_state = (
        jnp.full((kv_local, group, tok_count), masked_score, jnp.float32),
        jnp.zeros((kv_local, group, tok_count), jnp.float32),
        jnp.zeros((kv_local, group, tok_count, head_dim), jnp.float32),
    )
    own_slots = prior_keys.shape[0]
    kept_slots = own_slots // 2
    slot_ids = seq_rank * own_slots + jnp.arange(own_slots, dtype=jnp.int32)
    used = jnp.any(slot_ids[:, None] == page_table[None, :], axis=1)
    used_rank = jnp.cumsum(used.astype(jnp.int32)) - 1
    kept_index = jnp.arange(kept_slots, dtype=jnp.int32)
    selector = (used[None, :] & (used_rank[None, :] == kept_index[:, None])).astype(jnp.bfloat16)
    packed_keys = jnp.einsum(
        "js,spc->jpc", selector, prior_keys, preferred_element_type=jnp.float32
    ).astype(jnp.bfloat16)
    packed_values = jnp.einsum(
        "js,spc->jpc", selector, prior_values, preferred_element_type=jnp.float32
    ).astype(jnp.bfloat16)
    slots_dev = tok_count // PAGE
    my_slots = seq_rank * slots_dev + jnp.arange(slots_dev, dtype=jnp.int32)
    page_of = locate(page_dest, my_slots)
    wanted_tokens = (page_of[:, None] * PAGE + jnp.arange(PAGE, dtype=jnp.int32)[None, :]).reshape(
        -1
    )
    source_block = locate(span_order, wanted_tokens // BLOCK)
    targets = source_block * BLOCK + wanted_tokens % BLOCK
    empty_pages = (
        jnp.zeros((slots_dev * PAGE, lane_width), jnp.bfloat16),
        jnp.zeros((slots_dev * PAGE, lane_width), jnp.bfloat16),
    )
    key_piece = lax.all_gather(packed_keys, "seq", axis=0, tiled=True)
    value_piece = lax.all_gather(packed_values, "seq", axis=0, tiled=True)
    slot_count = key_piece.shape[0]
    key_ok = jnp.ones((slot_count * PAGE,), dtype=bool)
    key_pos = jnp.full((slot_count * PAGE,), -1, jnp.int32)
    after_pool = fold_keys(
        start_state,
        query_heads,
        positions,
        key_piece.reshape(slot_count * PAGE, lane_width),
        value_piece.reshape(slot_count * PAGE, lane_width),
        key_pos,
        key_ok,
    )
    key_piece = lax.all_gather(k_cache, "seq", axis=0, tiled=True)
    value_piece = lax.all_gather(v_cache, "seq", axis=0, tiled=True)
    piece_rows = key_piece.shape[0]
    piece_ids = jnp.arange(piece_rows, dtype=jnp.int32)
    held_block = lookup(span_order, piece_ids // BLOCK)
    key_pos = prior_len + held_block * BLOCK + piece_ids % BLOCK
    key_ok = lookup(key_live, held_block) > 0
    span_result = fold_keys(
        after_pool, query_heads, positions, key_piece, value_piece, key_pos, key_ok
    )
    key_piece = lax.all_gather(k_cache, "seq", axis=0, tiled=True)
    value_piece = lax.all_gather(v_cache, "seq", axis=0, tiled=True)
    piece_rows = key_piece.shape[0]
    inside = (targets >= 0) & (targets < piece_rows)
    safe_rows = jnp.clip(targets, 0, piece_rows - 1)
    high_score, weight_sum, accum = span_result
    attn_heads = (
        (accum / weight_sum[..., None])
        .transpose(2, 0, 1, 3)
        .reshape(tok_count, q_local * head_dim)
        .astype(jnp.bfloat16)
    )
    partial_out = jnp.dot(attn_heads, w_output, preferred_element_type=jnp.float32)
    attn_out = lax.psum_scatter(partial_out, "head", scatter_dimension=1, tiled=True)
    new_keys = jnp.where(inside[:, None], key_piece[safe_rows], empty_pages[0]).reshape(
        slots_dev, PAGE, lane_width
    )
    new_values = jnp.where(inside[:, None], value_piece[safe_rows], empty_pages[1]).reshape(
        slots_dev, PAGE, lane_width
    )
    return (attn_out, new_keys, new_values)


def solution(mesh):
    return jax.shard_map(
        body,
        mesh=mesh,
        in_specs=(
            P("seq", None),
            P(),
            P(None, "head"),
            P(None, "head"),
            P(None, "head"),
            P(),
            P(),
            P("head", None),
            P("seq", None, "head"),
            P("seq", None, "head"),
            P(),
            P(),
            P(),
            P(),
        ),
        out_specs=(P("seq", "head"), P("seq", None, "head"), P("seq", None, "head")),
        check_vma=False,
    )
```

profile of v0, /device:TPU:0, one launch (start us, length us, event | category | flops | bytes accessed | tf_op | source)
XLA Modules:
  0.0 177.4 jit_solution(12484869760502282061)
XLA Ops:
  7.3 1.4 fusion.42
  10.4 1.2 fusion.25
  11.7 1.3 select_reduce_fusion.2
  17.3 1.6 convolution_convert_fusion
  18.9 1.6 multiply_reduce_fusion.1
  21.6 2.6 %multiply_reduce_fusion = (f32[128,8]{0,1:T(8,128)S(1)}, f32[128,512]{0,1:T(8,128)S(1)}) fusion(bf16[2048,512]{1,0:T(8,128)(2,1)} %param.24, bf16[128,2048]{1,0:T(8,128)(2,1)S(1)} %copy-done.3, f32[2048]{0:T(1024)S(1)} %copy-done.8, f32[128]{0:T(128)S(1)} %add_rsqrt_fusion.2), kind=kOutput, calls=%fused_computation.55 | convolution fusion | flops 269614080 | bytes 2896384 | tf_op jit(solution)/shard_map/dot_general | solution.py:131
  25.0 26.0 %all_gather.16 = bf16[2048,128]{1,0:T(8,128)(2,1)} all-gather(bf16[128,128]{1,0:T(8,128)(2,1)S(1)} %copy.39), channel_id=1, replica_groups=mesh['seq'=16,'head'=2] {'seq'}, dimensions={0}, use_global_device_ids=true | all-gather | bytes 557056 | tf_op jit(solution)/shard_map/all_gather | solution.py:187
  51.0 20.3 %all_gather.17 = bf16[2048,128]{1,0:T(8,128)(2,1)} all-gather(bf16[128,128]{1,0:T(8,128)(2,1)S(1)} %convolution_convert_fusion), channel_id=1, replica_groups=mesh['seq'=16,'head'=2] {'seq'}, dimensions={0}, use_global_device_ids=true | all-gather | bytes 557056 | tf_op jit(solution)/shard_map/all_gather | solution.py:188
  71.3 20.5 %all-gather = bf16[2048,128]{1,0:T(8,128)(2,1)S(1)} all-gather(bf16[128,128]{1,0:T(8,128)(2,1)S(1)} %convert_element_type.71), channel_id=2, replica_groups=mesh['seq'=16,'head'=2] {'seq'}, dimensions={0}, use_global_device_ids=true | all-gather | bytes 557056 | tf_op jit(solution)/shard_map/all_gather | solution.py:173
  92.0 20.7 %all-gather.1 = bf16[2048,128]{1,0:T(8,128)(2,1)} all-gather(bf16[128,128]{1,0:T(8,128)(2,1)} %convert_element_type.76), channel_id=3, replica_groups=mesh['seq'=16,'head'=2] {'seq'}, dimensions={0}, use_global_device_ids=true | all-gather | bytes 557056 | tf_op jit(solution)/shard_map/all_gather | solution.py:174
  112.7 1.2 copy.38
  116.9 12.3 %while.30 = (s32[]{:T(128)}, f32[2,4,128]{2,1,0:T(4,128)S(1)}, f32[2,4,128]{2,1,0:T(4,128)S(1)}, f32[2,4,128,64]{2,3,1,0:T(8,128)}, pred[]{:T(512)}, /*index=5*/...) while((s32[]{:T(128)}, f32[2,4,128]{2,1,0:T(4,128)S(1)}, ...), condition=%wide.region_11.12_spmd, body=%wide.region_6.11_spmd.sunk | while | flops 1620183168 | bytes 17106212 | solution.py:95
  116.9 6.2 %conditional.4 = ((f32[2,4,128]{2,1,0:T(4,128)S(1)}, f32[2,4,128]{2,1,0:T(4,128)S(1)}, f32[2,4,128,64]{2,3,1,0:T(8,128)})) conditional(s32[]{:T(128)} %convert_element_type.113, (f32[2,4,128]{2,1,0:T(4,128)S(1)}, f32[2,4,128]{2,1,0:T(4,128)S(1)}, f32[2,4,128,64]{2,3,1,0:T(8,128)}) %tuple.93, (s32[128]{0:T(128)S(1)}, ...), branch_computations={%region_7.7_spmd, %region_8.10_spmd} | conditional | flops 1620183168 | bytes 17106012 | solution.py:79
  117.0 2.1 %bitcast_reduce_fusion = (f32[2,4,128]{2,1,0:T(4,128)S(1)}, f32[2,1024,4,128]{3,1,2,0:T(8,128)S(1)}) fusion(pred[128]{0:T(512)(128)(4,1)S(1)} %broadcast_compare_fusion, bf16[1024,2,64,1]{0,2,3,1:T(8,128)(2,1)S(1)} %bitcast.114, f32[2,4,128,64]{2,3,1,0:T(8,128)S(1)} %get-tuple-element.291), kind=kOutput, calls=%fused_computation.3 | convolution fusion | flops 807402496 | bytes 4722816 | tf_op jit(solution)/shard_map/while/body/eval_jaxpr/cond/branch_1_fun/hgqd,khd->hgqk/dot_general | solution.py:56
  119.9 2.4 %fusion.10 = f32[2,4,128,64]{2,3,1,0:T(8,128)S(1)} fusion(bf16[1024,2,64,1]{0,2,3,1:T(8,128)(2,1)S(1)} %bitcast.116, f32[2,1024,4,128]{3,1,2,0:T(8,128)S(1)} %get-tuple-element.446, f32[2,4,128]{2,1,0:T(4,128)S(1)} %max.12, pred[128]{0:T(512)(128)(4,1)S(1)} %broadcast_compare_fusion, f32[2,4,128,64]{2,3,1,0:T(8,128)S(1)} %copy-done.4, ...), kind=kOutput, calls=%fused_computation.13 | convolution fusion | flops 808583168 | bytes 4989056 | tf_op jit(solution)/shard_map/while/body/eval_jaxpr/cond/branch_1_fun/hgqk,khd->hgqd/dot_general | solution.py:62
  123.1 6.2 %conditional.4 = ((f32[2,4,128]{2,1,0:T(4,128)S(1)}, f32[2,4,128]{2,1,0:T(4,128)S(1)}, f32[2,4,128,64]{2,3,1,0:T(8,128)})) conditional(s32[]{:T(128)} %convert_element_type.113, (f32[2,4,128]{2,1,0:T(4,128)S(1)}, f32[2,4,128]{2,1,0:T(4,128)S(1)}, f32[2,4,128,64]{2,3,1,0:T(8,128)}) %tuple.93, (s32[128]{0:T(128)S(1)}, ...), branch_computations={%region_7.7_spmd, %region_8.10_spmd} | conditional | flops 1620183168 | bytes 17106012 | solution.py:79
  123.1 2.1 %bitcast_reduce_fusion = (f32[2,4,128]{2,1,0:T(4,128)S(1)}, f32[2,1024,4,128]{3,1,2,0:T(8,128)S(1)}) fusion(pred[128]{0:T(512)(128)(4,1)S(1)} %broadcast_compare_fusion, bf16[1024,2,64,1]{0,2,3,1:T(8,128)(2,1)S(1)} %bitcast.114, f32[2,4,128,64]{2,3,1,0:T(8,128)S(1)} %get-tuple-element.291), kind=kOutput, calls=%fused_computation.3 | convolution fusion | flops 807402496 | bytes 4722816 | tf_op jit(solution)/shard_map/while/body/eval_jaxpr/cond/branch_1_fun/hgqd,khd->hgqk/dot_general | solution.py:56
  126.1 2.4 %fusion.10 = f32[2,4,128,64]{2,3,1,0:T(8,128)S(1)} fusion(bf16[1024,2,64,1]{0,2,3,1:T(8,128)(2,1)S(1)} %bitcast.116, f32[2,1024,4,128]{3,1,2,0:T(8,128)S(1)} %get-tuple-element.446, f32[2,4,128]{2,1,0:T(4,128)S(1)} %max.12, pred[128]{0:T(512)(128)(4,1)S(1)} %broadcast_compare_fusion, f32[2,4,128,64]{2,3,1,0:T(8,128)S(1)} %copy-done.4, ...), kind=kOutput, calls=%fused_computation.13 | convolution fusion | flops 808583168 | bytes 4989056 | tf_op jit(solution)/shard_map/while/body/eval_jaxpr/cond/branch_1_fun/hgqk,khd->hgqd/dot_general | solution.py:62
  129.2 1.2 copy.41
  130.5 1.2 copy.40
  131.7 17.3 %while.31 = (s32[]{:T(128)}, f32[2,4,128]{2,1,0:T(4,128)S(1)}, f32[2,4,128]{2,1,0:T(4,128)S(1)}, f32[2,4,128,64]{2,3,1,0:T(8,128)}, pred[2,1024]{1,0:T(4,128)(4,...) while((s32[]{:T(128)}, f32[2,4,128]{2,1,0:T(4,128)S(1)}, ...), condition=%wide.region_21.22_spmd, body=%wide.region_15.21_spmd.sunk | while | flops 1620448256 | bytes 17650516 | solution.py:95
  131.8 1.3 and_reduce_fusion.2
  133.7 6.7 %conditional.5 = ((f32[2,4,128]{2,1,0:T(4,128)S(1)}, f32[2,4,128]{2,1,0:T(4,128)S(1)}, f32[2,4,128,64]{2,3,1,0:T(8,128)})) conditional(s32[]{:T(128)} %convert_element_type.114, (f32[2,4,128]{2,1,0:T(4,128)S(1)}, f32[2,4,128]{2,1,0:T(4,128)S(1)}, f32[2,4,128,64]{2,3,1,0:T(8,128)}) %tuple.96, (pred[1024]{0:T(1024)(128)(4,1)S(1)}, ...), branch_computations={%region_17.17_spmd, %region_18.20_spmd} | conditional | flops 1620445184 | bytes 17634908 | solution.py:79
  134.2 2.1 %fusion.15 = (f32[2,4,128]{2,1,0:T(4,128)S(1)}, f32[2,1024,4,128]{3,1,2,0:T(8,128)S(1)}) fusion(pred[128,1024]{0,1:T(8,128)(4,1)S(1)} %compare_and_fusion, bf16[1024,2,64,1]{0,2,3,1:T(8,128)(2,1)S(1)} %bitcast.115, f32[2,4,128,64]{2,3,1,0:T(8,128)S(1)} %get-tuple-element.314), kind=kOutput, calls=%fused_computation.23 | convolution fusion | flops 807402496 | bytes 4853760 | tf_op jit(solution)/shard_map/while/body/eval_jaxpr/cond/branch_1_fun/hgqd,khd->hgqk/dot_general | solution.py:56
  137.2 2.5 %fusion.22 = f32[2,4,128,64]{2,3,1,0:T(8,128)S(1)} fusion(bf16[1024,2,64,1]{0,2,3,1:T(8,128)(2,1)S(1)} %bitcast.117, f32[2,1024,4,128]{3,1,2,0:T(8,128)S(1)} %get-tuple-element.450, f32[2,4,128]{2,1,0:T(4,128)S(1)} %max.13, pred[128,1024]{0,1:T(8,128)(4,1)S(1)} %compare_and_fusion, f32[2,4,128,64]{2,3,1,0:T(8,128)S(1)} %copy-done.6, ...), kind=kOutput, calls=%fused_computation.30 | convolution fusion | flops 808583168 | bytes 5120000 | tf_op jit(solution)/shard_map/while/body/eval_jaxpr/cond/branch_1_fun/hgqk,khd->hgqd/dot_general | solution.py:62
  140.4 1.3 and_reduce_fusion.2
  142.4 6.7 %conditional.5 = ((f32[2,4,128]{2,1,0:T(4,128)S(1)}, f32[2,4,128]{2,1,0:T(4,128)S(1)}, f32[2,4,128,64]{2,3,1,0:T(8,128)})) conditional(s32[]{:T(128)} %convert_element_type.114, (f32[2,4,128]{2,1,0:T(4,128)S(1)}, f32[2,4,128]{2,1,0:T(4,128)S(1)}, f32[2,4,128,64]{2,3,1,0:T(8,128)}) %tuple.96, (pred[1024]{0:T(1024)(128)(4,1)S(1)}, ...), branch_computations={%region_17.17_spmd, %region_18.20_spmd} | conditional | flops 1620445184 | bytes 17634908 | solution.py:79
  142.8 2.1 %fusion.15 = (f32[2,4,128]{2,1,0:T(4,128)S(1)}, f32[2,1024,4,128]{3,1,2,0:T(8,128)S(1)}) fusion(pred[128,1024]{0,1:T(8,128)(4,1)S(1)} %compare_and_fusion, bf16[1024,2,64,1]{0,2,3,1:T(8,128)(2,1)S(1)} %bitcast.115, f32[2,4,128,64]{2,3,1,0:T(8,128)S(1)} %get-tuple-element.314), kind=kOutput, calls=%fused_computation.23 | convolution fusion | flops 807402496 | bytes 4853760 | tf_op jit(solution)/shard_map/while/body/eval_jaxpr/cond/branch_1_fun/hgqd,khd->hgqk/dot_general | solution.py:56
  145.8 2.5 %fusion.22 = f32[2,4,128,64]{2,3,1,0:T(8,128)S(1)} fusion(bf16[1024,2,64,1]{0,2,3,1:T(8,128)(2,1)S(1)} %bitcast.117, f32[2,1024,4,128]{3,1,2,0:T(8,128)S(1)} %get-tuple-element.450, f32[2,4,128]{2,1,0:T(4,128)S(1)} %max.13, pred[128,1024]{0,1:T(8,128)(4,1)S(1)} %compare_and_fusion, f32[2,4,128,64]{2,3,1,0:T(8,128)S(1)} %copy-done.6, ...), kind=kOutput, calls=%fused_computation.30 | convolution fusion | flops 808583168 | bytes 5120000 | tf_op jit(solution)/shard_map/while/body/eval_jaxpr/cond/branch_1_fun/hgqk,khd->hgqd/dot_general | solution.py:62
  149.0 1.1 divide_convert_fusion
  150.1 1.5 fusion.54
  153.8 16.7 %reduce-scatter.2.cloned.1.call-done = f32[128,1024]{1,0:T(8,128)} async-done(((f32[128,2048]{1,0:T(8,128)}), f32[128,1024]{1,0:T(8,128)}) %reduce-scatter.2.cloned.1.call-update) | async-done | bytes 524304 | tf_op jit(solution)/shard_map/reduce_scatter | solution.py:210
  (101 shorter events, 19.1 us)
Async XLA Ops:
  7.2 143.0 %copy-start = (bf16[512,2048]{1,0:T(8,128)(2,1)S(1)}, bf16[512,2048]{1,0:T(8,128)(2,1)}, u32[]{:S(2)}) copy-start(bf16[512,2048]{1,0:T(8,128)(2,1)} %param.29) | copy-start | bytes 6291460
  7.2 14.4 %copy-start.3 = (bf16[128,2048]{1,0:T(8,128)(2,1)S(1)}, bf16[128,2048]{1,0:T(8,128)(2,1)}, u32[]{:S(2)}) copy-start(bf16[128,2048]{1,0:T(8,128)(2,1)} %param.22) | copy-start | bytes 1572868
  7.2 14.4 %copy-start.8 = (f32[2048]{0:T(1024)S(1)}, f32[2048]{0:T(1024)}, u32[]{:S(2)}) copy-start(f32[2048]{0:T(1024)} %param.23) | copy-start | bytes 24580
  7.2 17.0 %copy-start.9 = (f32[64]{0:T(128)S(1)}, f32[64]{0:T(128)}, u32[]{:S(2)}) copy-start(f32[64]{0:T(128)} %param.27) | copy-start | bytes 772
  7.2 163.3 %reduce-scatter.2.cloned.1.call-start = ((), (), s32[]{:S(2)}) async-start(), calls=%async_computation.1 | async-start | bytes 1572864 | tf_op jit(solution)/shard_map/reduce_scatter | solution.py:210
  117.0 3.0 %copy-start.4 = (f32[2,4,128,64]{2,3,1,0:T(8,128)S(1)}, f32[2,4,128,64]{2,3,1,0:T(8,128)}, u32[]{:S(2)}) copy-start(f32[2,4,128,64]{2,3,1,0:T(8,128)} %get-tuple-element.293) | copy-start | bytes 786436 | tf_op jit(solution)/shard_map/while/body/eval_jaxpr/cond
  122.4 0.7 copy-start.5
  123.1 3.0 %copy-start.4 = (f32[2,4,128,64]{2,3,1,0:T(8,128)S(1)}, f32[2,4,128,64]{2,3,1,0:T(8,128)}, u32[]{:S(2)}) copy-start(f32[2,4,128,64]{2,3,1,0:T(8,128)} %get-tuple-element.293) | copy-start | bytes 786436 | tf_op jit(solution)/shard_map/while/body/eval_jaxpr/cond
  128.5 0.7 copy-start.5
  134.1 3.0 %copy-start.6 = (f32[2,4,128,64]{2,3,1,0:T(8,128)S(1)}, f32[2,4,128,64]{2,3,1,0:T(8,128)}, u32[]{:S(2)}) copy-start(f32[2,4,128,64]{2,3,1,0:T(8,128)} %get-tuple-element.316) | copy-start | bytes 786436 | tf_op jit(solution)/shard_map/while/body/eval_jaxpr/cond
  139.7 0.7 copy-start.7
  142.8 3.0 %copy-start.6 = (f32[2,4,128,64]{2,3,1,0:T(8,128)S(1)}, f32[2,4,128,64]{2,3,1,0:T(8,128)}, u32[]{:S(2)}) copy-start(f32[2,4,128,64]{2,3,1,0:T(8,128)} %get-tuple-element.316) | copy-start | bytes 786436 | tf_op jit(solution)/shard_map/while/body/eval_jaxpr/cond
  148.3 0.7 copy-start.7
  149.0 2.6 %copy-start.10 = (s32[128]{0:T(128)S(1)}, s32[128]{0:T(128)}, u32[]{:S(2)}) copy-start(s32[128]{0:T(128)} %get-tuple-element.397) | copy-start | bytes 1540
  149.0 2.6 %copy-start.1 = (bf16[2048,128]{1,0:T(8,128)(2,1)S(1)}, bf16[2048,128]{1,0:T(8,128)(2,1)}, u32[]{:S(2)}) copy-start(bf16[2048,128]{1,0:T(8,128)(2,1)} %all_gather.16) | copy-start | bytes 1572868
  149.0 3.3 %copy-start.2 = (bf16[2048,128]{1,0:T(8,128)(2,1)S(1)}, bf16[2048,128]{1,0:T(8,128)(2,1)}, u32[]{:S(2)}) copy-start(bf16[2048,128]{1,0:T(8,128)(2,1)} %all_gather.17) | copy-start | bytes 1572868
Sparse Core Ops, SparseCore 0:
  151.7 18.7 reduce-scatter.1
where the time goes:
time: 178 us; the launch traced here: 177 us
  blocking collectives  87.5 us (49%)
  matrix products  27.6 us (16%)
  other arithmetic  19 us (11%)
  waiting for transfers between devices  16.7 us (9%)
  between operations  15.6 us (9%)
  local copies, waits for them, and re-layouts  9.28 us (5%)
    all_gather x1, blocking collectives, body(): key_piece = lax.all_gather(k_cache, 'seq', axis=0, tiled=True)  26 us
    all_gather x1, blocking collectives, body(): value_piece = lax.all_gather(packed_values, 'seq', axis=0, tiled=True)  20.7 us
    all_gather x1, blocking collectives, body(): key_piece = lax.all_gather(packed_keys, 'seq', axis=0, tiled=True)  20.5 us
    all_gather x1, blocking collectives, body(): value_piece = lax.all_gather(v_cache, 'seq', axis=0, tiled=True)  20.3 us
    reduce_scatter x1, waiting for transfers between devices, body(): lax.psum_scatter(partial_out, 'head', scatter_dimension=1, tiled=True)  16.7 us
    dot_general x4, matrix products, attend_block(): jnp.einsum('hgqk,khd->hgqd', weights, value_float, precision=lax.Precisio...  9.84 us
    dot_general x4, matrix products, attend_block(): jnp.einsum('hgqd,khd->hgqk', query_heads, key_float, precision=lax.Precis...  8.4 us
    while x4, local copies, waits for them, and re-layouts, fold_keys(): carried, _ = lax.scan(visit, carried, stacked)  3.95 us
  transfers between devices with their start and end apart: 1, of which 1 were waited for; matrix products, arithmetic and copies ran while one was open for 1% of the time, Pallas kernels for 0%

commit v1 on v0

v1 whole, which is shorter than its diff:
```python
import functools

import jax
import jax.numpy as jnp
import numpy as np
from jax import lax
from jax.experimental import pallas as pl
from jax.experimental.pallas import tpu as pltpu
from jax.sharding import PartitionSpec as P

PAGE = 128
BLOCK = 64
EPS = 1e-06
MASKED = -1e30
F32 = jnp.float32
BF16 = jnp.bfloat16
VMEM = pltpu.VMEM
SMEM = pltpu.SMEM
LOG2E = 1.4426950408889634


def spec(space):
    return pl.BlockSpec(memory_space=space)


def params(mib=32):
    return pltpu.CompilerParams(vmem_limit_bytes=mib * 1024 * 1024)


def cost(flops, size):
    return pl.CostEstimate(flops=int(flops), bytes_accessed=int(size), transcendentals=0)


def lanes_of(shape):
    return lax.broadcasted_iota(jnp.int32, shape, len(shape) - 1)


def select_kernel(table, prior_keys, prior_values, out, sems):
    first = lax.axis_index("seq") * prior_keys.shape[0]

    def look(i, found):
        slot = table[i] - first
        return jnp.where((slot >= 0) & (slot < prior_keys.shape[0]), slot, found)

    slot = lax.fori_loop(0, table.shape[0], look, 0)
    width = prior_keys.shape[-1]
    copies = [
        pltpu.make_async_copy(prior_keys.at[slot], out.at[:, :width], sems.at[0]),
        pltpu.make_async_copy(prior_values.at[slot], out.at[:, width:], sems.at[1]),
    ]
    for copy in copies:
        copy.start()
    for copy in copies:
        copy.wait()


def norm_and_rotate(x, gain, cosine, sine):
    lane = lanes_of(x.shape)
    left = lane < 64
    square = x * x
    sum_left = jnp.sum(jnp.where(left, square, 0.0), axis=-1, keepdims=True)
    sum_right = jnp.sum(jnp.where(left, 0.0, square), axis=-1, keepdims=True)
    mean = jnp.where(left, sum_left, sum_right) * (1.0 / 64)
    y = x * lax.rsqrt(mean + EPS) * gain
    swapped = jnp.where(lane % 64 < 32, pltpu.roll(y, 96, 1), pltpu.roll(y, 32, 1))
    return y * cosine + swapped * sine


def twice(gain_ref):
    gain = gain_ref[...]
    return jnp.concatenate([gain, gain], axis=-1)


def kv_kernel(
    prior_len, order, hidden, gain, w_key, w_value, key_gain, freq, kv, normed_out, cos_out, sin_out
):
    rows = hidden.shape[0]
    blocks = rows // BLOCK
    me = lax.axis_index("seq")
    wide = hidden[...].astype(F32)
    mean = jnp.mean(wide * wide, axis=-1, keepdims=True)
    normed = (wide * lax.rsqrt(mean + EPS) * gain[...]).astype(BF16)
    normed_out[...] = normed
    values = jnp.dot(normed, w_value[...], preferred_element_type=F32)
    keys = jnp.dot(normed, w_key[...], preferred_element_type=F32)
    row = lax.broadcasted_iota(jnp.int32, (BLOCK, 128), 0)
    lane = lanes_of((BLOCK, 128))
    for b in range(blocks):
        base = prior_len + order[me * blocks + b] * BLOCK
        angle = (base + row).astype(F32) * freq[...]
        part = pl.ds(b * BLOCK, BLOCK)
        sine = jnp.sin(angle)
        cos_out[part, :] = jnp.cos(angle)
        sin_out[part, :] = jnp.where(lane % 64 < 32, -sine, sine)
    rotated = norm_and_rotate(keys, twice(key_gain), cos_out[...], sin_out[...])
    kv[:, :128] = rotated.astype(BF16)
    kv[:, 128:] = values.astype(BF16)


def query_kernel(normed, w_query, query_gain, cosine, sine, q_out):
    rows = normed.shape[0]
    blocks = rows // BLOCK
    tiles = w_query.shape[1] // 128
    per_kv = tiles // 2
    group = 2 * per_kv
    queries = jnp.dot(normed[...], w_query[...], preferred_element_type=F32)
    gain = twice(query_gain)
    left = lanes_of((rows, 128)) < 64
    for t in range(tiles):
        kv_head, u = divmod(t, per_kv)
        x = norm_and_rotate(queries[:, t * 128 : (t + 1) * 128], gain, cosine[...], sine[...])
        x = x * (64**-0.5 * LOG2E)
        turned = pltpu.roll(x, 64, 1)
        pair = (x, turned) if kv_head == 0 else (turned, x)
        for odd, head in enumerate(pair):
            kept = jnp.where(left if kv_head == 0 else ~left, head, 0.0)
            high = kept.astype(BF16)
            low = (kept - high.astype(F32)).astype(BF16)
            both = jnp.concatenate([high, low], axis=-1)
            for b in range(blocks):
                at = ((kv_head * blocks + b) * group + 2 * u + odd) * BLOCK
                q_out[at : at + BLOCK, :] = both[b * BLOCK : (b + 1) * BLOCK, :]


def fold(q, kv_rows, bias, kv_head, m_old, acc_old):
    keys = kv_rows[:, :128]
    values = kv_rows[:, 128:]
    scores = lax.dot_general(
        q,
        jnp.concatenate([keys, keys], axis=-1),
        (((1,), (1,)), ((), ())),
        preferred_element_type=F32,
    )
    if bias is not None:
        scores = scores + bias
    left = lanes_of(values.shape) < 64
    mine = left if kv_head == 0 else ~left
    extended = jnp.where(mine, values, jnp.ones_like(values))
    m_new = jnp.max(scores, axis=-1, keepdims=True)
    if m_old is not None:
        m_new = jnp.maximum(m_old, m_new)
    weights = jnp.exp2(scores - m_new).astype(BF16)
    acc = jnp.dot(weights, extended, preferred_element_type=F32)
    if m_old is not None:
        acc = acc + acc_old * jnp.exp2(m_old - m_new)
    return m_new, acc


def attention_kernel(
    n_chunks, own, first, last, step, blocks, group, chunk_slots, *refs
):
    refs = list(refs)
    q = refs.pop(0)
    if own:
        own_kv = refs.pop(0)
    chunks = [refs.pop(0) for _ in range(n_chunks)]
    order, live = refs.pop(0), refs.pop(0)
    masked = chunk_slots is not None
    if masked:
        slots_ref = refs.pop(0)
    if not first:
        m_in, acc_in = refs.pop(0), refs.pop(0)
    if last:
        out = refs.pop(0)
    m_ref, acc_ref = refs.pop(0), refs.pop(0)
    held, sems = refs.pop(0), refs.pop(0)
    me = lax.axis_index("seq")

    copies = []
    at = 0
    for i, chunk in enumerate(chunks):
        size = chunk.shape[0]
        copies.append(pltpu.make_async_copy(chunk, held.at[pl.ds(at, size)], sems.at[i]))
        at += size
    for copy in copies:
        copy.start()

    part = group * BLOCK
    tiles = 2 * blocks
    q_logical = [order[me * blocks + b] for b in range(blocks)]
    if own:
        total = blocks * BLOCK
        key_at = lanes_of((part, total))
        row = lax.broadcasted_iota(jnp.int32, (part, total), 0) % BLOCK
        for tile in range(tiles):
            kv_head, b = divmod(tile, blocks)
            bias = jnp.full((part, total), MASKED, F32)
            for kb in range(blocks):
                alive = live[q_logical[kb]] > 0
                before = (q_logical[kb] < q_logical[b]) & alive
                here = key_at // BLOCK == kb
                if kb == b:
                    allowed = here & (key_at % BLOCK <= row)
                    bias = jnp.where(allowed, jnp.where(alive, 0.0, MASKED), bias)
                else:
                    bias = jnp.where(here, jnp.where(before, 0.0, MASKED), bias)
            rows = pl.ds(tile * part, part)
            m, acc = fold(q[rows, :], own_kv[...], bias, kv_head, None, None)
            m_ref[rows, :] = jnp.broadcast_to(m, (part, 128))
            acc_ref[rows, :] = acc
    for copy in copies:
        copy.wait()

    n_steps = at // step
    for_loop_started = own

    def visit(c, started):
        key_rows = held[pl.ds(pl.multiple_of(c * step, step), step), :]
        if masked:
            biases = []
            lane = lanes_of((1, 128))
            for b in range(blocks):
                pieces = []
                for s in range(step // 128):
                    rank = me ^ slots_ref[me % 2, chunk_slots + c * (step // 128) + s]
                    value = []
                    for half in range(2):
                        logical = order[rank * 2 + half]
                        fine = (live[logical] > 0) & (logical < q_logical[b]) & (rank != me)
                        value.append(jnp.where(fine, 0.0, MASKED))
                    pieces.append(jnp.where(lane < 64, value[0], value[1]))
                biases.append(jnp.concatenate(pieces, axis=-1))
        for tile in range(tiles):
            kv_head, b = divmod(tile, blocks)
            rows = pl.ds(tile * part, part)
            if started:
                m_old, acc_old = m_ref[rows, :1], acc_ref[rows, :]
            elif not first:
                m_old, acc_old = m_in[rows, :1], acc_in[rows, :]
            else:
                m_old = acc_old = None
            bias = biases[b] if masked else None
            m, acc = fold(q[rows, :], key_rows, bias, kv_head, m_old, acc_old)
            m_ref[rows, :] = jnp.broadcast_to(m, (part, 128))
            acc_ref[rows, :] = acc

    visit(0, for_loop_started)
    if n_steps > 1:
        pl.loop(1, n_steps)(lambda c: visit(c, True))

    if last:
        left = lanes_of((BLOCK, 128)) < 64
        for kv_head in range(2):
            for b in range(blocks):
                for u in range(group // 2):
                    heads = []
                    for odd in range(2):
                        at = ((kv_head * blocks + b) * group + 2 * u + odd) * BLOCK
                        acc = acc_ref[at : at + BLOCK, :]
                        turned = pltpu.roll(acc, 64, 1)
                        ratio = acc / turned
                        heads.append(pltpu.roll(ratio, 64, 1) if odd != kv_head else ratio)
                    both = jnp.where(left, heads[0], heads[1]).astype(BF16)
                    tile = kv_head * (group // 2) + u
                    out[b * BLOCK : (b + 1) * BLOCK, tile * 128 : (tile + 1) * 128] = both


def attention(q, own_kv, chunks, order, live, slots, state, last, chunk_slots, step, blocks, group):
    own = own_kv is not None
    rows = sum(c.shape[0] for c in chunks)
    step = min(step, rows)
    first = state is None
    operands = [q] + ([own_kv] if own else []) + list(chunks) + [order, live]
    specs = [spec(VMEM)] + ([spec(VMEM)] if own else []) + [spec(pl.ANY)] * len(chunks)
    specs += [spec(SMEM), spec(SMEM)]
    if chunk_slots is not None:
        operands.append(slots)
        specs.append(spec(SMEM))
    if not first:
        operands += list(state)
        specs += [spec(VMEM)] * 2
    n = q.shape[0]
    pair = [jax.ShapeDtypeStruct((n, 128), F32)] * 2
    scratch = [VMEM((rows, 256), BF16), pltpu.SemaphoreType.DMA((len(chunks),))]
    if last:
        outs = jax.ShapeDtypeStruct((blocks * BLOCK, 2 * group * 64), BF16)
        out_specs = spec(VMEM)
        scratch = [VMEM((n, 128), F32)] * 2 + scratch
    else:
        outs, out_specs = pair, [spec(VMEM)] * 2
    return pl.pallas_call(
        functools.partial(
            attention_kernel, len(chunks), own, first, last, step, blocks, group, chunk_slots
        ),
        out_shape=outs,
        in_specs=specs,
        out_specs=out_specs,
        scratch_shapes=scratch,
        compiler_params=params(48),
        cost_estimate=cost(4 * n * rows * 256, rows * 512 + n * 2048),
    )(*operands)


def pages_kernel(n_chunks, dest, order, where, *refs):
    chunks, (keys, values, sems) = refs[:n_chunks], refs[n_chunks:]
    me = lax.axis_index("seq")

    def find(table):
        def body(wanted):
            return lax.fori_loop(
                0, table.shape[0], lambda i, f: jnp.where(table[i] == wanted, i, f), 0
            )

        return body

    page = find(dest)(me)
    for half in range(2):
        source = find(order)(page * 2 + half)
        slot = where[me % 2, me ^ (source // 2)]
        row = slot * PAGE + (source % 2) * BLOCK
        at = 0
        for chunk in chunks:
            size = chunk.shape[0]
            inside = (row >= at) & (row < at + size)

            @pl.when(inside)
            def _(chunk=chunk, at=at):
                rows = pl.ds(pl.multiple_of(row - at, BLOCK), BLOCK)
                to = pl.ds(half * BLOCK, BLOCK)
                a = pltpu.make_async_copy(chunk.at[rows, :128], keys.at[0, to], sems.at[0])
                b = pltpu.make_async_copy(chunk.at[rows, 128:], values.at[0, to], sems.at[1])
                a.start()
                b.start()
                a.wait()
                b.wait()

            at += size


def project_kernel(mine, peer, w_mine_all, w_peer, out, w_mine, sem):
    width = out.shape[1]
    x = lax.axis_index("head")
    columns = pl.ds(pl.multiple_of(x * width, width), width)
    copy = pltpu.make_async_copy(w_mine_all.at[:, columns], w_mine, sem)
    copy.start()
    total = jnp.dot(peer[...], w_peer[...], preferred_element_type=F32)
    copy.wait()
    out[...] = total + jnp.dot(mine[...], w_mine[...], preferred_element_type=F32)


def plan(n):
    bits = [1 << i for i in range(1, n.bit_length() - 1)]
    down = bits[::-1]
    even = down
    odd = [down[-1]] + down[:-1] if len(down) > 1 else down
    return [list(pair) for pair in zip(even, odd)]


def slot_masks(steps):
    masks = []
    for parity in range(2):
        held = [0]
        for step in steps:
            held = held + [m ^ step[parity] for m in held]
        masks.append(held)
    full = [masks[p] + [m ^ 1 for m in masks[1 - p]] for p in range(2)]
    return np.array(full, np.int32)


def swap(x, n, step):
    return lax.ppermute(x, "seq", [(i, i ^ step[i & 1]) for i in range(n)])


def spread(own, n, steps):
    first = swap(own, n, steps[0])
    near = jnp.concatenate([own, first], axis=0)
    chunks = [near]
    for step in steps[1:]:
        chunks = chunks + [swap(c, n, step) for c in chunks]
    other = [swap(c, n, [1, 1]) for c in chunks]
    return chunks, other


def body(
    n,
    hidden_in,
    attn_gain,
    w_query,
    w_key,
    w_value,
    query_gain,
    key_gain,
    w_output,
    prior_keys,
    prior_values,
    span_order,
    key_live,
    page_table,
    page_dest,
):
    rows, width = hidden_in.shape
    blocks = rows // BLOCK
    head_dim = query_gain.shape[0]
    group = w_query.shape[1] // w_key.shape[1]
    prior_len = page_table.shape[0] * PAGE
    steps = plan(n)
    masks = slot_masks(steps)
    where = np.zeros_like(masks)
    for p in range(2):
        where[p, masks[p]] = np.arange(n)
    half = head_dim // 2
    freq = np.tile((10000.0 ** (-np.arange(half) / half)).astype(np.float32), 4)[None, :]
    slots = jnp.asarray(masks)

    prior = pl.pallas_call(
        select_kernel,
        out_shape=jax.ShapeDtypeStruct((PAGE, 256), BF16),
        in_specs=[spec(SMEM), spec(pl.ANY), spec(pl.ANY)],
        out_specs=spec(VMEM),
        scratch_shapes=[pltpu.SemaphoreType.DMA((2,))],
        compiler_params=params(),
        cost_estimate=cost(1000, 1 << 17),
    )(page_table, prior_keys, prior_values)

    kv, normed, cosine, sine = pl.pallas_call(
        functools.partial(kv_kernel, prior_len),
        out_shape=[
            jax.ShapeDtypeStruct((rows, 256), BF16),
            jax.ShapeDtypeStruct((rows, width), BF16),
            jax.ShapeDtypeStruct((rows, 128), F32),
            jax.ShapeDtypeStruct((rows, 128), F32),
        ],
        in_specs=[spec(SMEM)] + [spec(VMEM)] * 6,
        out_specs=[spec(VMEM)] * 4,
        compiler_params=params(),
        cost_estimate=cost(2 * rows * width * 256, 3 << 20),
    )(
        span_order,
        hidden_in,
        attn_gain.reshape(1, -1),
        w_key,
        w_value,
        key_gain.reshape(1, -1),
        jnp.asarray(freq),
    )

    prior_same, prior_other = spread(prior, n, steps)
    span_same, span_other = spread(kv, n, steps)

    x = lax.axis_index("head")
    out_width = w_output.shape[1] // 2
    w_send = lax.dynamic_slice_in_dim(w_output, (1 - x) * out_width, out_width, 1)
    w_peer = lax.ppermute(w_send, "head", [(0, 1), (1, 0)])

    q = pl.pallas_call(
        query_kernel,
        out_shape=jax.ShapeDtypeStruct((2 * blocks * group * BLOCK, 256), BF16),
        in_specs=[spec(VMEM)] * 5,
        out_specs=spec(VMEM),
        compiler_params=params(),
        cost_estimate=cost(2 * rows * width * 512, 4 << 20),
    )(normed, w_query, query_gain.reshape(1, -1), cosine, sine)

    common = dict(order=span_order, live=key_live, slots=slots, blocks=blocks, group=group)
    state = attention(
        q, kv, prior_same + prior_other, state=None, last=False, chunk_slots=None, step=1024, **common
    )
    state = attention(
        q, None, span_same, state=state, last=False, chunk_slots=0, step=1024, **common
    )
    heads = attention(
        q, None, span_other, state=state, last=True, chunk_slots=n // 2, step=1024, **common
    )
    peer = lax.ppermute(heads, "head", [(0, 1), (1, 0)])

    all_span = span_same + span_other
    new_keys, new_values = pl.pallas_call(
        functools.partial(pages_kernel, len(all_span)),
        out_shape=[jax.ShapeDtypeStruct((1, PAGE, 128), BF16)] * 2,
        in_specs=[spec(SMEM)] * 3 + [spec(pl.ANY)] * len(all_span),
        out_specs=[spec(VMEM)] * 2,
        scratch_shapes=[pltpu.SemaphoreType.DMA((2,))],
        compiler_params=params(),
        cost_estimate=cost(1000, 1 << 18),
    )(page_dest, span_order, jnp.asarray(where), *all_span)

    attn_out = pl.pallas_call(
        project_kernel,
        out_shape=jax.ShapeDtypeStruct((rows, out_width), F32),
        in_specs=[spec(VMEM), spec(VMEM), spec(pl.ANY), spec(VMEM)],
        out_specs=spec(VMEM),
        scratch_shapes=[VMEM((w_output.shape[0], out_width), BF16), pltpu.SemaphoreType.DMA],
        compiler_params=params(),
        cost_estimate=cost(4 * rows * 512 * out_width, 4 << 20),
    )(heads, peer, w_output, w_peer)
    return attn_out, new_keys, new_values


def solution(mesh):
    return jax.shard_map(
        functools.partial(body, mesh.shape["seq"]),
        mesh=mesh,
        in_specs=(
            P("seq", None),
            P(),
            P(None, "head"),
            P(None, "head"),
            P(None, "head"),
            P(),
            P(),
            P("head", None),
            P("seq", None, "head"),
            P("seq", None, "head"),
            P(),
            P(),
            P(),
            P(),
        ),
        out_specs=(P("seq", "head"), P("seq", None, "head"), P("seq", None, "head")),
        check_vma=False,
    )
```

time: 178 us -> 59.5 us (0.33)
  blocking collectives: 87.5 us -> 0 us
  matrix products: 27.6 us -> 0 us
  Pallas kernels: 0 us -> 22.4 us
  starting transfers between devices: 0.04 us -> 19.4 us
  other arithmetic: 19 us -> 0.01 us
  between operations: 15.6 us -> 1 us
  waiting for transfers between devices: 16.7 us -> 6.74 us
    all_gather x4 -> x0, blocking collectives: 87.5 us -> none  [the longest x1 26 us: body(): key_piece = lax.all_gather(k_cache, 'seq', axis=0, tiled=True)]
    dot_general x14 -> x0, matrix products: 27.6 us -> none  [the longest x4 9.84 us: attend_block(): jnp.einsum('hgqk,khd->hgqd', weights, value_float, precision=lax.Precisio...]
    pallas_call x0 -> x8, Pallas kernels: none -> 22.4 us  [the longest x3 15.7 us: attention(): pl.pallas_call(functools.partial(attention_kernel, len(chunks), own, firs...]
    ppermute x0 -> x18, starting transfers between devices: none -> 19.4 us  [the longest x16 17 us: swap(): return lax.ppermute(x, 'seq', [(i, i ^ step[i & 1]) for i in range(n)])]
    reduce_scatter x1 -> x0, waiting for transfers between devices: 16.7 us -> none  [body(): lax.psum_scatter(partial_out, 'head', scatter_dimension=1, tiled=True)]
    reduce_sum x9 -> x0, other arithmetic: 8.86 us -> none  [the longest x4 3.39 us: attend_block(): weight_sum = weight_sum * factor + jnp.sum(weights, axis=-1)]
    unnamed x14 -> x37, local copies, waits for them, and re-layouts: 0.04 us -> 8.16 us
    ppermute x0 -> x18, waiting for transfers between devices: none -> 6.74 us  [the longest x16 4.05 us: swap(): return lax.ppermute(x, 'seq', [(i, i ^ step[i & 1]) for i in range(n)])]
  transfers between devices with their start and end apart: 1 -> 18, of which waited for: 1 -> 3; matrix products, arithmetic and copies ran while one was open for 1% -> 2% of each run, Pallas kernels for 0% -> 34%
where the time goes in v1:
time: 59.5 us; the launch traced here: 59 us
  Pallas kernels  22.4 us (38%)
  starting transfers between devices  19.4 us (33%)
  local copies, waits for them, and re-layouts  9.47 us (16%)
  waiting for transfers between devices  6.74 us (11%)
  between operations  1 us (2%)
    ppermute x16, starting transfers between devices, swap(): return lax.ppermute(x, 'seq', [(i, i ^ step[i & 1]) for i in range(n)])  17 us
    pallas_call x3, Pallas kernels, attention(): pl.pallas_call(functools.partial(attention_kernel, len(chunks), own, firs...  15.7 us
    unnamed x37, local copies, waits for them, and re-layouts  8.16 us
    ppermute x16, waiting for transfers between devices, swap(): return lax.ppermute(x, 'seq', [(i, i ^ step[i & 1]) for i in range(n)])  4.05 us
    ppermute x1, waiting for transfers between devices, body(): peer = lax.ppermute(heads, 'head', [(0, 1), (1, 0)])  2.69 us
    pallas_call x1, Pallas kernels, body(): pl.pallas_call(functools.partial(pages_kernel, len(all_span)), out_shape=...  2.18 us
    ppermute x1, starting transfers between devices, body(): w_peer = lax.ppermute(w_send, 'head', [(0, 1), (1, 0)])  1.87 us
    pallas_call x1, Pallas kernels, body(): pl.pallas_call(project_kernel, out_shape=jax.ShapeDtypeStruct((rows, out_...  1.47 us
  transfers between devices with their start and end apart: 18, of which 3 were waited for; matrix products, arithmetic and copies ran while one was open for 2% of the time, Pallas kernels for 34%

profile of v1, /device:TPU:0, one launch (start us, length us, event | category | flops | bytes accessed | tf_op | source)
XLA Modules:
  0.0 59.0 jit_solution(13585939687547100447)
XLA Ops:
  0.6 0.8 %copy-done.5 = bf16[2,128,128]{2,1,0:T(8,128)(2,1)S(1)} copy-done((bf16[2,128,128]{2,1,0:T(8,128)(2,1)S(1)}, bf16[2,128,128]{2,1,0:T(8,128)(2,1)}, u32[]{:S(2)}) %copy-start.5) | copy-done | bytes 65560
  1.5 0.8 %copy-done.6 = bf16[2,128,128]{2,1,0:T(8,128)(2,1)S(1)} copy-done((bf16[2,128,128]{2,1,0:T(8,128)(2,1)S(1)}, bf16[2,128,128]{2,1,0:T(8,128)(2,1)}, u32[]{:S(2)}) %copy-start.6) | copy-done | bytes 65560
  2.3 0.7 %copy-done.13 = s32[16]{0:T(128)S(1)} copy-done((s32[16]{0:T(128)S(1)}, s32[16]{0:T(128)}, u32[]{:S(2)}) %copy-start.13) | copy-done | bytes 88
  3.0 0.7 %shard_map.186 = bf16[128,256]{1,0:T(8,128)(2,1)S(1)} custom-call(s32[16]{0:T(128)S(1)} %copy-done.13, bf16[2,128,128]{2,1,0:T(8,128)(2,1)S(1)} %copy-done.5, bf16[2,128,128]{2,1,0:T(8,128)(2,1)S(1)} %copy-done.6), custom_call_target="tpu_custom_call" | custom-call | flops 1000 | bytes 131072 | tf_op jit(solution)/shard_map/pallas_call | solution.py:405
  3.7 4.1 %collective-permute-start.8 = (bf16[128,256]{1,0:T(8,128)(2,1)S(1)}, bf16[128,256]{1,0:T(8,128)(2,1)S(1)}, u32[]{:S(2)}, u32[]{:S(2)}) collective-permute-start(bf16[128,256]{1,0:T(8,128)(2,1)S(1)} %shard_map.186), channel_id=1, source_target_pairs={{0,16},{2,6},{4,20},{6,2},{8,24},{10,14},{12,28},{14,10},{16,0},{1... | collective-permute-start | bytes 196616 | tf_op jit(solution)/shard_map/ppermute | solution.py:361
  7.8 1.0 %copy-done.2 = bf16[128,2048]{1,0:T(8,128)(2,1)S(1)} copy-done((bf16[128,2048]{1,0:T(8,128)(2,1)S(1)}, bf16[128,2048]{1,0:T(8,128)(2,1)}, u32[]{:S(2)}) %copy-start.2) | copy-done | bytes 524312
  8.8 1.0 %copy-done.3 = bf16[2048,128]{1,0:T(8,128)(2,1)S(1)} copy-done((bf16[2048,128]{1,0:T(8,128)(2,1)S(1)}, bf16[2048,128]{1,0:T(8,128)(2,1)}, u32[]{:S(2)}) %copy-start.3) | copy-done | bytes 524312
  9.9 1.0 %copy-done.4 = bf16[2048,128]{1,0:T(8,128)(2,1)S(1)} copy-done((bf16[2048,128]{1,0:T(8,128)(2,1)S(1)}, bf16[2048,128]{1,0:T(8,128)(2,1)}, u32[]{:S(2)}) %copy-start.4) | copy-done | bytes 524312
  10.9 0.7 %copy-done.7 = f32[2048]{0:T(1024)S(1)} copy-done((f32[2048]{0:T(1024)S(1)}, f32[2048]{0:T(1024)}, u32[]{:S(2)}) %copy-start.7) | copy-done | bytes 8216
  11.6 0.7 %copy-done.8 = s32[32]{0:T(128)S(1)} copy-done((s32[32]{0:T(128)S(1)}, s32[32]{0:T(128)}, u32[]{:S(2)}) %copy-start.8) | copy-done | bytes 152
  12.3 0.7 %copy-done.11 = f32[64]{0:T(128)S(1)} copy-done((f32[64]{0:T(128)S(1)}, f32[64]{0:T(128)}, u32[]{:S(2)}) %copy-start.11) | copy-done | bytes 280
  12.9 0.7 %copy-done.12 = f32[1,128]{1,0:T(1,128)S(1)} copy-done((f32[1,128]{1,0:T(1,128)S(1)}, f32[1,128]{1,0:T(1,128)}, u32[]{:S(2)}) %copy-start.12) | copy-done | bytes 536
  13.6 1.4 %shard_map.184 = (bf16[128,256]{1,0:T(8,128)(2,1)S(1)}, bf16[128,2048]{1,0:T(8,128)(2,1)S(1)}, f32[128,128]{1,0:T(8,128)S(1)}, f32[128,128]{1,0:T(8,128)S(1)}) custom-call(s32[32]{0:T(128)S(1)} %copy-done.8, bf16[128,2048]{1,0:T(8,128)(2,1)S(1)} %copy-done.2, f32[1,2048]{1,0:T(1,128)S(1)} %bitcast.3, bf16[2048,128]{1,0:T(8,128)(2,1)S(1)} %copy-done.3, ...), custom_call_target="tpu_custom_call" | custom-call | flops 134217728 | bytes 3145728 | tf_op jit(solution)/shard_map/pallas_call | solution.py:415
  15.1 1.3 %constant_dynamic-slice_fusion = bf16[512,1024]{1,0:T(8,128)(2,1)S(1)} fusion(bf16[512,2048]{1,0:T(8,128)(2,1)} %w_mine_all.1, s32[]{:T(128)S(6)} %select_n.3), kind=kLoop, calls=%fused_computation.3 | loop fusion | bytes 2097156 | tf_op jit(solution)/shard_map/dynamic_slice | solution.py:442
  16.4 1.9 %collective-permute-start.17 = (bf16[512,1024]{1,0:T(8,128)(2,1)S(1)}, bf16[512,1024]{1,0:T(8,128)(2,1)S(1)}, u32[]{:S(2)}, u32[]{:S(2)}) collective-permute-start(bf16[512,1024]{1,0:T(8,128)(2,1)S(1)} %constant_dynamic-slice_fusion), channel_id=1, source_target_pairs={{0,1},{1,0},{2,3},{3,2},{4,5},{5,4},{6,7},{7,6},{8,9},{9,8},{10,11... | collective-permute-start | bytes 3145736 | tf_op jit(solution)/shard_map/ppermute | solution.py:443
  18.4 1.6 %collective-permute-start.9 = (bf16[256,256]{1,0:T(8,128)(2,1)S(1)}, bf16[256,256]{1,0:T(8,128)(2,1)S(1)}, u32[]{:S(2)}, u32[]{:S(2)}) collective-permute-start(bf16[256,256]{1,0:T(8,128)(2,1)S(1)} %pad_maximum_fusion.refs_2_), channel_id=1, source_target_pairs={{0,8},{2,18},{4,12},{6,22},{8,0},{10,26},{12,4},{14,30},{16,24},{1... | collective-permute-start | bytes 393224 | tf_op jit(solution)/shard_map/ppermute | solution.py:361
  20.0 1.5 %collective-permute-start.10 = (bf16[256,256]{1,0:T(8,128)(2,1)S(1)}, bf16[256,256]{1,0:T(8,128)(2,1)S(1)}, u32[]{:S(2)}, u32[]{:S(2)}) collective-permute-start(bf16[256,256]{1,0:T(8,128)(2,1)S(1)} %pad_maximum_fusion.refs_2_), channel_id=1, source_target_pairs={{0,4},{2,10},{4,0},{6,14},{8,12},{10,2},{12,8},{14,6},{16,20},{18,... | collective-permute-start | bytes 393224 | tf_op jit(solution)/shard_map/ppermute | solution.py:361
  22.1 1.2 %collective-permute-start.2 = (bf16[256,256]{1,0:T(8,128)(2,1)S(1)}, bf16[256,256]{1,0:T(8,128)(2,1)S(1)}, u32[]{:S(2)}, u32[]{:S(2)}) collective-permute-start(bf16[256,256]{1,0:T(8,128)(2,1)S(1)} %constant_dynamic-update-slice_fusion.refs_1_.refs_0_), channel_id=1, source_target_pairs={{0,8},{2,18},{4,12},{6,22},{8,0},{10,26},{12,4},{14,30},{16,24},{1... | collective-permute-start | bytes 393224 | tf_op jit(solution)/shard_map/ppermute | solution.py:361
  23.3 2.1 %collective-permute-done.9.refs_3_ = bf16[256,256]{1,0:T(8,128)(2,1)S(1)} collective-permute-done((bf16[256,256]{1,0:T(8,128)(2,1)S(1)}, bf16[256,256]{1,0:T(8,128)(2,1)S(1)}, u32[]{:S(2)}, u32[]{:S(2)}) %collective-permute-start.9) | collective-permute-done | bytes 131104 | tf_op jit(solution)/shard_map/ppermute | solution.py:361
  25.4 1.5 %collective-permute-start.11 = (bf16[256,256]{1,0:T(8,128)(2,1)S(1)}, bf16[256,256]{1,0:T(8,128)(2,1)S(1)}, u32[]{:S(2)}, u32[]{:S(2)}) collective-permute-start(bf16[256,256]{1,0:T(8,128)(2,1)S(1)} %collective-permute-done.9.refs_3_), channel_id=1, source_target_pairs={{0,4},{2,10},{4,0},{6,14},{8,12},{10,2},{12,8},{14,6},{16,20},{18,... | collective-permute-start | bytes 393224 | tf_op jit(solution)/shard_map/ppermute | solution.py:361
  27.0 1.2 %collective-permute-start.14 = (bf16[256,256]{1,0:T(8,128)(2,1)S(1)}, bf16[256,256]{1,0:T(8,128)(2,1)S(1)}, u32[]{:S(2)}, u32[]{:S(2)}) collective-permute-start(bf16[256,256]{1,0:T(8,128)(2,1)S(1)} %collective-permute-done.10.refs_4_), channel_id=1, source_target_pairs={{0,2},{2,0},{4,6},{6,4},{8,10},{10,8},{12,14},{14,12},{16,18},{18,... | collective-permute-start | bytes 393224 | tf_op jit(solution)/shard_map/ppermute | solution.py:361
  28.2 2.4 %collective-permute-start.13 = (bf16[256,256]{1,0:T(8,128)(2,1)S(1)}, bf16[256,256]{1,0:T(8,128)(2,1)S(1)}, u32[]{:S(2)}, u32[]{:S(2)}) collective-permute-start(bf16[256,256]{1,0:T(8,128)(2,1)S(1)} %collective-permute-done.9.refs_3_), channel_id=1, source_target_pairs={{0,2},{2,0},{4,6},{6,4},{8,10},{10,8},{12,14},{14,12},{16,18},{18,... | collective-permute-start | bytes 393224 | tf_op jit(solution)/shard_map/ppermute | solution.py:361
  30.6 1.5 %collective-permute-start.6 = (bf16[256,256]{1,0:T(8,128)(2,1)S(1)}, bf16[256,256]{1,0:T(8,128)(2,1)S(1)}, u32[]{:S(2)}, u32[]{:S(2)}) collective-permute-start(bf16[256,256]{1,0:T(8,128)(2,1)S(1)} %collective-permute-done.2.refs_2_.refs_1_), channel_id=1, source_target_pairs={{0,4},{2,10},{4,0},{6,14},{8,12},{10,2},{12,8},{14,6},{16,20},{18,... | collective-permute-start | bytes 393224 | tf_op jit(solution)/shard_map/ppermute | solution.py:361
  32.1 0.8 %shard_map.185.refs_0_ = bf16[1024,256]{1,0:T(8,128)(2,1)S(1)} custom-call(bf16[128,2048]{1,0:T(8,128)(2,1)S(1)} %get-tuple-element.13.normed, bf16[2048,512]{1,0:T(8,128)(2,1)S(1)} %copy-done.1, f32[1,64]{1,0:T(1,128)S(1)} %bitcast.5, f32[128,128]{1,0:T(8,128)S(1)} %get-tuple-element.14.cosine, f32[128,128]{1,0:T(8,128)S(1)} %get-tuple-element.15.sine), custom_call_target="tpu_custom_call" | custom-call | flops 268435456 | bytes 4194304 | tf_op jit(solution)/shard_map/pallas_call | solution.py:445
  33.6 1.9 %collective-permute-done.6.refs_4_.refs_3_ = bf16[256,256]{1,0:T(8,128)(2,1)S(1)} collective-permute-done((bf16[256,256]{1,0:T(8,128)(2,1)S(1)}, bf16[256,256]{1,0:T(8,128)(2,1)S(1)}, u32[]{:S(2)}, u32[]{:S(2)}) %collective-permute-start.6) | collective-permute-done | bytes 131104 | tf_op jit(solution)/shard_map/ppermute | solution.py:361
  36.0 7.8 %shard_map.187 = (f32[1024,128]{1,0:T(8,128)S(1)}, f32[1024,128]{1,0:T(8,128)S(1)}) custom-call(bf16[1024,256]{1,0:T(8,128)(2,1)S(1)} %shard_map.185.refs_0_, bf16[128,256]{1,0:T(8,128)(2,1)S(1)} %get-tuple-element.16.refs_1_, bf16[256,256]{1,0:T(8,128)(2,1)S(1)} %pad_maximum_fusion.refs_2_, bf16[256,256]{1,0:T(8,128)(2,1)S(1)} %collective-permute-done.9.refs_3_, ...), custom_call_target="tpu_custom_call" | custom-call | flops 2147483648 | bytes 3145728 | tf_op jit(solution)/shard_map/pallas_call | solution.py:281
  43.9 3.8 %shard_map.188 = (f32[1024,128]{1,0:T(8,128)S(1)}, f32[1024,128]{1,0:T(8,128)S(1)}) custom-call(bf16[1024,256]{1,0:T(8,128)(2,1)S(1)} %shard_map.185.refs_0_, bf16[256,256]{1,0:T(8,128)(2,1)S(1)} %constant_dynamic-update-slice_fusion.refs_1_.refs_0_, bf16[256,256]{1,0:T(8,128)(2,1)S(1)} %collective-permute-done.2.refs_2_.refs_1_, ...), custom_call_target="tpu_custom_call" | custom-call | flops 1073741824 | bytes 2621440 | tf_op jit(solution)/shard_map/pallas_call | solution.py:281
  47.8 4.1 %shard_map.189.mine = bf16[128,512]{1,0:T(8,128)(2,1)S(1)} custom-call(bf16[1024,256]{1,0:T(8,128)(2,1)S(1)} %shard_map.185.refs_0_, bf16[256,256]{1,0:T(8,128)(2,1)S(1)} %collective-permute-done.1.refs_1_.refs_4_, bf16[256,256]{1,0:T(8,128)(2,1)S(1)} %collective-permute-done.3.refs_2_.refs_5_, bf16[256,256]{1,0:T(8,128)(2,1)S(1)} %collective-permute-done.5.refs_3_.refs_6_, ...), custom_call_target="tpu_custom_call" | custom-call | flops 1073741824 | bytes 2621440 | tf_op jit(solution)/shard_map/pallas_call | solution.py:281
  51.9 0.6 %collective-permute-start.16 = (bf16[128,512]{1,0:T(8,128)(2,1)S(1)}, bf16[128,512]{1,0:T(8,128)(2,1)S(1)}, u32[]{:S(2)}, u32[]{:S(2)}) collective-permute-start(bf16[128,512]{1,0:T(8,128)(2,1)S(1)} %shard_map.189.mine), channel_id=1, source_target_pairs={{0,1},{1,0},{2,3},{3,2},{4,5},{5,4},{6,7},{7,6},{8,9},{9,8},{10,11... | collective-permute-start | bytes 393224 | tf_op jit(solution)/shard_map/ppermute | solution.py:464
  52.5 2.2 %shard_map.191 = (bf16[1,128,128]{2,1,0:T(8,128)(2,1)}, bf16[1,128,128]{2,1,0:T(8,128)(2,1)}) custom-call(s32[16]{0:T(128)S(1)} %copy-done.14, s32[32]{0:T(128)S(1)} %copy-done.9, s32[2,16]{1,0:T(2,128)S(1)} %copy-done.10, bf16[256,256]{1,0:T(8,128)(2,1)S(1)} %constant_dynamic-update-slice_fusion.refs_1_.refs_0_, ...), custom_call_target="tpu_custom_call" | custom-call | flops 1000 | bytes 262144 | tf_op jit(solution)/shard_map/pallas_call | solution.py:467
  54.7 2.7 %collective-permute-done.16.peer = bf16[128,512]{1,0:T(8,128)(2,1)S(1)} collective-permute-done((bf16[128,512]{1,0:T(8,128)(2,1)S(1)}, bf16[128,512]{1,0:T(8,128)(2,1)S(1)}, u32[]{:S(2)}, u32[]{:S(2)}) %collective-permute-start.16) | collective-permute-done | bytes 131104 | tf_op jit(solution)/shard_map/ppermute | solution.py:464
  57.4 1.5 %shard_map.190 = f32[128,1024]{1,0:T(8,128)} custom-call(bf16[128,512]{1,0:T(8,128)(2,1)S(1)} %shard_map.189.mine, bf16[128,512]{1,0:T(8,128)(2,1)S(1)} %collective-permute-done.16.peer, bf16[512,2048]{1,0:T(8,128)(2,1)S(1)} %copy-done, bf16[512,1024]{1,0:T(8,128)(2,1)S(1)} %collective-permute-done.17.w_peer), custom_call_target="tpu_custom_call" | custom-call | flops 268435456 | bytes 4194304 | tf_op jit(solution)/shard_map/pallas_call | solution.py:477
  (52 shorter events, 2.0 us)
Async XLA Ops:
  0.6 0.8 %copy-start.5 = (bf16[2,128,128]{2,1,0:T(8,128)(2,1)S(1)}, bf16[2,128,128]{2,1,0:T(8,128)(2,1)}, u32[]{:S(2)}) copy-start(bf16[2,128,128]{2,1,0:T(8,128)(2,1)} %prior_keys.1) | copy-start | bytes 196612
  1.5 0.8 %copy-start.6 = (bf16[2,128,128]{2,1,0:T(8,128)(2,1)S(1)}, bf16[2,128,128]{2,1,0:T(8,128)(2,1)}, u32[]{:S(2)}) copy-start(bf16[2,128,128]{2,1,0:T(8,128)(2,1)} %prior_values.1) | copy-start | bytes 196612
  3.7 14.6 %collective-permute-start.8 = (bf16[128,256]{1,0:T(8,128)(2,1)S(1)}, bf16[128,256]{1,0:T(8,128)(2,1)S(1)}, u32[]{:S(2)}, u32[]{:S(2)}) collective-permute-start(bf16[128,256]{1,0:T(8,128)(2,1)S(1)} %shard_map.186), channel_id=1, source_target_pairs={{0,16},{2,6},{4,20},{6,2},{8,24},{10,14},{12,28},{14,10},{16,0},{1... | collective-permute-start | bytes 196616 | tf_op jit(solution)/shard_map/ppermute | solution.py:361
  7.8 1.0 %copy-start.2 = (bf16[128,2048]{1,0:T(8,128)(2,1)S(1)}, bf16[128,2048]{1,0:T(8,128)(2,1)}, u32[]{:S(2)}) copy-start(bf16[128,2048]{1,0:T(8,128)(2,1)} %hidden.1) | copy-start | bytes 1572868
  8.8 1.0 %copy-start.3 = (bf16[2048,128]{1,0:T(8,128)(2,1)S(1)}, bf16[2048,128]{1,0:T(8,128)(2,1)}, u32[]{:S(2)}) copy-start(bf16[2048,128]{1,0:T(8,128)(2,1)} %w_key.1) | copy-start | bytes 1572868
  9.9 1.0 %copy-start.4 = (bf16[2048,128]{1,0:T(8,128)(2,1)S(1)}, bf16[2048,128]{1,0:T(8,128)(2,1)}, u32[]{:S(2)}) copy-start(bf16[2048,128]{1,0:T(8,128)(2,1)} %w_value.1) | copy-start | bytes 1572868
  10.9 0.7 %copy-start.7 = (f32[2048]{0:T(1024)S(1)}, f32[2048]{0:T(1024)}, u32[]{:S(2)}) copy-start(f32[2048]{0:T(1024)} %param.18) | copy-start | bytes 24580
  13.6 18.5 %copy-start.1 = (bf16[2048,512]{1,0:T(8,128)(2,1)S(1)}, bf16[2048,512]{1,0:T(8,128)(2,1)}, u32[]{:S(2)}) copy-start(bf16[2048,512]{1,0:T(8,128)(2,1)} %w_query.1) | copy-start | bytes 6291460
  13.6 18.5 %copy-start.15 = (f32[64]{0:T(128)S(1)}, f32[64]{0:T(128)}, u32[]{:S(2)}) copy-start(f32[64]{0:T(128)} %param.22) | copy-start | bytes 772
  15.0 6.5 %collective-permute-start = (bf16[128,256]{1,0:T(8,128)(2,1)S(1)}, bf16[128,256]{1,0:T(8,128)(2,1)S(1)}, u32[]{:S(2)}, u32[]{:S(2)}) collective-permute-start(bf16[128,256]{1,0:T(8,128)(2,1)S(1)} %get-tuple-element.16.refs_1_), channel_id=1, source_target_pairs={{0,16},{2,6},{4,20},{6,2},{8,24},{10,14},{12,28},{14,10},{16,0},{1... | collective-permute-start | bytes 196616 | tf_op jit(solution)/shard_map/ppermute | solution.py:361
  16.4 19.6 %copy-start.9 = (s32[32]{0:T(128)S(1)}, s32[32]{0:T(128)}, u32[]{:S(2)}) copy-start(s32[32]{0:T(128)} %order.3) | copy-start | bytes 388
  16.4 19.6 %copy-start.16 = (s32[32]{0:T(128)S(1)}, s32[32]{0:T(128)}, u32[]{:S(2)}) copy-start(s32[32]{0:T(128)} %refs_6_.3) | copy-start | bytes 388
  16.4 41.0 %collective-permute-start.17 = (bf16[512,1024]{1,0:T(8,128)(2,1)S(1)}, bf16[512,1024]{1,0:T(8,128)(2,1)S(1)}, u32[]{:S(2)}, u32[]{:S(2)}) collective-permute-start(bf16[512,1024]{1,0:T(8,128)(2,1)S(1)} %constant_dynamic-slice_fusion), channel_id=1, source_target_pairs={{0,1},{1,0},{2,3},{3,2},{4,5},{5,4},{6,7},{7,6},{8,9},{9,8},{10,11... | collective-permute-start | bytes 3145736 | tf_op jit(solution)/shard_map/ppermute | solution.py:443
  18.3 3.8 %collective-permute-start.12 = (bf16[256,256]{1,0:T(8,128)(2,1)S(1)}, bf16[256,256]{1,0:T(8,128)(2,1)S(1)}, u32[]{:S(2)}, u32[]{:S(2)}) collective-permute-start(bf16[256,256]{1,0:T(8,128)(2,1)S(1)} %pad_maximum_fusion.refs_2_), channel_id=1, source_target_pairs={{0,2},{2,0},{4,6},{6,4},{8,10},{10,8},{12,14},{14,12},{16,18},{18,... | collective-permute-start | bytes 393224 | tf_op jit(solution)/shard_map/ppermute | solution.py:361
  18.4 7.1 %collective-permute-start.9 = (bf16[256,256]{1,0:T(8,128)(2,1)S(1)}, bf16[256,256]{1,0:T(8,128)(2,1)S(1)}, u32[]{:S(2)}, u32[]{:S(2)}) collective-permute-start(bf16[256,256]{1,0:T(8,128)(2,1)S(1)} %pad_maximum_fusion.refs_2_), channel_id=1, source_target_pairs={{0,8},{2,18},{4,12},{6,22},{8,0},{10,26},{12,4},{14,30},{16,24},{1... | collective-permute-start | bytes 393224 | tf_op jit(solution)/shard_map/ppermute | solution.py:361
  20.0 6.9 %collective-permute-start.10 = (bf16[256,256]{1,0:T(8,128)(2,1)S(1)}, bf16[256,256]{1,0:T(8,128)(2,1)S(1)}, u32[]{:S(2)}, u32[]{:S(2)}) collective-permute-start(bf16[256,256]{1,0:T(8,128)(2,1)S(1)} %pad_maximum_fusion.refs_2_), channel_id=1, source_target_pairs={{0,4},{2,10},{4,0},{6,14},{8,12},{10,2},{12,8},{14,6},{16,20},{18,... | collective-permute-start | bytes 393224 | tf_op jit(solution)/shard_map/ppermute | solution.py:361
  21.6 6.6 %collective-permute-start.4 = (bf16[256,256]{1,0:T(8,128)(2,1)S(1)}, bf16[256,256]{1,0:T(8,128)(2,1)S(1)}, u32[]{:S(2)}, u32[]{:S(2)}) collective-permute-start(bf16[256,256]{1,0:T(8,128)(2,1)S(1)} %constant_dynamic-update-slice_fusion.refs_1_.refs_0_), channel_id=1, source_target_pairs={{0,4},{2,10},{4,0},{6,14},{8,12},{10,2},{12,8},{14,6},{16,20},{18,... | collective-permute-start | bytes 393224 | tf_op jit(solution)/shard_map/ppermute | solution.py:361
  22.1 8.4 %collective-permute-start.2 = (bf16[256,256]{1,0:T(8,128)(2,1)S(1)}, bf16[256,256]{1,0:T(8,128)(2,1)S(1)}, u32[]{:S(2)}, u32[]{:S(2)}) collective-permute-start(bf16[256,256]{1,0:T(8,128)(2,1)S(1)} %constant_dynamic-update-slice_fusion.refs_1_.refs_0_), channel_id=1, source_target_pairs={{0,8},{2,18},{4,12},{6,22},{8,0},{10,26},{12,4},{14,30},{16,24},{1... | collective-permute-start | bytes 393224 | tf_op jit(solution)/shard_map/ppermute | solution.py:361
  25.4 6.6 %collective-permute-start.11 = (bf16[256,256]{1,0:T(8,128)(2,1)S(1)}, bf16[256,256]{1,0:T(8,128)(2,1)S(1)}, u32[]{:S(2)}, u32[]{:S(2)}) collective-permute-start(bf16[256,256]{1,0:T(8,128)(2,1)S(1)} %collective-permute-done.9.refs_3_), channel_id=1, source_target_pairs={{0,4},{2,10},{4,0},{6,14},{8,12},{10,2},{12,8},{14,6},{16,20},{18,... | collective-permute-start | bytes 393224 | tf_op jit(solution)/shard_map/ppermute | solution.py:361
  27.0 6.0 %collective-permute-start.14 = (bf16[256,256]{1,0:T(8,128)(2,1)S(1)}, bf16[256,256]{1,0:T(8,128)(2,1)S(1)}, u32[]{:S(2)}, u32[]{:S(2)}) collective-permute-start(bf16[256,256]{1,0:T(8,128)(2,1)S(1)} %collective-permute-done.10.refs_4_), channel_id=1, source_target_pairs={{0,2},{2,0},{4,6},{6,4},{8,10},{10,8},{12,14},{14,12},{16,18},{18,... | collective-permute-start | bytes 393224 | tf_op jit(solution)/shard_map/ppermute | solution.py:361
  28.2 5.3 %collective-permute-start.13 = (bf16[256,256]{1,0:T(8,128)(2,1)S(1)}, bf16[256,256]{1,0:T(8,128)(2,1)S(1)}, u32[]{:S(2)}, u32[]{:S(2)}) collective-permute-start(bf16[256,256]{1,0:T(8,128)(2,1)S(1)} %collective-permute-done.9.refs_3_), channel_id=1, source_target_pairs={{0,2},{2,0},{4,6},{6,4},{8,10},{10,8},{12,14},{14,12},{16,18},{18,... | collective-permute-start | bytes 393224 | tf_op jit(solution)/shard_map/ppermute | solution.py:361
  30.6 5.0 %collective-permute-start.6 = (bf16[256,256]{1,0:T(8,128)(2,1)S(1)}, bf16[256,256]{1,0:T(8,128)(2,1)S(1)}, u32[]{:S(2)}, u32[]{:S(2)}) collective-permute-start(bf16[256,256]{1,0:T(8,128)(2,1)S(1)} %collective-permute-done.2.refs_2_.refs_1_), channel_id=1, source_target_pairs={{0,4},{2,10},{4,0},{6,14},{8,12},{10,2},{12,8},{14,6},{16,20},{18,... | collective-permute-start | bytes 393224 | tf_op jit(solution)/shard_map/ppermute | solution.py:361
  32.1 3.5 %collective-permute-start.15 = (bf16[256,256]{1,0:T(8,128)(2,1)S(1)}, bf16[256,256]{1,0:T(8,128)(2,1)S(1)}, u32[]{:S(2)}, u32[]{:S(2)}) collective-permute-start(bf16[256,256]{1,0:T(8,128)(2,1)S(1)} %collective-permute-done.11.refs_5_), channel_id=1, source_target_pairs={{0,2},{2,0},{4,6},{6,4},{8,10},{10,8},{12,14},{14,12},{16,18},{18,... | collective-permute-start | bytes 393224 | tf_op jit(solution)/shard_map/ppermute | solution.py:361
  32.9 10.9 %copy-start.17 = (s32[2,16]{1,0:T(2,128)S(1)}, s32[2,16]{1,0:T(2,128)}, u32[]{:S(2)}) copy-start(s32[2,16]{1,0:T(2,128)} %constant.18.clone.refs_7_) | copy-start | bytes 388
  33.0 14.8 %collective-permute-start.1 = (bf16[256,256]{1,0:T(8,128)(2,1)S(1)}, bf16[256,256]{1,0:T(8,128)(2,1)S(1)}, u32[]{:S(2)}, u32[]{:S(2)}) collective-permute-start(bf16[256,256]{1,0:T(8,128)(2,1)S(1)} %constant_dynamic-update-slice_fusion.refs_1_.refs_0_), channel_id=1, source_target_pairs={{0,2},{2,0},{4,6},{6,4},{8,10},{10,8},{12,14},{14,12},{16,18},{18,... | collective-permute-start | bytes 393224 | tf_op jit(solution)/shard_map/ppermute | solution.py:361
  33.5 14.2 %collective-permute-start.3 = (bf16[256,256]{1,0:T(8,128)(2,1)S(1)}, bf16[256,256]{1,0:T(8,128)(2,1)S(1)}, u32[]{:S(2)}, u32[]{:S(2)}) collective-permute-start(bf16[256,256]{1,0:T(8,128)(2,1)S(1)} %collective-permute-done.2.refs_2_.refs_1_), channel_id=1, source_target_pairs={{0,2},{2,0},{4,6},{6,4},{8,10},{10,8},{12,14},{14,12},{16,18},{18,... | collective-permute-start | bytes 393224 | tf_op jit(solution)/shard_map/ppermute | solution.py:361
  35.5 12.2 %collective-permute-start.5 = (bf16[256,256]{1,0:T(8,128)(2,1)S(1)}, bf16[256,256]{1,0:T(8,128)(2,1)S(1)}, u32[]{:S(2)}, u32[]{:S(2)}) collective-permute-start(bf16[256,256]{1,0:T(8,128)(2,1)S(1)} %collective-permute-done.4.refs_3_.refs_2_), channel_id=1, source_target_pairs={{0,2},{2,0},{4,6},{6,4},{8,10},{10,8},{12,14},{14,12},{16,18},{18,... | collective-permute-start | bytes 393224 | tf_op jit(solution)/shard_map/ppermute | solution.py:361
  35.5 12.3 %collective-permute-start.7 = (bf16[256,256]{1,0:T(8,128)(2,1)S(1)}, bf16[256,256]{1,0:T(8,128)(2,1)S(1)}, u32[]{:S(2)}, u32[]{:S(2)}) collective-permute-start(bf16[256,256]{1,0:T(8,128)(2,1)S(1)} %collective-permute-done.6.refs_4_.refs_3_), channel_id=1, source_target_pairs={{0,2},{2,0},{4,6},{6,4},{8,10},{10,8},{12,14},{14,12},{16,18},{18,... | collective-permute-start | bytes 393224 | tf_op jit(solution)/shard_map/ppermute | solution.py:361
  47.7 4.8 %copy-start.10 = (s32[2,16]{1,0:T(2,128)S(1)}, s32[2,16]{1,0:T(2,128)}, u32[]{:S(2)}) copy-start(s32[2,16]{1,0:T(2,128)} %constant.20.clone.where) | copy-start | bytes 388
  47.7 4.8 %copy-start.14 = (s32[16]{0:T(128)S(1)}, s32[16]{0:T(128)}, u32[]{:S(2)}) copy-start(s32[16]{0:T(128)} %dest.1) | copy-start | bytes 196
  47.8 9.6 %copy-start = (bf16[512,2048]{1,0:T(8,128)(2,1)S(1)}, bf16[512,2048]{1,0:T(8,128)(2,1)}, u32[]{:S(2)}) copy-start(bf16[512,2048]{1,0:T(8,128)(2,1)} %w_mine_all.1) | copy-start | bytes 6291460
  51.9 5.5 %collective-permute-start.16 = (bf16[128,512]{1,0:T(8,128)(2,1)S(1)}, bf16[128,512]{1,0:T(8,128)(2,1)S(1)}, u32[]{:S(2)}, u32[]{:S(2)}) collective-permute-start(bf16[128,512]{1,0:T(8,128)(2,1)S(1)} %shard_map.189.mine), channel_id=1, source_target_pairs={{0,1},{1,0},{2,3},{3,2},{4,5},{5,4},{6,7},{7,6},{8,9},{9,8},{10,11... | collective-permute-start | bytes 393224 | tf_op jit(solution)/shard_map/ppermute | solution.py:464
  (4 other events, 2.6 us)

commit v2 on v1

v2 whole, which is shorter than its diff:
```python
import functools

import jax
import jax.numpy as jnp
import numpy as np
from jax import lax
from jax.experimental import pallas as pl
from jax.experimental.pallas import tpu as pltpu
from jax.sharding import PartitionSpec as P

PAGE = 128
BLOCK = 64
EPS = 1e-06
MASKED = -1e30
F32 = jnp.float32
BF16 = jnp.bfloat16
VMEM = pltpu.VMEM
SMEM = pltpu.SMEM
LOG2E = 1.4426950408889634


def spec(space):
    return pl.BlockSpec(memory_space=space)


def in_hbm(*arrays):
    return [pltpu.with_memory_space_constraint(a, pltpu.HBM) for a in arrays]


def params(mib=32):
    return pltpu.CompilerParams(vmem_limit_bytes=mib * 1024 * 1024)


def cost(flops, size):
    return pl.CostEstimate(flops=int(flops), bytes_accessed=int(size), transcendentals=0)


def lanes_of(shape):
    return lax.broadcasted_iota(jnp.int32, shape, len(shape) - 1)


def norm_and_rotate(x, gain, cosine, sine):
    lane = lanes_of(x.shape)
    left = lane < 64
    square = x * x
    sum_left = jnp.sum(jnp.where(left, square, 0.0), axis=-1, keepdims=True)
    sum_right = jnp.sum(jnp.where(left, 0.0, square), axis=-1, keepdims=True)
    mean = jnp.where(left, sum_left, sum_right) * (1.0 / 64)
    y = x * lax.rsqrt(mean + EPS) * gain
    swapped = jnp.where(lane % 64 < 32, pltpu.roll(y, 96, 1), pltpu.roll(y, 32, 1))
    return y * cosine + swapped * sine


def twice(gain_ref):
    gain = gain_ref[...]
    return jnp.concatenate([gain, gain], axis=-1)


def kv_kernel(
    prior_len, order, table, hidden, gain, w_key, w_value, key_gain, freq, prior_keys, prior_values,
    w_query, w_output,
    kv, prior, normed_out, cos_out, sin_out, w_query_out, w_send,
    order_s, table_s, hidden_v, gain_v, w_key_v, w_value_v, key_gain_v, freq_v, sems,
):
    rows = hidden.shape[0]
    blocks = rows // BLOCK
    me = lax.axis_index("seq")
    pairs = [
        (table, table_s), (order, order_s), (freq, freq_v), (key_gain, key_gain_v),
        (gain, gain_v), (hidden, hidden_v), (w_key, w_key_v), (w_value, w_value_v),
    ]
    copies = [pltpu.make_async_copy(a, b, sems.at[i]) for i, (a, b) in enumerate(pairs)]
    later = [
        pltpu.make_async_copy(w_query, w_query_out, sems.at[10]),
        pltpu.make_async_copy(
            w_output.at[half_rows(w_send, me % 2), columns(w_send, 1)], w_send, sems.at[11]
        ),
    ]
    for copy in copies + later:
        copy.start()
    copies[0].wait()
    first = me * prior_keys.shape[0]

    def look(i, found):
        slot = table_s[i] - first
        return jnp.where((slot >= 0) & (slot < prior_keys.shape[0]), slot, found)

    slot = lax.fori_loop(0, table.shape[0], look, 0)
    pages = [
        pltpu.make_async_copy(prior_keys.at[slot], prior.at[:, :128], sems.at[8]),
        pltpu.make_async_copy(prior_values.at[slot], prior.at[:, 128:], sems.at[9]),
    ]
    for copy in pages:
        copy.start()
    for copy in copies[1:4]:
        copy.wait()
    row = lax.broadcasted_iota(jnp.int32, (BLOCK, 128), 0)
    lane = lanes_of((BLOCK, 128))
    for b in range(blocks):
        base = prior_len + order_s[me * blocks + b] * BLOCK
        angle = (base + row).astype(F32) * freq_v[...]
        part = pl.ds(b * BLOCK, BLOCK)
        sine = jnp.sin(angle)
        cos_out[part, :] = jnp.cos(angle)
        sin_out[part, :] = jnp.where(lane % 64 < 32, -sine, sine)
    for copy in copies[4:6]:
        copy.wait()
    wide = hidden_v[...].astype(F32)
    mean = jnp.mean(wide * wide, axis=-1, keepdims=True)
    normed = (wide * lax.rsqrt(mean + EPS) * gain_v[...]).astype(BF16)
    normed_out[...] = normed
    for copy in copies[6:]:
        copy.wait()
    keys = jnp.dot(normed, w_key_v[...], preferred_element_type=F32)
    values = jnp.dot(normed, w_value_v[...], preferred_element_type=F32)
    rotated = norm_and_rotate(keys, twice(key_gain_v), cos_out[...], sin_out[...])
    kv[:, :128] = rotated.astype(BF16)
    kv[:, 128:] = values.astype(BF16)
    for copy in pages + later:
        copy.wait()


def half_rows(ref, core):
    return pl.ds(pl.multiple_of(core * ref.shape[0], ref.shape[0]), ref.shape[0])


def columns(ref, other):
    x = lax.axis_index("head")
    x = 1 - x if other else x
    return pl.ds(pl.multiple_of(x * ref.shape[1], ref.shape[1]), ref.shape[1])


def query_kernel(
    normed, w_query, cosine, sine, query_gain, order, live, masks,
    q_out, own_bias, span_bias, query_gain_v, order_s, live_s, masks_s, sems,
):
    pairs = [
        (order, order_s), (live, live_s), (masks, masks_s), (query_gain, query_gain_v)
    ]
    copies = [pltpu.make_async_copy(a, b, sems.at[i]) for i, (a, b) in enumerate(pairs)]
    for copy in copies:
        copy.start()
    rows = normed.shape[0]
    blocks = rows // BLOCK
    tiles = w_query.shape[1] // 128
    per_kv = tiles // 2
    group = 2 * per_kv
    queries = jnp.dot(normed[...], w_query[...], preferred_element_type=F32)
    for copy in copies:
        copy.wait()
    gain = twice(query_gain_v)
    left = lanes_of((rows, 128)) < 64
    for t in range(tiles):
        kv_head, u = divmod(t, per_kv)
        x = norm_and_rotate(queries[:, t * 128 : (t + 1) * 128], gain, cosine[...], sine[...])
        x = x * (64**-0.5 * LOG2E)
        turned = pltpu.roll(x, 64, 1)
        pair = (x, turned) if kv_head == 0 else (turned, x)
        for odd, head in enumerate(pair):
            kept = jnp.where(left if kv_head == 0 else ~left, head, 0.0)
            high = kept.astype(BF16)
            low = (kept - high.astype(F32)).astype(BF16)
            both = jnp.concatenate([high, low], axis=-1)
            for b in range(blocks):
                at = ((kv_head * blocks + b) * group + 2 * u + odd) * BLOCK
                q_out[at : at + BLOCK, :] = both[b * BLOCK : (b + 1) * BLOCK, :]

    me = lax.axis_index("seq")
    logical = [order_s[me * blocks + b] for b in range(blocks)]
    key_at = lanes_of((BLOCK, blocks * BLOCK))
    row = lax.broadcasted_iota(jnp.int32, key_at.shape, 0)
    for b in range(blocks):
        bias = jnp.full(key_at.shape, MASKED, F32)
        for kb in range(blocks):
            alive = live_s[logical[kb]] > 0
            here = key_at // BLOCK == kb
            if kb == b:
                here = here & (key_at % BLOCK <= row)
            else:
                alive = alive & (logical[kb] < logical[b])
            bias = jnp.where(here, jnp.where(alive, 0.0, MASKED), bias)
        own_bias[b * BLOCK : (b + 1) * BLOCK, :] = bias

    count = masks.shape[0]
    lane = lanes_of((1, PAGE))

    def visit(i, carry):
        rank = me ^ masks_s[i]
        held = [order_s[rank * 2 + half] for half in range(2)]
        alive = [(live_s[block] > 0) & (rank != me) for block in held]
        for b in range(blocks):
            value = [
                jnp.where(alive[h] & (held[h] < logical[b]), 0.0, MASKED) for h in range(2)
            ]
            at = pl.ds(pl.multiple_of(i * PAGE, PAGE), PAGE)
            span_bias[b : b + 1, at] = jnp.where(lane < BLOCK, value[0], value[1])
        return carry

    lax.fori_loop(0, count, visit, 0)


class Piece:
    def __init__(self, rows, biases):
        keys, values = rows[:, :128], rows[:, 128:]
        left = lanes_of(values.shape) < 64
        ones = jnp.ones_like(values)
        self.keys = jnp.concatenate([keys, keys], axis=-1)
        self.values = [jnp.where(left, values, ones), jnp.where(left, ones, values)]
        self.biases = biases


def fold(q, m_in, acc_in, m_out, acc_out, pieces, blocks, part):
    tiles = 2 * blocks
    scores, weights = {}, {}

    def score(t):
        rows = pl.ds(t * part, part)
        scores[t] = []
        for piece in pieces:
            s = lax.dot_general(
                q[rows, :], piece.keys, (((1,), (1,)), ((), ())), preferred_element_type=F32
            )
            scores[t].append(s if piece.biases is None else s + piece.biases[t % blocks])

    def weigh(t):
        rows = pl.ds(t * part, part)
        top = functools.reduce(jnp.maximum, [jnp.max(s, -1, keepdims=True) for s in scores[t]])
        factor = None
        if m_in is not None:
            old = m_in[rows, :1]
            top = jnp.maximum(top, old)
            factor = jnp.exp2(old - top)
        if m_out is not None:
            m_out[rows, :] = jnp.broadcast_to(top, (part, 128))
        weights[t] = [jnp.exp2(s - top).astype(BF16) for s in scores[t]], factor
        del scores[t]

    def mix(t):
        rows = pl.ds(t * part, part)
        parts, factor = weights.pop(t)
        total = 0.0 if factor is None else acc_in[rows, :] * factor
        for p, piece in zip(parts, pieces):
            total = total + jnp.dot(p, piece.values[t // blocks], preferred_element_type=F32)
        acc_out[rows, :] = total

    score(0)
    for t in range(tiles + 1):
        if t + 1 < tiles:
            score(t + 1)
        if t < tiles:
            weigh(t)
        if t > 0:
            mix(t - 1)


def attention_kernel(n_chunks, own, first, last, step, blocks, group, *refs):
    refs = list(refs)
    q = refs.pop(0)
    own_kv, own_bias = (refs.pop(0), refs.pop(0)) if own else (None, None)
    chunks = [refs.pop(0) for _ in range(n_chunks)]
    bias = None if own else refs.pop(0)
    m_in, acc_in = (None, None) if first else (refs.pop(0), refs.pop(0))
    out = refs.pop(0) if last else None
    m_ref, acc_ref = refs.pop(0), refs.pop(0)
    part = group * BLOCK

    def piece(rows, at):
        if bias is None:
            return Piece(rows, None)
        size = rows.shape[0]
        return Piece(rows, [bias[b : b + 1, pl.ds(at, size)] for b in range(blocks)])

    extra = []
    if own:
        mine = [own_bias[b * BLOCK : (b + 1) * BLOCK, :] for b in range(blocks)]
        extra = [Piece(own_kv[...], [jnp.concatenate([m] * group, axis=0) for m in mine])]
    if not refs:
        pieces, at = [], 0
        for chunk in chunks:
            pieces.append(piece(chunk[...], at))
            at += chunk.shape[0]
        fold(q, m_in, acc_in, m_ref, acc_ref, pieces + extra, blocks, part)
    else:
        held, sems = refs
        copies, at = [], 0
        for i, chunk in enumerate(chunks):
            size = chunk.shape[0]
            copies.append(pltpu.make_async_copy(chunk, held.at[pl.ds(at, size)], sems.at[i]))
            at += size
        for copy in copies:
            copy.start()
        for copy in copies:
            copy.wait()

        def visit(c, m_from, acc_from, more):
            first_row = pl.multiple_of(c * step, step)
            pieces = [piece(held[pl.ds(first_row, step), :], first_row)]
            fold(q, m_from, acc_from, m_ref, acc_ref, pieces + more, blocks, part)

        visit(0, m_in, acc_in, extra)
        pl.loop(1, at // step)(lambda c: visit(c, m_ref, acc_ref, []))

    if last:
        left = lanes_of((BLOCK, 128)) < 64
        for kv_head in range(2):
            for b in range(blocks):
                for u in range(group // 2):
                    heads = []
                    for odd in range(2):
                        at = ((kv_head * blocks + b) * group + 2 * u + odd) * BLOCK
                        acc = acc_ref[at : at + BLOCK, :]
                        ratio = acc / pltpu.roll(acc, 64, 1)
                        heads.append(pltpu.roll(ratio, 64, 1) if odd != kv_head else ratio)
                    both = jnp.where(left, heads[0], heads[1]).astype(BF16)
                    tile = kv_head * (group // 2) + u
                    out[b * BLOCK : (b + 1) * BLOCK, tile * 128 : (tile + 1) * 128] = both


def attention(q, own, chunks, bias, state, last, blocks, group):
    rows = sum(c.shape[0] for c in chunks)
    step = min(1024, rows)
    direct = rows <= 2048
    first = state is None
    operands = [q, *(own or ()), *chunks, *([] if bias is None else [bias]), *(state or ())]
    specs = [spec(VMEM)] * len(operands)
    if not direct:
        at = 1 + len(own or ())
        specs[at : at + len(chunks)] = [spec(pl.ANY)] * len(chunks)
    n = q.shape[0]
    pair = [jax.ShapeDtypeStruct((n, 128), F32)] * 2
    scratch = []
    if not direct:
        scratch = [VMEM((rows, 256), BF16), pltpu.SemaphoreType.DMA((len(chunks),))]
    if last:
        outs = jax.ShapeDtypeStruct((blocks * BLOCK, 2 * group * 64), BF16)
        out_specs = spec(VMEM)
        scratch = [VMEM((n, 128), F32)] * 2 + scratch
    else:
        outs, out_specs = pair, [spec(VMEM)] * 2
    return pl.pallas_call(
        functools.partial(
            attention_kernel, len(chunks), own is not None, first, last, step, blocks, group
        ),
        out_shape=outs,
        in_specs=specs,
        out_specs=out_specs,
        scratch_shapes=scratch,
        compiler_params=params(32),
        cost_estimate=cost(4 * n * rows * 256, rows * 512 + n * 2048),
    )(*operands)


def pages_kernel(n_chunks, dest, order, where, mine, w_output, *refs):
    chunks, (keys, values, partial, w_mine, sems) = refs[:n_chunks], refs[n_chunks:]
    me = lax.axis_index("seq")
    copy = pltpu.make_async_copy(w_output.at[:, columns(w_mine, 0)], w_mine, sems.at[2])
    copy.start()

    def find(table):
        def body(wanted):
            return lax.fori_loop(
                0, table.shape[0], lambda i, f: jnp.where(table[i] == wanted, i, f), 0
            )

        return body

    page = find(dest)(me)
    for half in range(2):
        source = find(order)(page * 2 + half)
        slot = where[me ^ (source // 2)]
        row = slot * PAGE + (source % 2) * BLOCK
        at = 0
        for chunk in chunks:
            size = chunk.shape[0]
            inside = (row >= at) & (row < at + size)

            @pl.when(inside)
            def _(chunk=chunk, at=at):
                rows = pl.ds(pl.multiple_of(row - at, BLOCK), BLOCK)
                to = pl.ds(half * BLOCK, BLOCK)
                a = pltpu.make_async_copy(chunk.at[rows, :128], keys.at[0, to], sems.at[0])
                b = pltpu.make_async_copy(chunk.at[rows, 128:], values.at[0, to], sems.at[1])
                a.start()
                b.start()
                a.wait()
                b.wait()

            at += size
    copy.wait()
    partial[...] = jnp.dot(mine[...], w_mine[...], preferred_element_type=F32)


def project_kernel(partial, peer, w_near, w_far, out):
    even = lax.axis_index("seq") % 2 == 0
    depth = w_near.shape[0]
    low, high = peer[:, :depth], peer[:, depth:]
    near = jnp.where(even, low, high)
    far = jnp.where(even, high, low)
    total = partial[...] + jnp.dot(near, w_near[...], preferred_element_type=F32)
    out[...] = total + jnp.dot(far, w_far[...], preferred_element_type=F32)


def plan(n):
    bits = [1 << i for i in range(n.bit_length() - 2, 0, -1)]
    return bits, bits[-1:] + bits[:-1]


def slot_masks(steps):
    masks = [0]
    for step in steps + [1]:
        masks = masks + [m ^ step for m in masks]
    return np.array(masks, np.int32)


def swap(x, n, step):
    return lax.ppermute(x, "seq", [(i, i ^ step) for i in range(n)])


def grow(held, n, step):
    return jnp.concatenate([held, swap(held, n, step)], axis=0)


def after(x, *others):
    return lax.optimization_barrier((x, *others))[0]


def body(
    n,
    hidden_in,
    attn_gain,
    w_query,
    w_key,
    w_value,
    query_gain,
    key_gain,
    w_output,
    prior_keys,
    prior_values,
    span_order,
    key_live,
    page_table,
    page_dest,
):
    rows, width = hidden_in.shape
    blocks = rows // BLOCK
    head_dim = query_gain.shape[0]
    group = w_query.shape[1] // w_key.shape[1]
    prior_len = page_table.shape[0] * PAGE
    out_width = w_output.shape[1] // 2
    depth = w_output.shape[0] // 2
    steps, span_steps = plan(n)
    masks = slot_masks(span_steps)
    where = np.zeros_like(masks)
    where[masks] = np.arange(n)
    half = head_dim // 2
    freq = np.tile((10000.0 ** (-np.arange(half) / half)).astype(np.float32), 4)[None, :]

    kv, prior, normed, cosine, sine, w_query, w_send = pl.pallas_call(
        functools.partial(kv_kernel, prior_len),
        out_shape=[
            jax.ShapeDtypeStruct((rows, 256), BF16),
            jax.ShapeDtypeStruct((PAGE, 256), BF16),
            jax.ShapeDtypeStruct((rows, width), BF16),
            jax.ShapeDtypeStruct((rows, 128), F32),
            jax.ShapeDtypeStruct((rows, 128), F32),
            jax.ShapeDtypeStruct(w_query.shape, BF16),
            jax.ShapeDtypeStruct((depth, out_width), BF16),
        ],
        in_specs=[spec(pltpu.HBM)] * 12,
        out_specs=[spec(VMEM)] * 7,
        scratch_shapes=[
            SMEM(span_order.shape, jnp.int32),
            SMEM(page_table.shape, jnp.int32),
            VMEM(hidden_in.shape, BF16),
            VMEM((1, width), F32),
            VMEM(w_key.shape, BF16),
            VMEM(w_value.shape, BF16),
            VMEM((1, head_dim), F32),
            VMEM((1, 128), F32),
            pltpu.SemaphoreType.DMA((12,)),
        ],
        compiler_params=params(),
        cost_estimate=cost(2 * rows * width * 256, 3 << 20),
    )(
        *in_hbm(
            span_order,
            page_table,
            hidden_in,
            attn_gain.reshape(1, -1),
            w_key,
            w_value,
            key_gain.reshape(1, -1),
            jnp.asarray(freq),
            prior_keys,
            prior_values,
            w_query,
            w_output,
        )
    )

    with jax.named_scope("prior_step_0"):
        prior = grow(prior, n, steps[0])
    with jax.named_scope("span_step_0"):
        span = grow(kv, n, span_steps[0])
    normed = after(normed, prior, span)
    with jax.named_scope("weights_step"):
        w_near = lax.ppermute(w_send, "head", [(0, 1), (1, 0)])
        w_far = swap(w_near, n, 1)
    q, own_bias, span_bias = pl.pallas_call(
        query_kernel,
        out_shape=[
            jax.ShapeDtypeStruct((2 * blocks * group * BLOCK, 256), BF16),
            jax.ShapeDtypeStruct((rows, rows), F32),
            jax.ShapeDtypeStruct((blocks, n * PAGE), F32),
        ],
        in_specs=[spec(VMEM)] * 4 + [spec(pltpu.HBM)] * 4,
        out_specs=[spec(VMEM)] * 3,
        scratch_shapes=[
            VMEM((1, head_dim), F32),
            SMEM(span_order.shape, jnp.int32),
            SMEM(key_live.shape, jnp.int32),
            SMEM((masks.size,), jnp.int32),
            pltpu.SemaphoreType.DMA((4,)),
        ],
        compiler_params=params(),
        cost_estimate=cost(2 * rows * width * 512, 4 << 20),
    )(
        normed,
        w_query,
        cosine,
        sine,
        *in_hbm(query_gain.reshape(1, -1), span_order, key_live, jnp.asarray(masks.reshape(-1))),
    )

    for i, step in enumerate(steps[1:-1], 1):
        with jax.named_scope(f"prior_step_{i}"):
            prior = grow(prior, n, step)
        with jax.named_scope(f"span_step_{i}"):
            span = grow(span, n, span_steps[i])
    prior, span, _ = lax.optimization_barrier((prior, span, q))
    with jax.named_scope("prior_last"):
        prior_same = [prior, swap(prior, n, steps[-1])]
    with jax.named_scope("span_last"):
        span_same = [span, swap(span, n, span_steps[-1])]
    with jax.named_scope("prior_core"):
        prior_other = [swap(c, n, 1) for c in prior_same]
    with jax.named_scope("span_core"):
        span_other = [swap(c, n, 1) for c in span_same]

    common = dict(blocks=blocks, group=group)
    edge = n // 2 * PAGE
    state = attention(q, (kv, own_bias), prior_same + prior_other, None, None, False, **common)
    state = attention(q, None, span_same, span_bias[:, :edge], state, False, **common)
    heads = attention(q, None, span_other, span_bias[:, edge:], state, True, **common)
    peer = lax.ppermute(heads, "head", [(0, 1), (1, 0)])

    all_span = span_same + span_other
    new_keys, new_values, partial = pl.pallas_call(
        functools.partial(pages_kernel, len(all_span)),
        out_shape=[jax.ShapeDtypeStruct((1, PAGE, 128), BF16)] * 2
        + [jax.ShapeDtypeStruct((rows, out_width), F32)],
        in_specs=[spec(SMEM)] * 3 + [spec(VMEM), spec(pltpu.HBM)] + [spec(pl.ANY)] * len(all_span),
        out_specs=[spec(VMEM)] * 3,
        scratch_shapes=[
            VMEM((w_output.shape[0], out_width), BF16),
            pltpu.SemaphoreType.DMA((3,)),
        ],
        compiler_params=params(),
        cost_estimate=cost(2 * rows * 512 * out_width, 1 << 21),
    )(page_dest, span_order, jnp.asarray(where), heads, *in_hbm(w_output), *all_span)

    attn_out = pl.pallas_call(
        project_kernel,
        out_shape=jax.ShapeDtypeStruct((rows, out_width), F32),
        in_specs=[spec(VMEM)] * 4,
        out_specs=spec(VMEM),
        compiler_params=params(),
        cost_estimate=cost(2 * rows * 512 * out_width, 2 << 20),
    )(partial, peer, w_near, w_far)
    return attn_out, new_keys, new_values


def solution(mesh):
    return jax.shard_map(
        functools.partial(body, mesh.shape["seq"]),
        mesh=mesh,
        in_specs=(
            P("seq", None),
            P(),
            P(None, "head"),
            P(None, "head"),
            P(None, "head"),
            P(),
            P(),
            P("head", None),
            P("seq", None, "head"),
            P("seq", None, "head"),
            P(),
            P(),
            P(),
            P(),
        ),
        out_specs=(P("seq", "head"), P("seq", None, "head"), P("seq", None, "head")),
        check_vma=False,
    )
```

time: 59.5 us -> 41.8 us (0.70)
  local copies, waits for them, and re-layouts: 9.47 us -> 0.04 us
  Pallas kernels: 22.4 us -> 15.2 us
  starting transfers between devices: 19.4 us -> 13.3 us
  waiting for transfers between devices: 6.74 us -> 12.3 us
    unnamed x37 -> x8, local copies, waits for them, and re-layouts: 8.16 us -> 0.03 us
    pallas_call x5 -> x4, Pallas kernels: 17.3 us -> 9.3 us  [the longest x3 7.16 us: attention(): pl.pallas_call(functools.partial(attention_kernel, len(chunks), own is no...]
    ppermute x17 -> x12, starting transfers between devices: 18.8 us -> 11.7 us  [the longest x11 10.2 us: swap(): return lax.ppermute(x, 'seq', [(i, i ^ step) for i in range(n)])]
    ppermute x17 -> x12, waiting for transfers between devices: 4.05 us -> 10.8 us  [the longest x11 10.8 us: swap(): return lax.ppermute(x, 'seq', [(i, i ^ step) for i in range(n)])]
    dynamic_slice x1 -> x0, local copies, waits for them, and re-layouts: 1.3 us -> none  [body(): lax.dynamic_slice_in_dim(w_output, (1 - x) * out_width, out_width, 1)]
    ppermute x1, waiting for transfers between devices: 2.69 us -> 1.48 us  [body(): peer = lax.ppermute(heads, 'head', [(0, 1), (1, 0)])]
    ppermute x1, starting transfers between devices: 0.59 us -> 1.55 us  [body(): peer = lax.ppermute(heads, 'head', [(0, 1), (1, 0)])]
    pallas_call x1, Pallas kernels: 1.42 us -> 2.33 us  [body(): pl.pallas_call(functools.partial(kv_kernel, prior_len), out_shape=[jax.Sh...]
  transfers between devices with their start and end apart: 18 -> 13, of which waited for: 3 -> 5; matrix products, arithmetic and copies ran while one was open for 2% -> 0% of each run, Pallas kernels for 34% -> 28%
where the time goes in v2:
time: 41.8 us; the launch traced here: 41.6 us
  Pallas kernels  15.2 us (36%)
  starting transfers between devices  13.3 us (32%)
  waiting for transfers between devices  12.3 us (29%)
  between operations  0.76 us (2%)
    ppermute x11, waiting for transfers between devices, swap(): return lax.ppermute(x, 'seq', [(i, i ^ step) for i in range(n)])  10.8 us
    ppermute x11, starting transfers between devices, swap(): return lax.ppermute(x, 'seq', [(i, i ^ step) for i in range(n)])  10.2 us
    pallas_call x3, Pallas kernels, attention(): pl.pallas_call(functools.partial(attention_kernel, len(chunks), own is no...  7.16 us
    pallas_call x1, Pallas kernels, body(): pl.pallas_call(functools.partial(pages_kernel, len(all_span)), out_shape=...  2.44 us
    pallas_call x1, Pallas kernels, body(): pl.pallas_call(functools.partial(kv_kernel, prior_len), out_shape=[jax.Sh...  2.33 us
    pallas_call x1, Pallas kernels, body(): pl.pallas_call(query_kernel, out_shape=[jax.ShapeDtypeStruct((2 * blocks...  2.14 us
    ppermute x1, starting transfers between devices, body(): peer = lax.ppermute(heads, 'head', [(0, 1), (1, 0)])  1.55 us
    ppermute x1, starting transfers between devices, body(): w_near = lax.ppermute(w_send, 'head', [(0, 1), (1, 0)])  1.49 us
  transfers between devices with their start and end apart: 13, of which 5 were waited for; matrix products, arithmetic and copies ran while one was open for 0% of the time, Pallas kernels for 28%

profile of v2, /device:TPU:0, one launch (start us, length us, event | category | flops | bytes accessed | tf_op | source)
XLA Modules:
  0.0 41.6 jit_solution(5959401144852287477)
XLA Ops:
  0.6 2.3 %shard_map.184 = (bf16[128,256]{1,0:T(8,128)(2,1)S(1)}, bf16[128,256]{1,0:T(8,128)(2,1)S(1)}, bf16[128,2048]{1,0:T(8,128)(2,1)S(1)}, f32[128,128]{1,0:T(8,128)S(...) custom-call(s32[32]{0:T(128)} %order.5, s32[16]{0:T(128)} %table.1, ...), custom_call_target="tpu_custom_call" | custom-call | flops 134217728 | bytes 3145728 | tf_op jit(solution)/shard_map/pallas_call | solution.py:458
  3.0 4.1 %collective-permute-start = (bf16[128,256]{1,0:T(8,128)(2,1)S(1)}, bf16[128,256]{1,0:T(8,128)(2,1)S(1)}, u32[]{:S(2)}, u32[]{:S(2)}) collective-permute-start(bf16[128,256]{1,0:T(8,128)(2,1)S(1)} %get-tuple-element.24), channel_id=1, source_target_pairs={{0,16},{2,18},{4,20},{6,22},{8,24},{10,26},{12,28},{14,30},{16,0},... | collective-permute-start | bytes 196616 | tf_op jit(solution)/shard_map/prior_step_0/ppermute | solution.py:416
  7.1 1.5 %collective-permute-start.1 = (bf16[128,256]{1,0:T(8,128)(2,1)S(1)}, bf16[128,256]{1,0:T(8,128)(2,1)S(1)}, u32[]{:S(2)}, u32[]{:S(2)}) collective-permute-start(bf16[128,256]{1,0:T(8,128)(2,1)S(1)} %get-tuple-element.25.refs_1_), channel_id=1, source_target_pairs={{0,4},{2,6},{4,0},{6,2},{8,12},{10,14},{12,8},{14,10},{16,20},{18,... | collective-permute-start | bytes 196616 | tf_op jit(solution)/shard_map/span_step_0/ppermute | solution.py:416
  8.6 1.5 %collective-permute-start.11 = (bf16[256,1024]{1,0:T(8,128)(2,1)S(1)}, bf16[256,1024]{1,0:T(8,128)(2,1)S(1)}, u32[]{:S(2)}, u32[]{:S(2)}) collective-permute-start(bf16[256,1024]{1,0:T(8,128)(2,1)S(1)} %get-tuple-element.40), channel_id=1, source_target_pairs={{0,1},{1,0},{2,3},{3,2},{4,5},{5,4},{6,7},{7,6},{8,9},{9,8},{10,11... | collective-permute-start | bytes 1572872 | tf_op jit(solution)/shard_map/weights_step/ppermute | solution.py:507
  10.1 1.2 %collective-permute-done.1 = bf16[128,256]{1,0:T(8,128)(2,1)S(1)} collective-permute-done((bf16[128,256]{1,0:T(8,128)(2,1)S(1)}, bf16[128,256]{1,0:T(8,128)(2,1)S(1)}, u32[]{:S(2)}, u32[]{:S(2)}) %collective-permute-start.1) | collective-permute-done | bytes 65568 | tf_op jit(solution)/shard_map/span_step_0/ppermute | solution.py:416
  11.3 0.1 collective-permute-start.3
  11.4 0.0 collective-permute-done
  11.4 1.9 %collective-permute-start.2 = (bf16[256,256]{1,0:T(8,128)(2,1)S(1)}, bf16[256,256]{1,0:T(8,128)(2,1)S(1)}, u32[]{:S(2)}, u32[]{:S(2)}) collective-permute-start(bf16[256,256]{1,0:T(8,128)(2,1)S(1)} %constant_dynamic-update-slice_fusion), channel_id=1, source_target_pairs={{0,8},{2,10},{4,12},{6,14},{8,0},{10,2},{12,4},{14,6},{16,24},{18,... | collective-permute-start | bytes 393224 | tf_op jit(solution)/shard_map/prior_step_1/ppermute | solution.py:416
  13.3 2.1 %shard_map.185 = (bf16[1024,256]{1,0:T(8,128)(2,1)S(1)}, f32[128,128]{1,0:T(8,128)S(1)}, f32[2,2048]{1,0:T(2,128)S(1)}) custom-call(bf16[128,2048]{1,0:T(8,128)(2,1)S(1)} %get-tuple-element.26.normed, bf16[2048,512]{1,0:T(8,128)(2,1)S(1)} %get-tuple-element.27.w_query, f32[128,128]{1,0:T(8,128)S(1)} %get-tuple-element.28.cosine, ...), custom_call_target="tpu_custom_call" | custom-call | flops 268435456 | bytes 4194304 | tf_op jit(solution)/shard_map/pallas_call | solution.py:509
  15.5 3.7 %collective-permute-done.3 = bf16[256,256]{1,0:T(8,128)(2,1)S(1)} collective-permute-done((bf16[256,256]{1,0:T(8,128)(2,1)S(1)}, bf16[256,256]{1,0:T(8,128)(2,1)S(1)}, u32[]{:S(2)}, u32[]{:S(2)}) %collective-permute-start.3) | collective-permute-done | bytes 131104 | tf_op jit(solution)/shard_map/span_step_1/ppermute | solution.py:416
  19.2 0.0 collective-permute-done.2
  19.3 1.6 %collective-permute-start.7 = (bf16[512,256]{1,0:T(8,128)(2,1)S(1)}, bf16[512,256]{1,0:T(8,128)(2,1)S(1)}, u32[]{:S(2)}, u32[]{:S(2)}) collective-permute-start(bf16[512,256]{1,0:T(8,128)(2,1)S(1)} %pad_maximum_fusion.refs_3_), channel_id=1, source_target_pairs={{0,4},{2,6},{4,0},{6,2},{8,12},{10,14},{12,8},{14,10},{16,20},{18,... | collective-permute-start | bytes 786440 | tf_op jit(solution)/shard_map/prior_last/ppermute | solution.py:416
  20.8 0.0 collective-permute-start.8
  20.9 4.8 %collective-permute-done.7.refs_4_ = bf16[512,256]{1,0:T(8,128)(2,1)S(1)} collective-permute-done((bf16[512,256]{1,0:T(8,128)(2,1)S(1)}, bf16[512,256]{1,0:T(8,128)(2,1)S(1)}, u32[]{:S(2)}, u32[]{:S(2)}) %collective-permute-start.7) | collective-permute-done | bytes 262176 | tf_op jit(solution)/shard_map/prior_last/ppermute | solution.py:416
  25.7 0.0 collective-permute-start.9
  25.7 0.5 %collective-permute-start.4 = (bf16[512,256]{1,0:T(8,128)(2,1)S(1)}, bf16[512,256]{1,0:T(8,128)(2,1)S(1)}, u32[]{:S(2)}, u32[]{:S(2)}) collective-permute-start(bf16[512,256]{1,0:T(8,128)(2,1)S(1)} %pad_maximum_fusion.1.refs_1_.refs_0_), channel_id=1, source_target_pairs={{0,2},{2,0},{4,6},{6,4},{8,10},{10,8},{12,14},{14,12},{16,18},{18,... | collective-permute-start | bytes 786440 | tf_op jit(solution)/shard_map/span_core/ppermute | solution.py:416
  26.2 1.0 %collective-permute-done.5.refs_2_.refs_1_ = bf16[512,256]{1,0:T(8,128)(2,1)S(1)} collective-permute-done((bf16[512,256]{1,0:T(8,128)(2,1)S(1)}, bf16[512,256]{1,0:T(8,128)(2,1)S(1)}, u32[]{:S(2)}, u32[]{:S(2)}) %collective-permute-start.5) | collective-permute-done | bytes 262176 | tf_op jit(solution)/shard_map/span_last/ppermute | solution.py:416
  27.2 0.0 collective-permute-start.6
  27.2 0.0 collective-permute-done.11.w_near
  27.2 0.5 %collective-permute-start.12 = (bf16[256,1024]{1,0:T(8,128)(2,1)S(1)}, bf16[256,1024]{1,0:T(8,128)(2,1)S(1)}, u32[]{:S(2)}, u32[]{:S(2)}) collective-permute-start(bf16[256,1024]{1,0:T(8,128)(2,1)S(1)} %collective-permute-done.11.w_near), channel_id=1, source_target_pairs={{0,2},{2,0},{4,6},{6,4},{8,10},{10,8},{12,14},{14,12},{16,18},{18,... | collective-permute-start | bytes 1572872 | tf_op jit(solution)/shard_map/weights_step/ppermute | solution.py:416
  27.7 0.0 collective-permute-done.8.refs_5_
  27.7 2.9 %shard_map.186 = (f32[1024,128]{1,0:T(8,128)S(1)}, f32[1024,128]{1,0:T(8,128)S(1)}) custom-call(bf16[1024,256]{1,0:T(8,128)(2,1)S(1)} %get-tuple-element.30.refs_0_, bf16[128,256]{1,0:T(8,128)(2,1)S(1)} %get-tuple-element.25.refs_1_, f32[128,128]{1,0:T(8,128)S(1)} %get-tuple-element.33.refs_2_, bf16[512,256]{1,0:T(8,128)(2,1)S(1)} %pad_maximum_fusion.refs_3_, ...), custom_call_target="tpu_custom_call" | custom-call | flops 2147483648 | bytes 3145728 | tf_op jit(solution)/shard_map/pallas_call | solution.py:340
  30.6 1.8 %shard_map.187 = (f32[1024,128]{1,0:T(8,128)S(1)}, f32[1024,128]{1,0:T(8,128)S(1)}) custom-call(bf16[1024,256]{1,0:T(8,128)(2,1)S(1)} %get-tuple-element.30.refs_0_, bf16[512,256]{1,0:T(8,128)(2,1)S(1)} %pad_maximum_fusion.1.refs_1_.refs_0_, bf16[512,256]{1,0:T(8,128)(2,1)S(1)} %collective-permute-done.5.refs_2_.refs_1_, ...), custom_call_target="tpu_custom_call" | custom-call | flops 1073741824 | bytes 2621440 | tf_op jit(solution)/shard_map/pallas_call | solution.py:340
  32.4 0.0 copy-start
  32.4 0.0 copy-start.1
  32.4 0.0 copy-start.2
  32.4 0.0 collective-permute-done.6.refs_2_.refs_3_
  32.4 2.5 %shard_map.188.mine = bf16[128,512]{1,0:T(8,128)(2,1)S(1)} custom-call(bf16[1024,256]{1,0:T(8,128)(2,1)S(1)} %get-tuple-element.30.refs_0_, bf16[512,256]{1,0:T(8,128)(2,1)S(1)} %collective-permute-done.4.refs_1_.refs_2_, bf16[512,256]{1,0:T(8,128)(2,1)S(1)} %collective-permute-done.6.refs_2_.refs_3_, f32[2,1024]{1,0:T(2,128)S(1)} %get-tuple-element.44.refs_3_, ...), custom_call_target="tpu_custom_call" | custom-call | flops 1073741824 | bytes 2621440 | tf_op jit(solution)/shard_map/pallas_call | solution.py:340
  35.0 1.6 %collective-permute-start.10 = (bf16[128,512]{1,0:T(8,128)(2,1)S(1)}, bf16[128,512]{1,0:T(8,128)(2,1)S(1)}, u32[]{:S(2)}, u32[]{:S(2)}) collective-permute-start(bf16[128,512]{1,0:T(8,128)(2,1)S(1)} %shard_map.188.mine), channel_id=1, source_target_pairs={{0,1},{1,0},{2,3},{3,2},{4,5},{5,4},{6,7},{7,6},{8,9},{9,8},{10,11... | collective-permute-start | bytes 393224 | tf_op jit(solution)/shard_map/ppermute | solution.py:555
  36.5 2.4 %shard_map.189 = (bf16[1,128,128]{2,1,0:T(8,128)(2,1)}, bf16[1,128,128]{2,1,0:T(8,128)(2,1)}, f32[128,1024]{1,0:T(8,128)S(1)}) custom-call(s32[16]{0:T(128)S(1)} %copy-done.1, s32[32]{0:T(128)S(1)} %copy-done, s32[16]{0:T(128)S(1)} %copy-done.2, bf16[128,512]{1,0:T(8,128)(2,1)S(1)} %shard_map.188.mine, bf16[512,2048]{1,0:T(8,128)(2,1)} %w_output.3, ...), custom_call_target="tpu_custom_call" | custom-call | flops 134217728 | bytes 2097152 | tf_op jit(solution)/shard_map/pallas_call | solution.py:558
  39.0 1.5 %collective-permute-done.10.peer = bf16[128,512]{1,0:T(8,128)(2,1)S(1)} collective-permute-done((bf16[128,512]{1,0:T(8,128)(2,1)S(1)}, bf16[128,512]{1,0:T(8,128)(2,1)S(1)}, u32[]{:S(2)}, u32[]{:S(2)}) %collective-permute-start.10) | collective-permute-done | bytes 131104 | tf_op jit(solution)/shard_map/ppermute | solution.py:555
  40.5 1.1 %shard_map.190 = f32[128,1024]{1,0:T(8,128)} custom-call(f32[128,1024]{1,0:T(8,128)S(1)} %get-tuple-element.39.partial, bf16[128,512]{1,0:T(8,128)(2,1)S(1)} %collective-permute-done.10.peer, bf16[256,1024]{1,0:T(8,128)(2,1)S(1)} %collective-permute-done.11.w_near, bf16[256,1024]{1,0:T(8,128)(2,1)S(1)} %collective-permute-done.12.w_far), custom_call_target="tpu_custom_call" | custom-call | flops 134217728 | bytes 2097152 | tf_op jit(solution)/shard_map/pallas_call | solution.py:572
  (14 shorter events, 0.1 us)
Async XLA Ops:
  3.0 8.5 %collective-permute-start = (bf16[128,256]{1,0:T(8,128)(2,1)S(1)}, bf16[128,256]{1,0:T(8,128)(2,1)S(1)}, u32[]{:S(2)}, u32[]{:S(2)}) collective-permute-start(bf16[128,256]{1,0:T(8,128)(2,1)S(1)} %get-tuple-element.24), channel_id=1, source_target_pairs={{0,16},{2,18},{4,20},{6,22},{8,24},{10,26},{12,28},{14,30},{16,0},... | collective-permute-start | bytes 196616 | tf_op jit(solution)/shard_map/prior_step_0/ppermute | solution.py:416
  7.1 4.3 %collective-permute-start.1 = (bf16[128,256]{1,0:T(8,128)(2,1)S(1)}, bf16[128,256]{1,0:T(8,128)(2,1)S(1)}, u32[]{:S(2)}, u32[]{:S(2)}) collective-permute-start(bf16[128,256]{1,0:T(8,128)(2,1)S(1)} %get-tuple-element.25.refs_1_), channel_id=1, source_target_pairs={{0,4},{2,6},{4,0},{6,2},{8,12},{10,14},{12,8},{14,10},{16,20},{18,... | collective-permute-start | bytes 196616 | tf_op jit(solution)/shard_map/span_step_0/ppermute | solution.py:416
  8.6 18.6 %collective-permute-start.11 = (bf16[256,1024]{1,0:T(8,128)(2,1)S(1)}, bf16[256,1024]{1,0:T(8,128)(2,1)S(1)}, u32[]{:S(2)}, u32[]{:S(2)}) collective-permute-start(bf16[256,1024]{1,0:T(8,128)(2,1)S(1)} %get-tuple-element.40), channel_id=1, source_target_pairs={{0,1},{1,0},{2,3},{3,2},{4,5},{5,4},{6,7},{7,6},{8,9},{9,8},{10,11... | collective-permute-start | bytes 1572872 | tf_op jit(solution)/shard_map/weights_step/ppermute | solution.py:507
  11.3 7.9 %collective-permute-start.3 = (bf16[256,256]{1,0:T(8,128)(2,1)S(1)}, bf16[256,256]{1,0:T(8,128)(2,1)S(1)}, u32[]{:S(2)}, u32[]{:S(2)}) collective-permute-start(bf16[256,256]{1,0:T(8,128)(2,1)S(1)} %constant_dynamic-update-slice_fusion.2), channel_id=1, source_target_pairs={{0,16},{2,18},{4,20},{6,22},{8,24},{10,26},{12,28},{14,30},{16,0},... | collective-permute-start | bytes 393224 | tf_op jit(solution)/shard_map/span_step_1/ppermute | solution.py:416
  11.4 7.8 %collective-permute-start.2 = (bf16[256,256]{1,0:T(8,128)(2,1)S(1)}, bf16[256,256]{1,0:T(8,128)(2,1)S(1)}, u32[]{:S(2)}, u32[]{:S(2)}) collective-permute-start(bf16[256,256]{1,0:T(8,128)(2,1)S(1)} %constant_dynamic-update-slice_fusion), channel_id=1, source_target_pairs={{0,8},{2,10},{4,12},{6,14},{8,0},{10,2},{12,4},{14,6},{16,24},{18,... | collective-permute-start | bytes 393224 | tf_op jit(solution)/shard_map/prior_step_1/ppermute | solution.py:416
  19.3 6.4 %collective-permute-start.7 = (bf16[512,256]{1,0:T(8,128)(2,1)S(1)}, bf16[512,256]{1,0:T(8,128)(2,1)S(1)}, u32[]{:S(2)}, u32[]{:S(2)}) collective-permute-start(bf16[512,256]{1,0:T(8,128)(2,1)S(1)} %pad_maximum_fusion.refs_3_), channel_id=1, source_target_pairs={{0,4},{2,6},{4,0},{6,2},{8,12},{10,14},{12,8},{14,10},{16,20},{18,... | collective-permute-start | bytes 786440 | tf_op jit(solution)/shard_map/prior_last/ppermute | solution.py:416
  20.8 6.4 %collective-permute-start.5 = (bf16[512,256]{1,0:T(8,128)(2,1)S(1)}, bf16[512,256]{1,0:T(8,128)(2,1)S(1)}, u32[]{:S(2)}, u32[]{:S(2)}) collective-permute-start(bf16[512,256]{1,0:T(8,128)(2,1)S(1)} %pad_maximum_fusion.1.refs_1_.refs_0_), channel_id=1, source_target_pairs={{0,8},{2,10},{4,12},{6,14},{8,0},{10,2},{12,4},{14,6},{16,24},{18,... | collective-permute-start | bytes 786440 | tf_op jit(solution)/shard_map/span_last/ppermute | solution.py:416
  20.8 6.9 %collective-permute-start.8 = (bf16[512,256]{1,0:T(8,128)(2,1)S(1)}, bf16[512,256]{1,0:T(8,128)(2,1)S(1)}, u32[]{:S(2)}, u32[]{:S(2)}) collective-permute-start(bf16[512,256]{1,0:T(8,128)(2,1)S(1)} %pad_maximum_fusion.refs_3_), channel_id=1, source_target_pairs={{0,2},{2,0},{4,6},{6,4},{8,10},{10,8},{12,14},{14,12},{16,18},{18,... | collective-permute-start | bytes 786440 | tf_op jit(solution)/shard_map/prior_core/ppermute | solution.py:416
  25.7 2.0 %collective-permute-start.9 = (bf16[512,256]{1,0:T(8,128)(2,1)S(1)}, bf16[512,256]{1,0:T(8,128)(2,1)S(1)}, u32[]{:S(2)}, u32[]{:S(2)}) collective-permute-start(bf16[512,256]{1,0:T(8,128)(2,1)S(1)} %collective-permute-done.7.refs_4_), channel_id=1, source_target_pairs={{0,2},{2,0},{4,6},{6,4},{8,10},{10,8},{12,14},{14,12},{16,18},{18,... | collective-permute-start | bytes 786440 | tf_op jit(solution)/shard_map/prior_core/ppermute | solution.py:416
  25.7 6.7 %collective-permute-start.4 = (bf16[512,256]{1,0:T(8,128)(2,1)S(1)}, bf16[512,256]{1,0:T(8,128)(2,1)S(1)}, u32[]{:S(2)}, u32[]{:S(2)}) collective-permute-start(bf16[512,256]{1,0:T(8,128)(2,1)S(1)} %pad_maximum_fusion.1.refs_1_.refs_0_), channel_id=1, source_target_pairs={{0,2},{2,0},{4,6},{6,4},{8,10},{10,8},{12,14},{14,12},{16,18},{18,... | collective-permute-start | bytes 786440 | tf_op jit(solution)/shard_map/span_core/ppermute | solution.py:416
  27.2 5.2 %collective-permute-start.6 = (bf16[512,256]{1,0:T(8,128)(2,1)S(1)}, bf16[512,256]{1,0:T(8,128)(2,1)S(1)}, u32[]{:S(2)}, u32[]{:S(2)}) collective-permute-start(bf16[512,256]{1,0:T(8,128)(2,1)S(1)} %collective-permute-done.5.refs_2_.refs_1_), channel_id=1, source_target_pairs={{0,2},{2,0},{4,6},{6,4},{8,10},{10,8},{12,14},{14,12},{16,18},{18,... | collective-permute-start | bytes 786440 | tf_op jit(solution)/shard_map/span_core/ppermute | solution.py:416
  27.2 13.2 %collective-permute-start.12 = (bf16[256,1024]{1,0:T(8,128)(2,1)S(1)}, bf16[256,1024]{1,0:T(8,128)(2,1)S(1)}, u32[]{:S(2)}, u32[]{:S(2)}) collective-permute-start(bf16[256,1024]{1,0:T(8,128)(2,1)S(1)} %collective-permute-done.11.w_near), channel_id=1, source_target_pairs={{0,2},{2,0},{4,6},{6,4},{8,10},{10,8},{12,14},{14,12},{16,18},{18,... | collective-permute-start | bytes 1572872 | tf_op jit(solution)/shard_map/weights_step/ppermute | solution.py:416
  32.4 4.1 %copy-start = (s32[32]{0:T(128)S(1)}, s32[32]{0:T(128)}, u32[]{:S(2)}) copy-start(s32[32]{0:T(128)} %order.5) | copy-start | bytes 388
  32.4 4.1 %copy-start.1 = (s32[16]{0:T(128)S(1)}, s32[16]{0:T(128)}, u32[]{:S(2)}) copy-start(s32[16]{0:T(128)} %dest.1) | copy-start | bytes 196
  32.4 4.1 %copy-start.2 = (s32[16]{0:T(128)S(1)}, s32[16]{0:T(128)}, u32[]{:S(2)}) copy-start(s32[16]{0:T(128)} %constant.8.clone.where) | copy-start | bytes 196
  35.0 5.5 %collective-permute-start.10 = (bf16[128,512]{1,0:T(8,128)(2,1)S(1)}, bf16[128,512]{1,0:T(8,128)(2,1)S(1)}, u32[]{:S(2)}, u32[]{:S(2)}) collective-permute-start(bf16[128,512]{1,0:T(8,128)(2,1)S(1)} %shard_map.188.mine), channel_id=1, source_target_pairs={{0,1},{1,0},{2,3},{3,2},{4,5},{5,4},{6,7},{7,6},{8,9},{9,8},{10,11... | collective-permute-start | bytes 393224 | tf_op jit(solution)/shard_map/ppermute | solution.py:555

commit v3 on v2

--- a/solution.py
+++ b/solution.py
@@ -58,8 +58,8 @@
 
 def kv_kernel(
     prior_len, order, table, hidden, gain, w_key, w_value, key_gain, freq, prior_keys, prior_values,
-    w_query, w_output,
-    kv, prior, normed_out, cos_out, sin_out, w_query_out, w_send,
+    w_output,
+    kv, prior, normed_out, cos_out, sin_out, w_send,
     order_s, table_s, hidden_v, gain_v, w_key_v, w_value_v, key_gain_v, freq_v, sems,
 ):
     rows = hidden.shape[0]
@@ -71,9 +71,8 @@
     ]
     copies = [pltpu.make_async_copy(a, b, sems.at[i]) for i, (a, b) in enumerate(pairs)]
     later = [
-        pltpu.make_async_copy(w_query, w_query_out, sems.at[10]),
         pltpu.make_async_copy(
-            w_output.at[half_rows(w_send, me % 2), columns(w_send, 1)], w_send, sems.at[11]
+            w_output.at[half_rows(w_send, me % 2), columns(w_send, 1)], w_send, sems.at[10]
         ),
     ]
     for copy in copies + later:
@@ -131,12 +130,9 @@
 
 
 def query_kernel(
-    normed, w_query, cosine, sine, query_gain, order, live, masks,
-    q_out, own_bias, span_bias, query_gain_v, order_s, live_s, masks_s, sems,
+    normed, cosine, sine, w_query, query_gain, q_out, w_query_v, query_gain_v, sems
 ):
-    pairs = [
-        (order, order_s), (live, live_s), (masks, masks_s), (query_gain, query_gain_v)
-    ]
+    pairs = [(w_query, w_query_v), (query_gain, query_gain_v)]
     copies = [pltpu.make_async_copy(a, b, sems.at[i]) for i, (a, b) in enumerate(pairs)]
     for copy in copies:
         copy.start()
@@ -145,9 +141,9 @@
     tiles = w_query.shape[1] // 128
     per_kv = tiles // 2
     group = 2 * per_kv
-    queries = jnp.dot(normed[...], w_query[...], preferred_element_type=F32)
     for copy in copies:
         copy.wait()
+    queries = jnp.dot(normed[...], w_query_v[...], preferred_element_type=F32)
     gain = twice(query_gain_v)
     left = lanes_of((rows, 128)) < 64
     for t in range(tiles):
@@ -165,6 +161,14 @@
                 at = ((kv_head * blocks + b) * group + 2 * u + odd) * BLOCK
                 q_out[at : at + BLOCK, :] = both[b * BLOCK : (b + 1) * BLOCK, :]
 
+
+def mask_kernel(blocks, order, live, masks, turn, own_bias, span_bias, order_s, live_s, masks_s, sems):
+    pairs = [(order, order_s), (live, live_s), (masks, masks_s)]
+    copies = [pltpu.make_async_copy(a, b, sems.at[i]) for i, (a, b) in enumerate(pairs)]
+    for copy in copies:
+        copy.start()
+    for copy in copies:
+        copy.wait()
     me = lax.axis_index("seq")
     logical = [order_s[me * blocks + b] for b in range(blocks)]
     key_at = lanes_of((BLOCK, blocks * BLOCK))
@@ -209,7 +213,7 @@
         self.biases = biases
 
 
-def fold(q, m_in, acc_in, m_out, acc_out, pieces, blocks, part):
+def fold(q, m_in, acc_in, m_out, acc_out, pieces, blocks, part, finish=None):
     tiles = 2 * blocks
     scores, weights = {}, {}
 
@@ -230,7 +234,7 @@
             old = m_in[rows, :1]
             top = jnp.maximum(top, old)
             factor = jnp.exp2(old - top)
-        if m_out is not None:
+        if finish is None:
             m_out[rows, :] = jnp.broadcast_to(top, (part, 128))
         weights[t] = [jnp.exp2(s - top).astype(BF16) for s in scores[t]], factor
         del scores[t]
@@ -241,7 +245,10 @@
         total = 0.0 if factor is None else acc_in[rows, :] * factor
         for p, piece in zip(parts, pieces):
             total = total + jnp.dot(p, piece.values[t // blocks], preferred_element_type=F32)
-        acc_out[rows, :] = total
+        if finish is None:
+            acc_out[rows, :] = total
+        else:
+            finish(t, total)
 
     score(0)
     for t in range(tiles + 1):
@@ -253,19 +260,19 @@
             mix(t - 1)
 
 
-def attention_kernel(n_chunks, own, first, last, step, blocks, group, *refs):
+def attention_kernel(offsets, own, first, last, step, blocks, group, *refs):
     refs = list(refs)
     q = refs.pop(0)
     own_kv, own_bias = (refs.pop(0), refs.pop(0)) if own else (None, None)
-    chunks = [refs.pop(0) for _ in range(n_chunks)]
-    bias = None if own else refs.pop(0)
+    chunks = [refs.pop(0) for _ in offsets]
+    bias = refs.pop(0)
     m_in, acc_in = (None, None) if first else (refs.pop(0), refs.pop(0))
     out = refs.pop(0) if last else None
     m_ref, acc_ref = refs.pop(0), refs.pop(0)
     part = group * BLOCK
 
     def piece(rows, at):
-        if bias is None:
+        if at is None:
             return Piece(rows, None)
         size = rows.shape[0]
         return Piece(rows, [bias[b : b + 1, pl.ds(at, size)] for b in range(blocks)])
@@ -274,63 +281,66 @@
     if own:
         mine = [own_bias[b * BLOCK : (b + 1) * BLOCK, :] for b in range(blocks)]
         extra = [Piece(own_kv[...], [jnp.concatenate([m] * group, axis=0) for m in mine])]
+
+    def finish(t, acc):
+        kv_head, b = divmod(t, blocks)
+        left = lanes_of((BLOCK, 128)) < 64
+        for u in range(group // 2):
+            even = acc[2 * u * BLOCK : (2 * u + 1) * BLOCK, :]
+            odd = acc[(2 * u + 1) * BLOCK : (2 * u + 2) * BLOCK, :]
+            even_t, odd_t = pltpu.roll(even, 64, 1), pltpu.roll(odd, 64, 1)
+            if kv_head == 0:
+                top, low = jnp.where(left, even, odd_t), jnp.where(left, even_t, odd)
+            else:
+                top, low = jnp.where(left, even_t, odd), jnp.where(left, even, odd_t)
+            tile = kv_head * (group // 2) + u
+            rows = slice(b * BLOCK, (b + 1) * BLOCK)
+            out[rows, tile * 128 : (tile + 1) * 128] = (top / low).astype(BF16)
+
     if not refs:
-        pieces, at = [], 0
-        for chunk in chunks:
-            pieces.append(piece(chunk[...], at))
-            at += chunk.shape[0]
-        fold(q, m_in, acc_in, m_ref, acc_ref, pieces + extra, blocks, part)
-    else:
-        held, sems = refs
-        copies, at = [], 0
-        for i, chunk in enumerate(chunks):
-            size = chunk.shape[0]
-            copies.append(pltpu.make_async_copy(chunk, held.at[pl.ds(at, size)], sems.at[i]))
-            at += size
-        for copy in copies:
+        pieces = [piece(chunk[...], at) for chunk, at in zip(chunks, offsets)]
+        fold(
+            q, m_in, acc_in, m_ref, acc_ref, pieces + extra, blocks, part, finish if last else None
+        )
+        return
+    held, sem = refs
+    if own:
+        fold(q, m_in, acc_in, m_ref, acc_ref, extra, blocks, part)
+    elif not first:
+        m_ref[...] = m_in[...]
+        acc_ref[...] = acc_in[...]
+    for chunk, at in zip(chunks, offsets):
+
+        def visit(c, chunk=chunk, at=at):
+            first_row = pl.multiple_of(c * step, step)
+            copy = pltpu.make_async_copy(chunk.at[pl.ds(first_row, step)], held, sem)
             copy.start()
-        for copy in copies:
             copy.wait()
-
-        def visit(c, m_from, acc_from, more):
-            first_row = pl.multiple_of(c * step, step)
-            pieces = [piece(held[pl.ds(first_row, step), :], first_row)]
-            fold(q, m_from, acc_from, m_ref, acc_ref, pieces + more, blocks, part)
-
-        visit(0, m_in, acc_in, extra)
-        pl.loop(1, at // step)(lambda c: visit(c, m_ref, acc_ref, []))
-
+            pieces = [piece(held[...], None if at is None else at + first_row)]
+            fold(q, m_ref, acc_ref, m_ref, acc_ref, pieces, blocks, part)
+
+        pl.loop(0, chunk.shape[0] // step)(visit)
     if last:
-        left = lanes_of((BLOCK, 128)) < 64
-        for kv_head in range(2):
-            for b in range(blocks):
-                for u in range(group // 2):
-                    heads = []
-                    for odd in range(2):
-                        at = ((kv_head * blocks + b) * group + 2 * u + odd) * BLOCK
-                        acc = acc_ref[at : at + BLOCK, :]
-                        ratio = acc / pltpu.roll(acc, 64, 1)
-                        heads.append(pltpu.roll(ratio, 64, 1) if odd != kv_head else ratio)
-                    both = jnp.where(left, heads[0], heads[1]).astype(BF16)
-                    tile = kv_head * (group // 2) + u
-                    out[b * BLOCK : (b + 1) * BLOCK, tile * 128 : (tile + 1) * 128] = both
+        for t in range(2 * blocks):
+            finish(t, acc_ref[t * part : (t + 1) * part, :])
 
 
 def attention(q, own, chunks, bias, state, last, blocks, group):
-    rows = sum(c.shape[0] for c in chunks)
-    step = min(1024, rows)
+    arrays, offsets = zip(*chunks)
+    rows = sum(c.shape[0] for c in arrays)
     direct = rows <= 2048
+    step = min(1024, *(c.shape[0] for c in arrays))
     first = state is None
-    operands = [q, *(own or ()), *chunks, *([] if bias is None else [bias]), *(state or ())]
+    operands = [q, *(own or ()), *arrays, bias, *(state or ())]
     specs = [spec(VMEM)] * len(operands)
     if not direct:
         at = 1 + len(own or ())
-        specs[at : at + len(chunks)] = [spec(pl.ANY)] * len(chunks)
+        specs[at : at + len(arrays)] = [spec(pl.ANY)] * len(arrays)
     n = q.shape[0]
     pair = [jax.ShapeDtypeStruct((n, 128), F32)] * 2
     scratch = []
     if not direct:
-        scratch = [VMEM((rows, 256), BF16), pltpu.SemaphoreType.DMA((len(chunks),))]
+        scratch = [VMEM((step, 256), BF16), pltpu.SemaphoreType.DMA]
     if last:
         outs = jax.ShapeDtypeStruct((blocks * BLOCK, 2 * group * 64), BF16)
         out_specs = spec(VMEM)
@@ -339,7 +349,7 @@
         outs, out_specs = pair, [spec(VMEM)] * 2
     return pl.pallas_call(
         functools.partial(
-            attention_kernel, len(chunks), own is not None, first, last, step, blocks, group
+            attention_kernel, offsets, own is not None, first, last, step, blocks, group
         ),
         out_shape=outs,
         in_specs=specs,
@@ -455,7 +465,7 @@
     half = head_dim // 2
     freq = np.tile((10000.0 ** (-np.arange(half) / half)).astype(np.float32), 4)[None, :]
 
-    kv, prior, normed, cosine, sine, w_query, w_send = pl.pallas_call(
+    kv, prior, normed, cosine, sine, w_send = pl.pallas_call(
         functools.partial(kv_kernel, prior_len),
         out_shape=[
             jax.ShapeDtypeStruct((rows, 256), BF16),
@@ -463,11 +473,10 @@
             jax.ShapeDtypeStruct((rows, width), BF16),
             jax.ShapeDtypeStruct((rows, 128), F32),
             jax.ShapeDtypeStruct((rows, 128), F32),
-            jax.ShapeDtypeStruct(w_query.shape, BF16),
             jax.ShapeDtypeStruct((depth, out_width), BF16),
         ],
-        in_specs=[spec(pltpu.HBM)] * 12,
-        out_specs=[spec(VMEM)] * 7,
+        in_specs=[spec(pltpu.HBM)] * 11,
+        out_specs=[spec(VMEM)] * 6,
         scratch_shapes=[
             SMEM(span_order.shape, jnp.int32),
             SMEM(page_table.shape, jnp.int32),
@@ -477,7 +486,7 @@
             VMEM(w_value.shape, BF16),
             VMEM((1, head_dim), F32),
             VMEM((1, 128), F32),
-            pltpu.SemaphoreType.DMA((12,)),
+            pltpu.SemaphoreType.DMA((11,)),
         ],
         compiler_params=params(),
         cost_estimate=cost(2 * rows * width * 256, 3 << 20),
@@ -493,7 +502,6 @@
             jnp.asarray(freq),
             prior_keys,
             prior_values,
-            w_query,
             w_output,
         )
     )
@@ -506,32 +514,19 @@
     with jax.named_scope("weights_step"):
         w_near = lax.ppermute(w_send, "head", [(0, 1), (1, 0)])
         w_far = swap(w_near, n, 1)
-    q, own_bias, span_bias = pl.pallas_call(
+    q = pl.pallas_call(
         query_kernel,
-        out_shape=[
-            jax.ShapeDtypeStruct((2 * blocks * group * BLOCK, 256), BF16),
-            jax.ShapeDtypeStruct((rows, rows), F32),
-            jax.ShapeDtypeStruct((blocks, n * PAGE), F32),
-        ],
-        in_specs=[spec(VMEM)] * 4 + [spec(pltpu.HBM)] * 4,
-        out_specs=[spec(VMEM)] * 3,
+        out_shape=jax.ShapeDtypeStruct((2 * blocks * group * BLOCK, 256), BF16),
+        in_specs=[spec(VMEM)] * 3 + [spec(pltpu.HBM)] * 2,
+        out_specs=spec(VMEM),
         scratch_shapes=[
+            VMEM(w_query.shape, BF16),
             VMEM((1, head_dim), F32),
-            SMEM(span_order.shape, jnp.int32),
-            SMEM(key_live.shape, jnp.int32),
-            SMEM((masks.size,), jnp.int32),
-            pltpu.SemaphoreType.DMA((4,)),
+            pltpu.SemaphoreType.DMA((2,)),
         ],
         compiler_params=params(),
         cost_estimate=cost(2 * rows * width * 512, 4 << 20),
-    )(
-        normed,
-        w_query,
-        cosine,
-        sine,
-        *in_hbm(query_gain.reshape(1, -1), span_order, key_live, jnp.asarray(masks.reshape(-1))),
-    )
-
+    )(normed, cosine, sine, *in_hbm(w_query, query_gain.reshape(1, -1)))
     for i, step in enumerate(steps[1:-1], 1):
         with jax.named_scope(f"prior_step_{i}"):
             prior = grow(prior, n, step)
@@ -539,22 +534,48 @@
             span = grow(span, n, span_steps[i])
     prior, span, _ = lax.optimization_barrier((prior, span, q))
     with jax.named_scope("prior_last"):
-        prior_same = [prior, swap(prior, n, steps[-1])]
+        prior_far = swap(prior, n, steps[-1])
     with jax.named_scope("span_last"):
-        span_same = [span, swap(span, n, span_steps[-1])]
-    with jax.named_scope("prior_core"):
-        prior_other = [swap(c, n, 1) for c in prior_same]
-    with jax.named_scope("span_core"):
-        span_other = [swap(c, n, 1) for c in span_same]
-
-    common = dict(blocks=blocks, group=group)
-    edge = n // 2 * PAGE
-    state = attention(q, (kv, own_bias), prior_same + prior_other, None, None, False, **common)
-    state = attention(q, None, span_same, span_bias[:, :edge], state, False, **common)
-    heads = attention(q, None, span_other, span_bias[:, edge:], state, True, **common)
+        span_far = swap(span, n, span_steps[-1])
+    own_bias, span_bias = pl.pallas_call(
+        functools.partial(mask_kernel, blocks),
+        out_shape=[
+            jax.ShapeDtypeStruct((rows, rows), F32),
+            jax.ShapeDtypeStruct((blocks, n * PAGE), F32),
+        ],
+        in_specs=[spec(pltpu.HBM)] * 3 + [spec(pl.ANY)],
+        out_specs=[spec(VMEM)] * 2,
+        scratch_shapes=[
+            SMEM(span_order.shape, jnp.int32),
+            SMEM(key_live.shape, jnp.int32),
+            SMEM((masks.size,), jnp.int32),
+            pltpu.SemaphoreType.DMA((3,)),
+        ],
+        compiler_params=params(),
+        cost_estimate=cost(1 << 28, 1 << 20),
+    )(*in_hbm(span_order, key_live, jnp.asarray(masks)), q)
+    prior, span = after(prior, own_bias), after(span, own_bias)
+    with jax.named_scope("prior_core_near"):
+        prior_core = swap(prior, n, 1)
+    with jax.named_scope("span_core_near"):
+        span_core = swap(span, n, 1)
+
+    common = dict(bias=span_bias, blocks=blocks, group=group)
+    part = n // 4 * PAGE
+    chunks = [(prior, None), (prior_core, None), (span, 0), (span_core, 2 * part)]
+    state = attention(q, (kv, own_bias), chunks, state=None, last=False, **common)
+    prior_far, span_far, *state = lax.optimization_barrier((prior_far, span_far, *state))
+    with jax.named_scope("prior_core_far"):
+        prior_core_far = swap(prior_far, n, 1)
+    with jax.named_scope("span_core_far"):
+        span_core_far = swap(span_far, n, 1)
+    chunks = [(prior_far, None), (span_far, part)]
+    state = attention(q, None, chunks, state=state, last=False, **common)
+    chunks = [(prior_core_far, None), (span_core_far, 3 * part)]
+    heads = attention(q, None, chunks, state=state, last=True, **common)
     peer = lax.ppermute(heads, "head", [(0, 1), (1, 0)])
 
-    all_span = span_same + span_other
+    all_span = [span, span_far, span_core, span_core_far]
     new_keys, new_values, partial = pl.pallas_call(
         functools.partial(pages_kernel, len(all_span)),
         out_shape=[jax.ShapeDtypeStruct((1, PAGE, 128), BF16)] * 2

time: 41.8 us -> 38.7 us (0.926)
  waiting for transfers between devices: 12.3 us -> 6.24 us
  starting transfers between devices: 13.3 us -> 15.3 us
  Pallas kernels: 15.2 us -> 16 us
    ppermute x11, waiting for transfers between devices: 10.8 us -> 3.39 us  [swap(): return lax.ppermute(x, 'seq', [(i, i ^ step) for i in range(n)])]
    ppermute x11, starting transfers between devices: 10.2 us -> 12.3 us  [swap(): return lax.ppermute(x, 'seq', [(i, i ^ step) for i in range(n)])]
    ppermute x1, waiting for transfers between devices: 0.01 us -> 1.34 us  [body(): w_near = lax.ppermute(w_send, 'head', [(0, 1), (1, 0)])]
    pallas_call x4 -> x5, Pallas kernels: 9.3 us -> 10.5 us  [the longest x3 6.95 us: attention(): pl.pallas_call(functools.partial(attention_kernel, offsets, own is not No...]
  transfers between devices with their start and end apart: 13 -> 13, of which waited for: 5 -> 6; matrix products, arithmetic and copies ran while one was open for 0% -> 0% of each run, Pallas kernels for 28% -> 34%
where the time goes in v3:
time: 38.7 us; the launch traced here: 38.4 us
  Pallas kernels  16 us (41%)
  starting transfers between devices  15.3 us (40%)
  waiting for transfers between devices  6.24 us (16%)
  between operations  0.78 us (2%)
    ppermute x11, starting transfers between devices, swap(): return lax.ppermute(x, 'seq', [(i, i ^ step) for i in range(n)])  12.3 us
    pallas_call x3, Pallas kernels, attention(): pl.pallas_call(functools.partial(attention_kernel, offsets, own is not No...  6.95 us
    ppermute x11, waiting for transfers between devices, swap(): return lax.ppermute(x, 'seq', [(i, i ^ step) for i in range(n)])  3.39 us
    pallas_call x1, Pallas kernels, body(): pl.pallas_call(query_kernel, out_shape=jax.ShapeDtypeStruct((2 * blocks *...  2.46 us
    pallas_call x1, Pallas kernels, body(): pl.pallas_call(functools.partial(pages_kernel, len(all_span)), out_shape=...  2.44 us
    pallas_call x1, Pallas kernels, body(): pl.pallas_call(functools.partial(kv_kernel, prior_len), out_shape=[jax.Sh...  1.99 us
    ppermute x1, waiting for transfers between devices, body(): peer = lax.ppermute(heads, 'head', [(0, 1), (1, 0)])  1.51 us
    ppermute x1, starting transfers between devices, body(): peer = lax.ppermute(heads, 'head', [(0, 1), (1, 0)])  1.5 us
  transfers between devices with their start and end apart: 13, of which 6 were waited for; matrix products, arithmetic and copies ran while one was open for 0% of the time, Pallas kernels for 34%

profile of v3, /device:TPU:0, one launch (start us, length us, event | category | flops | bytes accessed | tf_op | source)
XLA Modules:
  0.0 38.4 jit_solution(9539431688416686104)
XLA Ops:
  0.6 2.0 %shard_map.184 = (bf16[128,256]{1,0:T(8,128)(2,1)S(1)}, bf16[128,256]{1,0:T(8,128)(2,1)S(1)}, bf16[128,2048]{1,0:T(8,128)(2,1)S(1)}, f32[128,128]{1,0:T(8,128)S(...) custom-call(s32[32]{0:T(128)} %order.5, s32[16]{0:T(128)} %table.1, bf16[128,2048]{1,0:T(8,128)(2,1)} %hidden.1, ...), custom_call_target="tpu_custom_call" | custom-call | flops 134217728 | bytes 3145728 | tf_op jit(solution)/shard_map/pallas_call | solution.py:468
  2.6 3.0 %collective-permute-start.1 = (bf16[128,256]{1,0:T(8,128)(2,1)S(1)}, bf16[128,256]{1,0:T(8,128)(2,1)S(1)}, u32[]{:S(2)}, u32[]{:S(2)}) collective-permute-start(bf16[128,256]{1,0:T(8,128)(2,1)S(1)} %get-tuple-element.29.refs_1_), channel_id=1, source_target_pairs={{0,4},{2,6},{4,0},{6,2},{8,12},{10,14},{12,8},{14,10},{16,20},{18,... | collective-permute-start | bytes 196616 | tf_op jit(solution)/shard_map/span_step_0/ppermute | solution.py:426
  5.7 2.6 %collective-permute-start = (bf16[128,256]{1,0:T(8,128)(2,1)S(1)}, bf16[128,256]{1,0:T(8,128)(2,1)S(1)}, u32[]{:S(2)}, u32[]{:S(2)}) collective-permute-start(bf16[128,256]{1,0:T(8,128)(2,1)S(1)} %get-tuple-element.28), channel_id=1, source_target_pairs={{0,16},{2,18},{4,20},{6,22},{8,24},{10,26},{12,28},{14,30},{16,0},... | collective-permute-start | bytes 196616 | tf_op jit(solution)/shard_map/prior_step_0/ppermute | solution.py:426
  8.3 1.5 %collective-permute-start.11 = (bf16[256,1024]{1,0:T(8,128)(2,1)S(1)}, bf16[256,1024]{1,0:T(8,128)(2,1)S(1)}, u32[]{:S(2)}, u32[]{:S(2)}) collective-permute-start(bf16[256,1024]{1,0:T(8,128)(2,1)S(1)} %get-tuple-element.48), channel_id=1, source_target_pairs={{0,1},{1,0},{2,3},{3,2},{4,5},{5,4},{6,7},{7,6},{8,9},{9,8},{10,11... | collective-permute-start | bytes 1572872 | tf_op jit(solution)/shard_map/weights_step/ppermute | solution.py:515
  9.8 0.0 collective-permute-done.1
  9.8 1.2 %collective-permute-start.3 = (bf16[256,256]{1,0:T(8,128)(2,1)S(1)}, bf16[256,256]{1,0:T(8,128)(2,1)S(1)}, u32[]{:S(2)}, u32[]{:S(2)}) collective-permute-start(bf16[256,256]{1,0:T(8,128)(2,1)S(1)} %constant_dynamic-update-slice_fusion.2), channel_id=1, source_target_pairs={{0,16},{2,18},{4,20},{6,22},{8,24},{10,26},{12,28},{14,30},{16,0},... | collective-permute-start | bytes 393224 | tf_op jit(solution)/shard_map/span_step_1/ppermute | solution.py:426
  11.0 0.1 collective-permute-done
  11.1 3.3 %collective-permute-start.2 = (bf16[256,256]{1,0:T(8,128)(2,1)S(1)}, bf16[256,256]{1,0:T(8,128)(2,1)S(1)}, u32[]{:S(2)}, u32[]{:S(2)}) collective-permute-start(bf16[256,256]{1,0:T(8,128)(2,1)S(1)} %constant_dynamic-update-slice_fusion), channel_id=1, source_target_pairs={{0,8},{2,10},{4,12},{6,14},{8,0},{10,2},{12,4},{14,6},{16,24},{18,... | collective-permute-start | bytes 393224 | tf_op jit(solution)/shard_map/prior_step_1/ppermute | solution.py:426
  14.4 2.5 %shard_map.185.turn.refs_0_ = bf16[1024,256]{1,0:T(8,128)(2,1)S(1)} custom-call(bf16[128,2048]{1,0:T(8,128)(2,1)S(1)} %get-tuple-element.30.normed, f32[128,128]{1,0:T(8,128)S(1)} %get-tuple-element.31.cosine, f32[128,128]{1,0:T(8,128)S(1)} %get-tuple-element.32.sine, bf16[2048,512]{1,0:T(8,128)(2,1)} %w_query.1, f32[1,64]{1,0:T(1,128)} %bitcast.5), custom_call_target="tpu_custom_call" | custom-call | flops 268435456 | bytes 4194304 | tf_op jit(solution)/shard_map/pallas_call | solution.py:517
  16.9 1.1 %shard_map.186 = (f32[128,128]{1,0:T(8,128)S(1)}, f32[2,2048]{1,0:T(2,128)S(1)}) custom-call(s32[32]{0:T(128)} %order.5, s32[32]{0:T(128)} %live.1, s32[16]{0:T(128)} %constant.7.clone.masks, bf16[1024,256]{1,0:T(8,128)(2,1)S(1)} %shard_map.185.turn.refs_0_), custom_call_target="tpu_custom_call" | custom-call | flops 268435456 | bytes 1048576 | tf_op jit(solution)/shard_map/pallas_call | solution.py:540
  18.0 0.1 collective-permute-done.3
  18.1 0.2 collective-permute-done.2
  18.3 0.1 collective-permute-start.7
  18.4 0.5 %collective-permute-start.6 = (bf16[512,256]{1,0:T(8,128)(2,1)S(1)}, bf16[512,256]{1,0:T(8,128)(2,1)S(1)}, u32[]{:S(2)}, u32[]{:S(2)}) collective-permute-start(bf16[512,256]{1,0:T(8,128)(2,1)S(1)} %pad_maximum_fusion.refs_3_), channel_id=1, source_target_pairs={{0,2},{2,0},{4,6},{6,4},{8,10},{10,8},{12,14},{14,12},{16,18},{18,... | collective-permute-start | bytes 786440 | tf_op jit(solution)/shard_map/prior_core_near/ppermute | solution.py:426
  18.9 0.3 collective-permute-start.4
  19.2 0.8 %collective-permute-start.5 = (bf16[512,256]{1,0:T(8,128)(2,1)S(1)}, bf16[512,256]{1,0:T(8,128)(2,1)S(1)}, u32[]{:S(2)}, u32[]{:S(2)}) collective-permute-start(bf16[512,256]{1,0:T(8,128)(2,1)S(1)} %pad_maximum_fusion.1.refs_5_.refs_0_), channel_id=1, source_target_pairs={{0,8},{2,10},{4,12},{6,14},{8,0},{10,2},{12,4},{14,6},{16,24},{18,... | collective-permute-start | bytes 786440 | tf_op jit(solution)/shard_map/span_last/ppermute | solution.py:426
  20.0 1.3 %collective-permute-done.11.w_near = bf16[256,1024]{1,0:T(8,128)(2,1)S(1)} collective-permute-done((bf16[256,1024]{1,0:T(8,128)(2,1)S(1)}, bf16[256,1024]{1,0:T(8,128)(2,1)S(1)}, u32[]{:S(2)}, u32[]{:S(2)}) %collective-permute-start.11) | collective-permute-done | bytes 524320 | tf_op jit(solution)/shard_map/weights_step/ppermute | solution.py:515
  21.4 0.0 collective-permute-start.12
  21.4 0.0 collective-permute-done.7.refs_6_.refs_2_
  21.4 2.9 %shard_map.187 = (f32[1024,128]{1,0:T(8,128)S(1)}, f32[1024,128]{1,0:T(8,128)S(1)}) custom-call(bf16[1024,256]{1,0:T(8,128)(2,1)S(1)} %shard_map.185.turn.refs_0_, bf16[128,256]{1,0:T(8,128)(2,1)S(1)} %get-tuple-element.29.refs_1_, f32[128,128]{1,0:T(8,128)S(1)} %get-tuple-element.35.refs_2_, bf16[512,256]{1,0:T(8,128)(2,1)S(1)} %pad_maximum_fusion.refs_3_, ...), custom_call_target="tpu_custom_call" | custom-call | flops 2147483648 | bytes 3145728 | tf_op jit(solution)/shard_map/pallas_call | solution.py:350
  24.3 2.9 %collective-permute-done.4.refs_1_ = bf16[512,256]{1,0:T(8,128)(2,1)S(1)} collective-permute-done((bf16[512,256]{1,0:T(8,128)(2,1)S(1)}, bf16[512,256]{1,0:T(8,128)(2,1)S(1)}, u32[]{:S(2)}, u32[]{:S(2)}) %collective-permute-start.4) | collective-permute-done | bytes 262176 | tf_op jit(solution)/shard_map/prior_last/ppermute | solution.py:426
  27.2 0.0 collective-permute-done.5.refs_2_.refs_1_
  27.2 0.5 %collective-permute-start.9 = (bf16[512,256]{1,0:T(8,128)(2,1)S(1)}, bf16[512,256]{1,0:T(8,128)(2,1)S(1)}, u32[]{:S(2)}, u32[]{:S(2)}) collective-permute-start(bf16[512,256]{1,0:T(8,128)(2,1)S(1)} %collective-permute-done.5.refs_2_.refs_1_), channel_id=1, source_target_pairs={{0,2},{2,0},{4,6},{6,4},{8,10},{10,8},{12,14},{14,12},{16,18},{18,... | collective-permute-start | bytes 786440 | tf_op jit(solution)/shard_map/span_core_far/ppermute | solution.py:426
  27.7 1.7 %shard_map.188 = (f32[1024,128]{1,0:T(8,128)S(1)}, f32[1024,128]{1,0:T(8,128)S(1)}) custom-call(bf16[1024,256]{1,0:T(8,128)(2,1)S(1)} %shard_map.185.turn.refs_0_, bf16[512,256]{1,0:T(8,128)(2,1)S(1)} %collective-permute-done.4.refs_1_, bf16[512,256]{1,0:T(8,128)(2,1)S(1)} %collective-permute-done.5.refs_2_.refs_1_, ...), custom_call_target="tpu_custom_call" | custom-call | flops 1073741824 | bytes 2621440 | tf_op jit(solution)/shard_map/pallas_call | solution.py:350
  29.4 0.0 copy-start
  29.4 0.0 copy-start.1
  29.4 0.0 copy-start.2
  29.5 2.4 %shard_map.189.mine = bf16[128,512]{1,0:T(8,128)(2,1)S(1)} custom-call(bf16[1024,256]{1,0:T(8,128)(2,1)S(1)} %shard_map.185.turn.refs_0_, bf16[512,256]{1,0:T(8,128)(2,1)S(1)} %collective-permute-done.8.refs_1_, bf16[512,256]{1,0:T(8,128)(2,1)S(1)} %collective-permute-done.9.refs_2_.refs_3_, f32[2,2048]{1,0:T(2,128)S(1)} %get-tuple-element.38.refs_7_.refs_3_, ...), custom_call_target="tpu_custom_call" | custom-call | flops 1073741824 | bytes 2621440 | tf_op jit(solution)/shard_map/pallas_call | solution.py:350
  31.9 1.5 %collective-permute-start.10 = (bf16[128,512]{1,0:T(8,128)(2,1)S(1)}, bf16[128,512]{1,0:T(8,128)(2,1)S(1)}, u32[]{:S(2)}, u32[]{:S(2)}) collective-permute-start(bf16[128,512]{1,0:T(8,128)(2,1)S(1)} %shard_map.189.mine), channel_id=1, source_target_pairs={{0,1},{1,0},{2,3},{3,2},{4,5},{5,4},{6,7},{7,6},{8,9},{9,8},{10,11... | collective-permute-start | bytes 393224 | tf_op jit(solution)/shard_map/ppermute | solution.py:576
  33.4 2.4 %shard_map.190 = (bf16[1,128,128]{2,1,0:T(8,128)(2,1)}, bf16[1,128,128]{2,1,0:T(8,128)(2,1)}, f32[128,1024]{1,0:T(8,128)S(1)}) custom-call(s32[16]{0:T(128)S(1)} %copy-done.1, s32[32]{0:T(128)S(1)} %copy-done, s32[16]{0:T(128)S(1)} %copy-done.2, bf16[128,512]{1,0:T(8,128)(2,1)S(1)} %shard_map.189.mine, bf16[512,2048]{1,0:T(8,128)(2,1)} %w_output.3, ...), custom_call_target="tpu_custom_call" | custom-call | flops 134217728 | bytes 2097152 | tf_op jit(solution)/shard_map/pallas_call | solution.py:579
  35.8 1.5 %collective-permute-done.10.peer = bf16[128,512]{1,0:T(8,128)(2,1)S(1)} collective-permute-done((bf16[128,512]{1,0:T(8,128)(2,1)S(1)}, bf16[128,512]{1,0:T(8,128)(2,1)S(1)}, u32[]{:S(2)}, u32[]{:S(2)}) %collective-permute-start.10) | collective-permute-done | bytes 131104 | tf_op jit(solution)/shard_map/ppermute | solution.py:576
  37.3 1.1 %shard_map.191 = f32[128,1024]{1,0:T(8,128)} custom-call(f32[128,1024]{1,0:T(8,128)S(1)} %get-tuple-element.47.partial, bf16[128,512]{1,0:T(8,128)(2,1)S(1)} %collective-permute-done.10.peer, bf16[256,1024]{1,0:T(8,128)(2,1)S(1)} %collective-permute-done.11.w_near, bf16[256,1024]{1,0:T(8,128)(2,1)S(1)} %collective-permute-done.12.w_far), custom_call_target="tpu_custom_call" | custom-call | flops 134217728 | bytes 2097152 | tf_op jit(solution)/shard_map/pallas_call | solution.py:593
  (14 shorter events, 0.1 us)
Async XLA Ops:
  2.6 7.1 %collective-permute-start.1 = (bf16[128,256]{1,0:T(8,128)(2,1)S(1)}, bf16[128,256]{1,0:T(8,128)(2,1)S(1)}, u32[]{:S(2)}, u32[]{:S(2)}) collective-permute-start(bf16[128,256]{1,0:T(8,128)(2,1)S(1)} %get-tuple-element.29.refs_1_), channel_id=1, source_target_pairs={{0,4},{2,6},{4,0},{6,2},{8,12},{10,14},{12,8},{14,10},{16,20},{18,... | collective-permute-start | bytes 196616 | tf_op jit(solution)/shard_map/span_step_0/ppermute | solution.py:426
  5.7 5.5 %collective-permute-start = (bf16[128,256]{1,0:T(8,128)(2,1)S(1)}, bf16[128,256]{1,0:T(8,128)(2,1)S(1)}, u32[]{:S(2)}, u32[]{:S(2)}) collective-permute-start(bf16[128,256]{1,0:T(8,128)(2,1)S(1)} %get-tuple-element.28), channel_id=1, source_target_pairs={{0,16},{2,18},{4,20},{6,22},{8,24},{10,26},{12,28},{14,30},{16,0},... | collective-permute-start | bytes 196616 | tf_op jit(solution)/shard_map/prior_step_0/ppermute | solution.py:426
  8.3 13.1 %collective-permute-start.11 = (bf16[256,1024]{1,0:T(8,128)(2,1)S(1)}, bf16[256,1024]{1,0:T(8,128)(2,1)S(1)}, u32[]{:S(2)}, u32[]{:S(2)}) collective-permute-start(bf16[256,1024]{1,0:T(8,128)(2,1)S(1)} %get-tuple-element.48), channel_id=1, source_target_pairs={{0,1},{1,0},{2,3},{3,2},{4,5},{5,4},{6,7},{7,6},{8,9},{9,8},{10,11... | collective-permute-start | bytes 1572872 | tf_op jit(solution)/shard_map/weights_step/ppermute | solution.py:515
  9.8 8.3 %collective-permute-start.3 = (bf16[256,256]{1,0:T(8,128)(2,1)S(1)}, bf16[256,256]{1,0:T(8,128)(2,1)S(1)}, u32[]{:S(2)}, u32[]{:S(2)}) collective-permute-start(bf16[256,256]{1,0:T(8,128)(2,1)S(1)} %constant_dynamic-update-slice_fusion.2), channel_id=1, source_target_pairs={{0,16},{2,18},{4,20},{6,22},{8,24},{10,26},{12,28},{14,30},{16,0},... | collective-permute-start | bytes 393224 | tf_op jit(solution)/shard_map/span_step_1/ppermute | solution.py:426
  11.1 7.2 %collective-permute-start.2 = (bf16[256,256]{1,0:T(8,128)(2,1)S(1)}, bf16[256,256]{1,0:T(8,128)(2,1)S(1)}, u32[]{:S(2)}, u32[]{:S(2)}) collective-permute-start(bf16[256,256]{1,0:T(8,128)(2,1)S(1)} %constant_dynamic-update-slice_fusion), channel_id=1, source_target_pairs={{0,8},{2,10},{4,12},{6,14},{8,0},{10,2},{12,4},{14,6},{16,24},{18,... | collective-permute-start | bytes 393224 | tf_op jit(solution)/shard_map/prior_step_1/ppermute | solution.py:426
  18.3 3.1 %collective-permute-start.7 = (bf16[512,256]{1,0:T(8,128)(2,1)S(1)}, bf16[512,256]{1,0:T(8,128)(2,1)S(1)}, u32[]{:S(2)}, u32[]{:S(2)}) collective-permute-start(bf16[512,256]{1,0:T(8,128)(2,1)S(1)} %pad_maximum_fusion.1.refs_5_.refs_0_), channel_id=1, source_target_pairs={{0,2},{2,0},{4,6},{6,4},{8,10},{10,8},{12,14},{14,12},{16,18},{18,... | collective-permute-start | bytes 786440 | tf_op jit(solution)/shard_map/span_core_near/ppermute | solution.py:426
  18.4 3.0 %collective-permute-start.6 = (bf16[512,256]{1,0:T(8,128)(2,1)S(1)}, bf16[512,256]{1,0:T(8,128)(2,1)S(1)}, u32[]{:S(2)}, u32[]{:S(2)}) collective-permute-start(bf16[512,256]{1,0:T(8,128)(2,1)S(1)} %pad_maximum_fusion.refs_3_), channel_id=1, source_target_pairs={{0,2},{2,0},{4,6},{6,4},{8,10},{10,8},{12,14},{14,12},{16,18},{18,... | collective-permute-start | bytes 786440 | tf_op jit(solution)/shard_map/prior_core_near/ppermute | solution.py:426
  18.9 8.3 %collective-permute-start.4 = (bf16[512,256]{1,0:T(8,128)(2,1)S(1)}, bf16[512,256]{1,0:T(8,128)(2,1)S(1)}, u32[]{:S(2)}, u32[]{:S(2)}) collective-permute-start(bf16[512,256]{1,0:T(8,128)(2,1)S(1)} %pad_maximum_fusion.refs_3_), channel_id=1, source_target_pairs={{0,4},{2,6},{4,0},{6,2},{8,12},{10,14},{12,8},{14,10},{16,20},{18,... | collective-permute-start | bytes 786440 | tf_op jit(solution)/shard_map/prior_last/ppermute | solution.py:426
  19.2 8.0 %collective-permute-start.5 = (bf16[512,256]{1,0:T(8,128)(2,1)S(1)}, bf16[512,256]{1,0:T(8,128)(2,1)S(1)}, u32[]{:S(2)}, u32[]{:S(2)}) collective-permute-start(bf16[512,256]{1,0:T(8,128)(2,1)S(1)} %pad_maximum_fusion.1.refs_5_.refs_0_), channel_id=1, source_target_pairs={{0,8},{2,10},{4,12},{6,14},{8,0},{10,2},{12,4},{14,6},{16,24},{18,... | collective-permute-start | bytes 786440 | tf_op jit(solution)/shard_map/span_last/ppermute | solution.py:426
  21.4 16.0 %collective-permute-start.12 = (bf16[256,1024]{1,0:T(8,128)(2,1)S(1)}, bf16[256,1024]{1,0:T(8,128)(2,1)S(1)}, u32[]{:S(2)}, u32[]{:S(2)}) collective-permute-start(bf16[256,1024]{1,0:T(8,128)(2,1)S(1)} %collective-permute-done.11.w_near), channel_id=1, source_target_pairs={{0,2},{2,0},{4,6},{6,4},{8,10},{10,8},{12,14},{14,12},{16,18},{18,... | collective-permute-start | bytes 1572872 | tf_op jit(solution)/shard_map/weights_step/ppermute | solution.py:426
  27.2 2.2 %collective-permute-start.8 = (bf16[512,256]{1,0:T(8,128)(2,1)S(1)}, bf16[512,256]{1,0:T(8,128)(2,1)S(1)}, u32[]{:S(2)}, u32[]{:S(2)}) collective-permute-start(bf16[512,256]{1,0:T(8,128)(2,1)S(1)} %collective-permute-done.4.refs_1_), channel_id=1, source_target_pairs={{0,2},{2,0},{4,6},{6,4},{8,10},{10,8},{12,14},{14,12},{16,18},{18,... | collective-permute-start | bytes 786440 | tf_op jit(solution)/shard_map/prior_core_far/ppermute | solution.py:426
  27.2 2.2 %collective-permute-start.9 = (bf16[512,256]{1,0:T(8,128)(2,1)S(1)}, bf16[512,256]{1,0:T(8,128)(2,1)S(1)}, u32[]{:S(2)}, u32[]{:S(2)}) collective-permute-start(bf16[512,256]{1,0:T(8,128)(2,1)S(1)} %collective-permute-done.5.refs_2_.refs_1_), channel_id=1, source_target_pairs={{0,2},{2,0},{4,6},{6,4},{8,10},{10,8},{12,14},{14,12},{16,18},{18,... | collective-permute-start | bytes 786440 | tf_op jit(solution)/shard_map/span_core_far/ppermute | solution.py:426
  29.4 4.0 %copy-start = (s32[32]{0:T(128)S(1)}, s32[32]{0:T(128)}, u32[]{:S(2)}) copy-start(s32[32]{0:T(128)} %order.5) | copy-start | bytes 388
  29.4 3.9 %copy-start.1 = (s32[16]{0:T(128)S(1)}, s32[16]{0:T(128)}, u32[]{:S(2)}) copy-start(s32[16]{0:T(128)} %dest.1) | copy-start | bytes 196
  29.4 3.9 %copy-start.2 = (s32[16]{0:T(128)S(1)}, s32[16]{0:T(128)}, u32[]{:S(2)}) copy-start(s32[16]{0:T(128)} %constant.8.clone.where) | copy-start | bytes 196
  31.9 5.5 %collective-permute-start.10 = (bf16[128,512]{1,0:T(8,128)(2,1)S(1)}, bf16[128,512]{1,0:T(8,128)(2,1)S(1)}, u32[]{:S(2)}, u32[]{:S(2)}) collective-permute-start(bf16[128,512]{1,0:T(8,128)(2,1)S(1)} %shard_map.189.mine), channel_id=1, source_target_pairs={{0,1},{1,0},{2,3},{3,2},{4,5},{5,4},{6,7},{7,6},{8,9},{9,8},{10,11... | collective-permute-start | bytes 393224 | tf_op jit(solution)/shard_map/ppermute | solution.py:576

commit v4 on v3

--- a/solution.py
+++ b/solution.py
@@ -60,7 +60,7 @@
     prior_len, order, table, hidden, gain, w_key, w_value, key_gain, freq, prior_keys, prior_values,
     w_output,
     kv, prior, normed_out, cos_out, sin_out, w_send,
-    order_s, table_s, hidden_v, gain_v, w_key_v, w_value_v, key_gain_v, freq_v, sems,
+    order_s, table_s, hidden_v, gain_v, w_key_v, w_value_v, key_gain_v, freq_v, sems, late_sems,
 ):
     rows = hidden.shape[0]
     blocks = rows // BLOCK
@@ -70,11 +70,7 @@
         (gain, gain_v), (hidden, hidden_v), (w_key, w_key_v), (w_value, w_value_v),
     ]
     copies = [pltpu.make_async_copy(a, b, sems.at[i]) for i, (a, b) in enumerate(pairs)]
-    later = [
-        pltpu.make_async_copy(
-            w_output.at[half_rows(w_send, me % 2), columns(w_send, 1)], w_send, sems.at[10]
-        ),
-    ]
+    later = head_copies(w_output, w_send, me % 2 * (w_send.shape[0] // 128), 1, late_sems)
     for copy in copies + later:
         copy.start()
     copies[0].wait()
@@ -119,8 +115,17 @@
         copy.wait()
 
 
-def half_rows(ref, core):
-    return pl.ds(pl.multiple_of(core * ref.shape[0], ref.shape[0]), ref.shape[0])
+def head_copies(w_output, target, first, other, sems):
+    group = w_output.shape[0] // 128
+    copies = []
+    for i in range(target.shape[0] // 64):
+        head = (i % 2) * group + first + i // 2
+        rows = pl.ds(pl.multiple_of(head * 64, 64), 64)
+        source = w_output.at[rows, columns(target, other)]
+        copies.append(
+            pltpu.make_async_copy(source, target.at[i * 64 : (i + 1) * 64, :], sems.at[i])
+        )
+    return copies
 
 
 def columns(ref, other):
@@ -129,22 +134,14 @@
     return pl.ds(pl.multiple_of(x * ref.shape[1], ref.shape[1]), ref.shape[1])
 
 
-def query_kernel(
-    normed, cosine, sine, w_query, query_gain, q_out, w_query_v, query_gain_v, sems
-):
-    pairs = [(w_query, w_query_v), (query_gain, query_gain_v)]
-    copies = [pltpu.make_async_copy(a, b, sems.at[i]) for i, (a, b) in enumerate(pairs)]
-    for copy in copies:
-        copy.start()
+def query_kernel(normed, cosine, sine, w_query, query_gain, q_out):
     rows = normed.shape[0]
     blocks = rows // BLOCK
     tiles = w_query.shape[1] // 128
     per_kv = tiles // 2
     group = 2 * per_kv
-    for copy in copies:
-        copy.wait()
-    queries = jnp.dot(normed[...], w_query_v[...], preferred_element_type=F32)
-    gain = twice(query_gain_v)
+    queries = jnp.dot(normed[...], w_query[...], preferred_element_type=F32)
+    gain = twice(query_gain)
     left = lanes_of((rows, 128)) < 64
     for t in range(tiles):
         kv_head, u = divmod(t, per_kv)
@@ -162,8 +159,13 @@
                 q_out[at : at + BLOCK, :] = both[b * BLOCK : (b + 1) * BLOCK, :]
 
 
-def mask_kernel(blocks, order, live, masks, turn, own_bias, span_bias, order_s, live_s, masks_s, sems):
+def mask_kernel(
+    blocks, order, live, masks, w_query, turn,
+    own_bias, span_bias, w_query_out, order_s, live_s, masks_s, sems,
+):
     pairs = [(order, order_s), (live, live_s), (masks, masks_s)]
+    bring = pltpu.make_async_copy(w_query, w_query_out, sems.at[3])
+    bring.start()
     copies = [pltpu.make_async_copy(a, b, sems.at[i]) for i, (a, b) in enumerate(pairs)]
     for copy in copies:
         copy.start()
@@ -200,7 +202,8 @@
             span_bias[b : b + 1, at] = jnp.where(lane < BLOCK, value[0], value[1])
         return carry
 
-    lax.fori_loop(0, count, visit, 0)
+    lax.fori_loop(0, count, visit, 0, unroll=count <= 16)
+    bring.wait()
 
 
 class Piece:
@@ -215,7 +218,7 @@
 
 def fold(q, m_in, acc_in, m_out, acc_out, pieces, blocks, part, finish=None):
     tiles = 2 * blocks
-    scores, weights = {}, {}
+    scores, weights, totals = {}, {}, {}
 
     def score(t):
         rows = pl.ds(t * part, part)
@@ -247,8 +250,10 @@
             total = total + jnp.dot(p, piece.values[t // blocks], preferred_element_type=F32)
         if finish is None:
             acc_out[rows, :] = total
-        else:
-            finish(t, total)
+            return
+        totals[t] = total
+        if t >= blocks:
+            finish(t - blocks, totals.pop(t - blocks), totals.pop(t))
 
     score(0)
     for t in range(tiles + 1):
@@ -282,20 +287,23 @@
         mine = [own_bias[b * BLOCK : (b + 1) * BLOCK, :] for b in range(blocks)]
         extra = [Piece(own_kv[...], [jnp.concatenate([m] * group, axis=0) for m in mine])]
 
-    def finish(t, acc):
-        kv_head, b = divmod(t, blocks)
-        left = lanes_of((BLOCK, 128)) < 64
-        for u in range(group // 2):
-            even = acc[2 * u * BLOCK : (2 * u + 1) * BLOCK, :]
-            odd = acc[(2 * u + 1) * BLOCK : (2 * u + 2) * BLOCK, :]
-            even_t, odd_t = pltpu.roll(even, 64, 1), pltpu.roll(odd, 64, 1)
-            if kv_head == 0:
-                top, low = jnp.where(left, even, odd_t), jnp.where(left, even_t, odd)
-            else:
-                top, low = jnp.where(left, even_t, odd), jnp.where(left, even, odd_t)
-            tile = kv_head * (group // 2) + u
-            rows = slice(b * BLOCK, (b + 1) * BLOCK)
-            out[rows, tile * 128 : (tile + 1) * 128] = (top / low).astype(BF16)
+    def finish(b, first_acc, second_acc):
+        left = lanes_of(first_acc.shape) < 64
+        top = jnp.where(left, first_acc, second_acc)
+        sums = jnp.where(left, second_acc, first_acc)
+        high = sums.astype(BF16)
+        low = (sums - high.astype(F32)).astype(BF16)
+        to = lax.broadcasted_iota(jnp.int32, (256, 128), 1)
+        of = lax.broadcasted_iota(jnp.int32, (256, 128), 0)
+        swapped = jnp.where(of % 128 == (to + 64) % 128, 1.0, 0.0).astype(BF16)
+        sums = jnp.dot(
+            jnp.concatenate([high, low], axis=-1), swapped, preferred_element_type=F32
+        )
+        ratio = (top / sums).astype(BF16)
+        for u in range(group):
+            out[b * BLOCK : (b + 1) * BLOCK, u * 128 : (u + 1) * 128] = ratio[
+                u * BLOCK : (u + 1) * BLOCK, :
+            ]
 
     if not refs:
         pieces = [piece(chunk[...], at) for chunk, at in zip(chunks, offsets)]
@@ -321,8 +329,9 @@
 
         pl.loop(0, chunk.shape[0] // step)(visit)
     if last:
-        for t in range(2 * blocks):
-            finish(t, acc_ref[t * part : (t + 1) * part, :])
+        tiles = [acc_ref[t * part : (t + 1) * part, :] for t in range(2 * blocks)]
+        for b in range(blocks):
+            finish(b, tiles[b], tiles[blocks + b])
 
 
 def attention(q, own, chunks, bias, state, last, blocks, group):
@@ -361,10 +370,11 @@
 
 
 def pages_kernel(n_chunks, dest, order, where, mine, w_output, *refs):
-    chunks, (keys, values, partial, w_mine, sems) = refs[:n_chunks], refs[n_chunks:]
+    chunks, (keys, values, partial, w_mine, sems, head_sems) = refs[:n_chunks], refs[n_chunks:]
     me = lax.axis_index("seq")
-    copy = pltpu.make_async_copy(w_output.at[:, columns(w_mine, 0)], w_mine, sems.at[2])
-    copy.start()
+    copies = head_copies(w_output, w_mine, 0, 0, head_sems)
+    for copy in copies:
+        copy.start()
 
     def find(table):
         def body(wanted):
@@ -396,7 +406,8 @@
                 b.wait()
 
             at += size
-    copy.wait()
+    for copy in copies:
+        copy.wait()
     partial[...] = jnp.dot(mine[...], w_mine[...], preferred_element_type=F32)
 
 
@@ -486,7 +497,8 @@
             VMEM(w_value.shape, BF16),
             VMEM((1, head_dim), F32),
             VMEM((1, 128), F32),
-            pltpu.SemaphoreType.DMA((11,)),
+            pltpu.SemaphoreType.DMA((10,)),
+            pltpu.SemaphoreType.DMA((depth // 64,)),
         ],
         compiler_params=params(),
         cost_estimate=cost(2 * rows * width * 256, 3 << 20),
@@ -514,19 +526,32 @@
     with jax.named_scope("weights_step"):
         w_near = lax.ppermute(w_send, "head", [(0, 1), (1, 0)])
         w_far = swap(w_near, n, 1)
+    own_bias, span_bias, w_query = pl.pallas_call(
+        functools.partial(mask_kernel, blocks),
+        out_shape=[
+            jax.ShapeDtypeStruct((rows, rows), F32),
+            jax.ShapeDtypeStruct((blocks, n * PAGE), F32),
+            jax.ShapeDtypeStruct(w_query.shape, BF16),
+        ],
+        in_specs=[spec(pltpu.HBM)] * 4 + [spec(pl.ANY)],
+        out_specs=[spec(VMEM)] * 3,
+        scratch_shapes=[
+            SMEM(span_order.shape, jnp.int32),
+            SMEM(key_live.shape, jnp.int32),
+            SMEM((masks.size,), jnp.int32),
+            pltpu.SemaphoreType.DMA((4,)),
+        ],
+        compiler_params=params(),
+        cost_estimate=cost(1 << 28, 1 << 20),
+    )(*in_hbm(span_order, key_live, jnp.asarray(masks), w_query), normed)
     q = pl.pallas_call(
         query_kernel,
         out_shape=jax.ShapeDtypeStruct((2 * blocks * group * BLOCK, 256), BF16),
-        in_specs=[spec(VMEM)] * 3 + [spec(pltpu.HBM)] * 2,
+        in_specs=[spec(VMEM)] * 5,
         out_specs=spec(VMEM),
-        scratch_shapes=[
-            VMEM(w_query.shape, BF16),
-            VMEM((1, head_dim), F32),
-            pltpu.SemaphoreType.DMA((2,)),
-        ],
         compiler_params=params(),
         cost_estimate=cost(2 * rows * width * 512, 4 << 20),
-    )(normed, cosine, sine, *in_hbm(w_query, query_gain.reshape(1, -1)))
+    )(normed, cosine, sine, w_query, query_gain.reshape(1, -1))
     for i, step in enumerate(steps[1:-1], 1):
         with jax.named_scope(f"prior_step_{i}"):
             prior = grow(prior, n, step)
@@ -537,23 +562,6 @@
         prior_far = swap(prior, n, steps[-1])
     with jax.named_scope("span_last"):
         span_far = swap(span, n, span_steps[-1])
-    own_bias, span_bias = pl.pallas_call(
-        functools.partial(mask_kernel, blocks),
-        out_shape=[
-            jax.ShapeDtypeStruct((rows, rows), F32),
-            jax.ShapeDtypeStruct((blocks, n * PAGE), F32),
-        ],
-        in_specs=[spec(pltpu.HBM)] * 3 + [spec(pl.ANY)],
-        out_specs=[spec(VMEM)] * 2,
-        scratch_shapes=[
-            SMEM(span_order.shape, jnp.int32),
-            SMEM(key_live.shape, jnp.int32),
-            SMEM((masks.size,), jnp.int32),
-            pltpu.SemaphoreType.DMA((3,)),
-        ],
-        compiler_params=params(),
-        cost_estimate=cost(1 << 28, 1 << 20),
-    )(*in_hbm(span_order, key_live, jnp.asarray(masks)), q)
     prior, span = after(prior, own_bias), after(span, own_bias)
     with jax.named_scope("prior_core_near"):
         prior_core = swap(prior, n, 1)
@@ -562,14 +570,14 @@
 
     common = dict(bias=span_bias, blocks=blocks, group=group)
     part = n // 4 * PAGE
-    chunks = [(prior, None), (prior_core, None), (span, 0), (span_core, 2 * part)]
+    chunks = [(prior, None), (span, 0)]
     state = attention(q, (kv, own_bias), chunks, state=None, last=False, **common)
     prior_far, span_far, *state = lax.optimization_barrier((prior_far, span_far, *state))
     with jax.named_scope("prior_core_far"):
         prior_core_far = swap(prior_far, n, 1)
     with jax.named_scope("span_core_far"):
         span_core_far = swap(span_far, n, 1)
-    chunks = [(prior_far, None), (span_far, part)]
+    chunks = [(prior_far, None), (span_far, part), (prior_core, None), (span_core, 2 * part)]
     state = attention(q, None, chunks, state=state, last=False, **common)
     chunks = [(prior_core_far, None), (span_core_far, 3 * part)]
     heads = attention(q, None, chunks, state=state, last=True, **common)
@@ -584,7 +592,8 @@
         out_specs=[spec(VMEM)] * 3,
         scratch_shapes=[
             VMEM((w_output.shape[0], out_width), BF16),
-            pltpu.SemaphoreType.DMA((3,)),
+            pltpu.SemaphoreType.DMA((2,)),
+            pltpu.SemaphoreType.DMA((w_output.shape[0] // 64,)),
         ],
         compiler_params=params(),
         cost_estimate=cost(2 * rows * 512 * out_width, 1 << 21),

time: 38.7 us -> 37.3 us (0.964)
  Pallas kernels: 16 us -> 14.7 us
    pallas_call x1, Pallas kernels: 2.46 us -> 0.88 us  [body(): pl.pallas_call(query_kernel, out_shape=jax.ShapeDtypeStruct((2 * blocks *...]
    pallas_call x3, Pallas kernels: 6.95 us -> 6.37 us  [attention(): pl.pallas_call(functools.partial(attention_kernel, offsets, own is not No...]
    pallas_call x1, Pallas kernels: 1.07 us -> 1.63 us  [body(): pl.pallas_call(functools.partial(mask_kernel, blocks), out_shape=[jax.Sha...]
  transfers between devices with their start and end apart: 13 -> 13, of which waited for: 6 -> 7; matrix products, arithmetic and copies ran while one was open for 0% -> 0% of each run, Pallas kernels for 34% -> 31%
where the time goes in v4:
time: 37.3 us; the launch traced here: 37.1 us
  starting transfers between devices  15.2 us (41%)
  Pallas kernels  14.7 us (39%)
  waiting for transfers between devices  6.36 us (17%)
  between operations  0.77 us (2%)
    ppermute x11, starting transfers between devices, swap(): return lax.ppermute(x, 'seq', [(i, i ^ step) for i in range(n)])  12.4 us
    pallas_call x3, Pallas kernels, attention(): pl.pallas_call(functools.partial(attention_kernel, offsets, own is not No...  6.37 us
    ppermute x11, waiting for transfers between devices, swap(): return lax.ppermute(x, 'seq', [(i, i ^ step) for i in range(n)])  3.49 us
    pallas_call x1, Pallas kernels, body(): pl.pallas_call(functools.partial(pages_kernel, len(all_span)), out_shape=...  2.56 us
    pallas_call x1, Pallas kernels, body(): pl.pallas_call(functools.partial(kv_kernel, prior_len), out_shape=[jax.Sh...  2.14 us
    pallas_call x1, Pallas kernels, body(): pl.pallas_call(functools.partial(mask_kernel, blocks), out_shape=[jax.Sha...  1.63 us
    ppermute x1, waiting for transfers between devices, body(): peer = lax.ppermute(heads, 'head', [(0, 1), (1, 0)])  1.58 us
    ppermute x1, starting transfers between devices, body(): w_near = lax.ppermute(w_send, 'head', [(0, 1), (1, 0)])  1.49 us
  transfers between devices with their start and end apart: 13, of which 7 were waited for; matrix products, arithmetic and copies ran while one was open for 0% of the time, Pallas kernels for 31%

profile of v4, /device:TPU:0, one launch (start us, length us, event | category | flops | bytes accessed | tf_op | source)
XLA Modules:
  0.0 37.1 jit_solution(17454619436085799368)
XLA Ops:
  0.6 2.1 %shard_map.184 = (bf16[128,256]{1,0:T(8,128)(2,1)S(1)}, bf16[128,256]{1,0:T(8,128)(2,1)S(1)}, bf16[128,2048]{1,0:T(8,128)(2,1)S(1)}, f32[128,128]{1,0:T(8,128)S(...) custom-call(s32[32]{0:T(128)} %order.5, s32[16]{0:T(128)} %table.1, bf16[128,2048]{1,0:T(8,128)(2,1)} %hidden.1, ...), custom_call_target="tpu_custom_call" | custom-call | flops 134217728 | bytes 3145728 | tf_op jit(solution)/shard_map/pallas_call | solution.py:479
  2.8 0.0 copy-start.3
  2.8 3.0 %collective-permute-start.1 = (bf16[128,256]{1,0:T(8,128)(2,1)S(1)}, bf16[128,256]{1,0:T(8,128)(2,1)S(1)}, u32[]{:S(2)}, u32[]{:S(2)}) collective-permute-start(bf16[128,256]{1,0:T(8,128)(2,1)S(1)} %get-tuple-element.30.refs_1_), channel_id=1, source_target_pairs={{0,4},{2,6},{4,0},{6,2},{8,12},{10,14},{12,8},{14,10},{16,20},{18,... | collective-permute-start | bytes 196616 | tf_op jit(solution)/shard_map/span_step_0/ppermute | solution.py:437
  5.8 2.6 %collective-permute-start = (bf16[128,256]{1,0:T(8,128)(2,1)S(1)}, bf16[128,256]{1,0:T(8,128)(2,1)S(1)}, u32[]{:S(2)}, u32[]{:S(2)}) collective-permute-start(bf16[128,256]{1,0:T(8,128)(2,1)S(1)} %get-tuple-element.29), channel_id=1, source_target_pairs={{0,16},{2,18},{4,20},{6,22},{8,24},{10,26},{12,28},{14,30},{16,0},... | collective-permute-start | bytes 196616 | tf_op jit(solution)/shard_map/prior_step_0/ppermute | solution.py:437
  8.4 1.5 %collective-permute-start.11 = (bf16[256,1024]{1,0:T(8,128)(2,1)S(1)}, bf16[256,1024]{1,0:T(8,128)(2,1)S(1)}, u32[]{:S(2)}, u32[]{:S(2)}) collective-permute-start(bf16[256,1024]{1,0:T(8,128)(2,1)S(1)} %get-tuple-element.50), channel_id=1, source_target_pairs={{0,1},{1,0},{2,3},{3,2},{4,5},{5,4},{6,7},{7,6},{8,9},{9,8},{10,11... | collective-permute-start | bytes 1572872 | tf_op jit(solution)/shard_map/weights_step/ppermute | solution.py:527
  9.9 1.2 %collective-permute-start.3 = (bf16[256,256]{1,0:T(8,128)(2,1)S(1)}, bf16[256,256]{1,0:T(8,128)(2,1)S(1)}, u32[]{:S(2)}, u32[]{:S(2)}) collective-permute-start(bf16[256,256]{1,0:T(8,128)(2,1)S(1)} %constant_dynamic-update-slice_fusion.2), channel_id=1, source_target_pairs={{0,16},{2,18},{4,20},{6,22},{8,24},{10,26},{12,28},{14,30},{16,0},... | collective-permute-start | bytes 393224 | tf_op jit(solution)/shard_map/span_step_1/ppermute | solution.py:437
  11.2 0.1 collective-permute-done
  11.3 3.3 %collective-permute-start.2 = (bf16[256,256]{1,0:T(8,128)(2,1)S(1)}, bf16[256,256]{1,0:T(8,128)(2,1)S(1)}, u32[]{:S(2)}, u32[]{:S(2)}) collective-permute-start(bf16[256,256]{1,0:T(8,128)(2,1)S(1)} %constant_dynamic-update-slice_fusion), channel_id=1, source_target_pairs={{0,8},{2,10},{4,12},{6,14},{8,0},{10,2},{12,4},{14,6},{16,24},{18,... | collective-permute-start | bytes 393224 | tf_op jit(solution)/shard_map/prior_step_1/ppermute | solution.py:437
  14.6 1.6 %shard_map.185 = (f32[128,128]{1,0:T(8,128)S(1)}, f32[2,2048]{1,0:T(2,128)S(1)}, bf16[2048,512]{1,0:T(8,128)(2,1)S(1)}) custom-call(s32[32]{0:T(128)} %order.5, s32[32]{0:T(128)} %live.1, s32[16]{0:T(128)} %constant.7.clone.masks, bf16[2048,512]{1,0:T(8,128)(2,1)} %w_query.1, bf16[128,2048]{1,0:T(8,128)(2,1)S(1)} %get-tuple-element.31.turn.normed), custom_call_target="tpu_custom_call" | custom-call | flops 268435456 | bytes 1048576 | tf_op jit(solution)/shard_map/pallas_call | solution.py:529
  16.2 0.9 %shard_map.186.refs_0_ = bf16[1024,256]{1,0:T(8,128)(2,1)S(1)} custom-call(bf16[128,2048]{1,0:T(8,128)(2,1)S(1)} %get-tuple-element.31.turn.normed, f32[128,128]{1,0:T(8,128)S(1)} %get-tuple-element.32.cosine, f32[128,128]{1,0:T(8,128)S(1)} %get-tuple-element.33.sine, bf16[2048,512]{1,0:T(8,128)(2,1)S(1)} %get-tuple-element.34.w_query, f32[1,64]{1,0:T(1,128)S(1)} %bitcast.3), custom_call_target="tpu_custom_call" | custom-call | flops 268435456 | bytes 4194304 | tf_op jit(solution)/shard_map/pallas_call | solution.py:547
  17.1 1.2 %collective-permute-done.3 = bf16[256,256]{1,0:T(8,128)(2,1)S(1)} collective-permute-done((bf16[256,256]{1,0:T(8,128)(2,1)S(1)}, bf16[256,256]{1,0:T(8,128)(2,1)S(1)}, u32[]{:S(2)}, u32[]{:S(2)}) %collective-permute-start.3) | collective-permute-done | bytes 131104 | tf_op jit(solution)/shard_map/span_step_1/ppermute | solution.py:437
  18.3 0.2 collective-permute-done.2
  18.5 0.4 %collective-permute-start.4 = (bf16[512,256]{1,0:T(8,128)(2,1)S(1)}, bf16[512,256]{1,0:T(8,128)(2,1)S(1)}, u32[]{:S(2)}, u32[]{:S(2)}) collective-permute-start(bf16[512,256]{1,0:T(8,128)(2,1)S(1)} %pad_maximum_fusion.refs_3_), channel_id=1, source_target_pairs={{0,4},{2,6},{4,0},{6,2},{8,12},{10,14},{12,8},{14,10},{16,20},{18,... | collective-permute-start | bytes 786440 | tf_op jit(solution)/shard_map/prior_last/ppermute | solution.py:437
  18.9 0.9 %collective-permute-start.5 = (bf16[512,256]{1,0:T(8,128)(2,1)S(1)}, bf16[512,256]{1,0:T(8,128)(2,1)S(1)}, u32[]{:S(2)}, u32[]{:S(2)}) collective-permute-start(bf16[512,256]{1,0:T(8,128)(2,1)S(1)} %pad_maximum_fusion.1.refs_4_.refs_0_), channel_id=1, source_target_pairs={{0,8},{2,10},{4,12},{6,14},{8,0},{10,2},{12,4},{14,6},{16,24},{18,... | collective-permute-start | bytes 786440 | tf_op jit(solution)/shard_map/span_last/ppermute | solution.py:437
  19.7 0.0 collective-permute-start.9
  19.7 0.5 %collective-permute-start.8 = (bf16[512,256]{1,0:T(8,128)(2,1)S(1)}, bf16[512,256]{1,0:T(8,128)(2,1)S(1)}, u32[]{:S(2)}, u32[]{:S(2)}) collective-permute-start(bf16[512,256]{1,0:T(8,128)(2,1)S(1)} %pad_maximum_fusion.refs_3_), channel_id=1, source_target_pairs={{0,2},{2,0},{4,6},{6,4},{8,10},{10,8},{12,14},{14,12},{16,18},{18,... | collective-permute-start | bytes 786440 | tf_op jit(solution)/shard_map/prior_core_near/ppermute | solution.py:437
  20.2 1.3 %collective-permute-done.11.w_near = bf16[256,1024]{1,0:T(8,128)(2,1)S(1)} collective-permute-done((bf16[256,1024]{1,0:T(8,128)(2,1)S(1)}, bf16[256,1024]{1,0:T(8,128)(2,1)S(1)}, u32[]{:S(2)}, u32[]{:S(2)}) %collective-permute-start.11) | collective-permute-done | bytes 524320 | tf_op jit(solution)/shard_map/weights_step/ppermute | solution.py:527
  21.5 0.0 collective-permute-start.12
  21.5 1.7 %shard_map.187 = (f32[1024,128]{1,0:T(8,128)S(1)}, f32[1024,128]{1,0:T(8,128)S(1)}) custom-call(bf16[1024,256]{1,0:T(8,128)(2,1)S(1)} %shard_map.186.refs_0_, bf16[128,256]{1,0:T(8,128)(2,1)S(1)} %get-tuple-element.30.refs_1_, f32[128,128]{1,0:T(8,128)S(1)} %get-tuple-element.37.refs_2_, bf16[512,256]{1,0:T(8,128)(2,1)S(1)} %pad_maximum_fusion.refs_3_, ...), custom_call_target="tpu_custom_call" | custom-call | flops 1073741824 | bytes 2621440 | tf_op jit(solution)/shard_map/pallas_call | solution.py:359
  23.2 1.7 %collective-permute-done.4.refs_1_ = bf16[512,256]{1,0:T(8,128)(2,1)S(1)} collective-permute-done((bf16[512,256]{1,0:T(8,128)(2,1)S(1)}, bf16[512,256]{1,0:T(8,128)(2,1)S(1)}, u32[]{:S(2)}, u32[]{:S(2)}) %collective-permute-start.4) | collective-permute-done | bytes 262176 | tf_op jit(solution)/shard_map/prior_last/ppermute | solution.py:437
  24.9 0.3 collective-permute-done.5.refs_2_.refs_1_
  25.2 0.0 collective-permute-start.6
  25.2 0.5 %collective-permute-start.7 = (bf16[512,256]{1,0:T(8,128)(2,1)S(1)}, bf16[512,256]{1,0:T(8,128)(2,1)S(1)}, u32[]{:S(2)}, u32[]{:S(2)}) collective-permute-start(bf16[512,256]{1,0:T(8,128)(2,1)S(1)} %collective-permute-done.5.refs_2_.refs_1_), channel_id=1, source_target_pairs={{0,2},{2,0},{4,6},{6,4},{8,10},{10,8},{12,14},{14,12},{16,18},{18,... | collective-permute-start | bytes 786440 | tf_op jit(solution)/shard_map/span_core_far/ppermute | solution.py:437
  25.7 2.8 %shard_map.188 = (f32[1024,128]{1,0:T(8,128)S(1)}, f32[1024,128]{1,0:T(8,128)S(1)}) custom-call(bf16[1024,256]{1,0:T(8,128)(2,1)S(1)} %shard_map.186.refs_0_, bf16[512,256]{1,0:T(8,128)(2,1)S(1)} %collective-permute-done.4.refs_1_, bf16[512,256]{1,0:T(8,128)(2,1)S(1)} %collective-permute-done.5.refs_2_.refs_1_, ...), custom_call_target="tpu_custom_call" | custom-call | flops 2147483648 | bytes 3145728 | tf_op jit(solution)/shard_map/pallas_call | solution.py:359
  28.6 0.0 copy-start
  28.6 0.0 copy-start.1
  28.6 0.0 copy-start.2
  28.6 1.9 %shard_map.189.mine = bf16[128,512]{1,0:T(8,128)(2,1)S(1)} custom-call(bf16[1024,256]{1,0:T(8,128)(2,1)S(1)} %shard_map.186.refs_0_, bf16[512,256]{1,0:T(8,128)(2,1)S(1)} %collective-permute-done.6.refs_1_, bf16[512,256]{1,0:T(8,128)(2,1)S(1)} %collective-permute-done.7.refs_2_.refs_3_, f32[2,2048]{1,0:T(2,128)S(1)} %get-tuple-element.40.refs_5_.refs_3_, ...), custom_call_target="tpu_custom_call" | custom-call | flops 1073741824 | bytes 2621440 | tf_op jit(solution)/shard_map/pallas_call | solution.py:359
  30.5 1.3 %collective-permute-start.10 = (bf16[128,512]{1,0:T(8,128)(2,1)S(1)}, bf16[128,512]{1,0:T(8,128)(2,1)S(1)}, u32[]{:S(2)}, u32[]{:S(2)}) collective-permute-start(bf16[128,512]{1,0:T(8,128)(2,1)S(1)} %shard_map.189.mine), channel_id=1, source_target_pairs={{0,1},{1,0},{2,3},{3,2},{4,5},{5,4},{6,7},{7,6},{8,9},{9,8},{10,11... | collective-permute-start | bytes 393224 | tf_op jit(solution)/shard_map/ppermute | solution.py:584
  31.9 2.6 %shard_map.190 = (bf16[1,128,128]{2,1,0:T(8,128)(2,1)}, bf16[1,128,128]{2,1,0:T(8,128)(2,1)}, f32[128,1024]{1,0:T(8,128)S(1)}) custom-call(s32[16]{0:T(128)S(1)} %copy-done.1, s32[32]{0:T(128)S(1)} %copy-done, s32[16]{0:T(128)S(1)} %copy-done.2, bf16[128,512]{1,0:T(8,128)(2,1)S(1)} %shard_map.189.mine, bf16[512,2048]{1,0:T(8,128)(2,1)} %w_output.3, ...), custom_call_target="tpu_custom_call" | custom-call | flops 134217728 | bytes 2097152 | tf_op jit(solution)/shard_map/pallas_call | solution.py:587
  34.4 1.6 %collective-permute-done.10.peer = bf16[128,512]{1,0:T(8,128)(2,1)S(1)} collective-permute-done((bf16[128,512]{1,0:T(8,128)(2,1)S(1)}, bf16[128,512]{1,0:T(8,128)(2,1)S(1)}, u32[]{:S(2)}, u32[]{:S(2)}) %collective-permute-start.10) | collective-permute-done | bytes 131104 | tf_op jit(solution)/shard_map/ppermute | solution.py:584
  36.0 1.1 %shard_map.191 = f32[128,1024]{1,0:T(8,128)} custom-call(f32[128,1024]{1,0:T(8,128)S(1)} %get-tuple-element.49.partial, bf16[128,512]{1,0:T(8,128)(2,1)S(1)} %collective-permute-done.10.peer, bf16[256,1024]{1,0:T(8,128)(2,1)S(1)} %collective-permute-done.11.w_near, bf16[256,1024]{1,0:T(8,128)(2,1)S(1)} %collective-permute-done.12.w_far), custom_call_target="tpu_custom_call" | custom-call | flops 134217728 | bytes 2097152 | tf_op jit(solution)/shard_map/pallas_call | solution.py:602
  (16 shorter events, 0.1 us)
Async XLA Ops:
  2.8 13.4 %copy-start.3 = (f32[64]{0:T(128)S(1)}, f32[64]{0:T(128)}, u32[]{:S(2)}) copy-start(f32[64]{0:T(128)} %param.22) | copy-start | bytes 772
  2.8 7.1 %collective-permute-start.1 = (bf16[128,256]{1,0:T(8,128)(2,1)S(1)}, bf16[128,256]{1,0:T(8,128)(2,1)S(1)}, u32[]{:S(2)}, u32[]{:S(2)}) collective-permute-start(bf16[128,256]{1,0:T(8,128)(2,1)S(1)} %get-tuple-element.30.refs_1_), channel_id=1, source_target_pairs={{0,4},{2,6},{4,0},{6,2},{8,12},{10,14},{12,8},{14,10},{16,20},{18,... | collective-permute-start | bytes 196616 | tf_op jit(solution)/shard_map/span_step_0/ppermute | solution.py:437
  5.8 5.5 %collective-permute-start = (bf16[128,256]{1,0:T(8,128)(2,1)S(1)}, bf16[128,256]{1,0:T(8,128)(2,1)S(1)}, u32[]{:S(2)}, u32[]{:S(2)}) collective-permute-start(bf16[128,256]{1,0:T(8,128)(2,1)S(1)} %get-tuple-element.29), channel_id=1, source_target_pairs={{0,16},{2,18},{4,20},{6,22},{8,24},{10,26},{12,28},{14,30},{16,0},... | collective-permute-start | bytes 196616 | tf_op jit(solution)/shard_map/prior_step_0/ppermute | solution.py:437
  8.4 13.1 %collective-permute-start.11 = (bf16[256,1024]{1,0:T(8,128)(2,1)S(1)}, bf16[256,1024]{1,0:T(8,128)(2,1)S(1)}, u32[]{:S(2)}, u32[]{:S(2)}) collective-permute-start(bf16[256,1024]{1,0:T(8,128)(2,1)S(1)} %get-tuple-element.50), channel_id=1, source_target_pairs={{0,1},{1,0},{2,3},{3,2},{4,5},{5,4},{6,7},{7,6},{8,9},{9,8},{10,11... | collective-permute-start | bytes 1572872 | tf_op jit(solution)/shard_map/weights_step/ppermute | solution.py:527
  9.9 8.3 %collective-permute-start.3 = (bf16[256,256]{1,0:T(8,128)(2,1)S(1)}, bf16[256,256]{1,0:T(8,128)(2,1)S(1)}, u32[]{:S(2)}, u32[]{:S(2)}) collective-permute-start(bf16[256,256]{1,0:T(8,128)(2,1)S(1)} %constant_dynamic-update-slice_fusion.2), channel_id=1, source_target_pairs={{0,16},{2,18},{4,20},{6,22},{8,24},{10,26},{12,28},{14,30},{16,0},... | collective-permute-start | bytes 393224 | tf_op jit(solution)/shard_map/span_step_1/ppermute | solution.py:437
  11.3 7.2 %collective-permute-start.2 = (bf16[256,256]{1,0:T(8,128)(2,1)S(1)}, bf16[256,256]{1,0:T(8,128)(2,1)S(1)}, u32[]{:S(2)}, u32[]{:S(2)}) collective-permute-start(bf16[256,256]{1,0:T(8,128)(2,1)S(1)} %constant_dynamic-update-slice_fusion), channel_id=1, source_target_pairs={{0,8},{2,10},{4,12},{6,14},{8,0},{10,2},{12,4},{14,6},{16,24},{18,... | collective-permute-start | bytes 393224 | tf_op jit(solution)/shard_map/prior_step_1/ppermute | solution.py:437
  18.5 6.4 %collective-permute-start.4 = (bf16[512,256]{1,0:T(8,128)(2,1)S(1)}, bf16[512,256]{1,0:T(8,128)(2,1)S(1)}, u32[]{:S(2)}, u32[]{:S(2)}) collective-permute-start(bf16[512,256]{1,0:T(8,128)(2,1)S(1)} %pad_maximum_fusion.refs_3_), channel_id=1, source_target_pairs={{0,4},{2,6},{4,0},{6,2},{8,12},{10,14},{12,8},{14,10},{16,20},{18,... | collective-permute-start | bytes 786440 | tf_op jit(solution)/shard_map/prior_last/ppermute | solution.py:437
  18.9 6.4 %collective-permute-start.5 = (bf16[512,256]{1,0:T(8,128)(2,1)S(1)}, bf16[512,256]{1,0:T(8,128)(2,1)S(1)}, u32[]{:S(2)}, u32[]{:S(2)}) collective-permute-start(bf16[512,256]{1,0:T(8,128)(2,1)S(1)} %pad_maximum_fusion.1.refs_4_.refs_0_), channel_id=1, source_target_pairs={{0,8},{2,10},{4,12},{6,14},{8,0},{10,2},{12,4},{14,6},{16,24},{18,... | collective-permute-start | bytes 786440 | tf_op jit(solution)/shard_map/span_last/ppermute | solution.py:437
  19.7 6.0 %collective-permute-start.9 = (bf16[512,256]{1,0:T(8,128)(2,1)S(1)}, bf16[512,256]{1,0:T(8,128)(2,1)S(1)}, u32[]{:S(2)}, u32[]{:S(2)}) collective-permute-start(bf16[512,256]{1,0:T(8,128)(2,1)S(1)} %pad_maximum_fusion.1.refs_4_.refs_0_), channel_id=1, source_target_pairs={{0,2},{2,0},{4,6},{6,4},{8,10},{10,8},{12,14},{14,12},{16,18},{18,... | collective-permute-start | bytes 786440 | tf_op jit(solution)/shard_map/span_core_near/ppermute | solution.py:437
  19.7 6.0 %collective-permute-start.8 = (bf16[512,256]{1,0:T(8,128)(2,1)S(1)}, bf16[512,256]{1,0:T(8,128)(2,1)S(1)}, u32[]{:S(2)}, u32[]{:S(2)}) collective-permute-start(bf16[512,256]{1,0:T(8,128)(2,1)S(1)} %pad_maximum_fusion.refs_3_), channel_id=1, source_target_pairs={{0,2},{2,0},{4,6},{6,4},{8,10},{10,8},{12,14},{14,12},{16,18},{18,... | collective-permute-start | bytes 786440 | tf_op jit(solution)/shard_map/prior_core_near/ppermute | solution.py:437
  21.5 14.5 %collective-permute-start.12 = (bf16[256,1024]{1,0:T(8,128)(2,1)S(1)}, bf16[256,1024]{1,0:T(8,128)(2,1)S(1)}, u32[]{:S(2)}, u32[]{:S(2)}) collective-permute-start(bf16[256,1024]{1,0:T(8,128)(2,1)S(1)} %collective-permute-done.11.w_near), channel_id=1, source_target_pairs={{0,2},{2,0},{4,6},{6,4},{8,10},{10,8},{12,14},{14,12},{16,18},{18,... | collective-permute-start | bytes 1572872 | tf_op jit(solution)/shard_map/weights_step/ppermute | solution.py:437
  25.2 3.4 %collective-permute-start.6 = (bf16[512,256]{1,0:T(8,128)(2,1)S(1)}, bf16[512,256]{1,0:T(8,128)(2,1)S(1)}, u32[]{:S(2)}, u32[]{:S(2)}) collective-permute-start(bf16[512,256]{1,0:T(8,128)(2,1)S(1)} %collective-permute-done.4.refs_1_), channel_id=1, source_target_pairs={{0,2},{2,0},{4,6},{6,4},{8,10},{10,8},{12,14},{14,12},{16,18},{18,... | collective-permute-start | bytes 786440 | tf_op jit(solution)/shard_map/prior_core_far/ppermute | solution.py:437
  25.2 3.4 %collective-permute-start.7 = (bf16[512,256]{1,0:T(8,128)(2,1)S(1)}, bf16[512,256]{1,0:T(8,128)(2,1)S(1)}, u32[]{:S(2)}, u32[]{:S(2)}) collective-permute-start(bf16[512,256]{1,0:T(8,128)(2,1)S(1)} %collective-permute-done.5.refs_2_.refs_1_), channel_id=1, source_target_pairs={{0,2},{2,0},{4,6},{6,4},{8,10},{10,8},{12,14},{14,12},{16,18},{18,... | collective-permute-start | bytes 786440 | tf_op jit(solution)/shard_map/span_core_far/ppermute | solution.py:437
  28.6 3.3 %copy-start = (s32[32]{0:T(128)S(1)}, s32[32]{0:T(128)}, u32[]{:S(2)}) copy-start(s32[32]{0:T(128)} %order.5) | copy-start | bytes 388
  28.6 3.2 %copy-start.1 = (s32[16]{0:T(128)S(1)}, s32[16]{0:T(128)}, u32[]{:S(2)}) copy-start(s32[16]{0:T(128)} %dest.1) | copy-start | bytes 196
  28.6 3.2 %copy-start.2 = (s32[16]{0:T(128)S(1)}, s32[16]{0:T(128)}, u32[]{:S(2)}) copy-start(s32[16]{0:T(128)} %constant.8.clone.where) | copy-start | bytes 196
  30.5 5.5 %collective-permute-start.10 = (bf16[128,512]{1,0:T(8,128)(2,1)S(1)}, bf16[128,512]{1,0:T(8,128)(2,1)S(1)}, u32[]{:S(2)}, u32[]{:S(2)}) collective-permute-start(bf16[128,512]{1,0:T(8,128)(2,1)S(1)} %shard_map.189.mine), channel_id=1, source_target_pairs={{0,1},{1,0},{2,3},{3,2},{4,5},{5,4},{6,7},{7,6},{8,9},{9,8},{10,11... | collective-permute-start | bytes 393224 | tf_op jit(solution)/shard_map/ppermute | solution.py:584

commit v5 on v4

--- a/solution.py
+++ b/solution.py
@@ -265,7 +265,7 @@
             mix(t - 1)
 
 
-def attention_kernel(offsets, own, first, last, step, blocks, group, *refs):
+def attention_kernel(offsets, join, own, first, last, step, blocks, group, *refs):
     refs = list(refs)
     q = refs.pop(0)
     own_kv, own_bias = (refs.pop(0), refs.pop(0)) if own else (None, None)
@@ -306,7 +306,9 @@
             ]
 
     if not refs:
-        pieces = [piece(chunk[...], at) for chunk, at in zip(chunks, offsets)]
+        rows = [chunk[...] for chunk in chunks]
+        starts = range(0, len(rows), join)
+        pieces = [piece(jnp.concatenate(rows[i : i + join], axis=0), offsets[i]) for i in starts]
         fold(
             q, m_in, acc_in, m_ref, acc_ref, pieces + extra, blocks, part, finish if last else None
         )
@@ -334,7 +336,7 @@
             finish(b, tiles[b], tiles[blocks + b])
 
 
-def attention(q, own, chunks, bias, state, last, blocks, group):
+def attention(q, own, chunks, bias, state, last, blocks, group, join=1):
     arrays, offsets = zip(*chunks)
     rows = sum(c.shape[0] for c in arrays)
     direct = rows <= 2048
@@ -358,14 +360,14 @@
         outs, out_specs = pair, [spec(VMEM)] * 2
     return pl.pallas_call(
         functools.partial(
-            attention_kernel, offsets, own is not None, first, last, step, blocks, group
+            attention_kernel, offsets, join, own is not None, first, last, step, blocks, group
         ),
         out_shape=outs,
         in_specs=specs,
         out_specs=out_specs,
         scratch_shapes=scratch,
         compiler_params=params(32),
-        cost_estimate=cost(4 * n * rows * 256, rows * 512 + n * 2048),
+        cost_estimate=cost(1000, 1000) if first or join > 1 else cost(4 * n * rows * 256, rows * 512 + n * 2048),
     )(*operands)
 
 
@@ -563,27 +565,31 @@
     with jax.named_scope("span_last"):
         span_far = swap(span, n, span_steps[-1])
     prior, span = after(prior, own_bias), after(span, own_bias)
+    half = prior.shape[0] // 2
     with jax.named_scope("prior_core_near"):
-        prior_core = swap(prior, n, 1)
+        prior_core = [swap(prior[:half], n, 1), swap(prior[half:], n, 1)]
     with jax.named_scope("span_core_near"):
-        span_core = swap(span, n, 1)
+        span_core = [swap(span[:half], n, 1), swap(span[half:], n, 1)]
 
     common = dict(bias=span_bias, blocks=blocks, group=group)
     part = n // 4 * PAGE
     chunks = [(prior, None), (span, 0)]
     state = attention(q, (kv, own_bias), chunks, state=None, last=False, **common)
+    chunks = [(c, None) for c in prior_core]
+    chunks += [(c, 2 * part + i * half) for i, c in enumerate(span_core)]
+    state = attention(q, None, chunks, state=state, last=False, join=2, **common)
     prior_far, span_far, *state = lax.optimization_barrier((prior_far, span_far, *state))
     with jax.named_scope("prior_core_far"):
         prior_core_far = swap(prior_far, n, 1)
     with jax.named_scope("span_core_far"):
         span_core_far = swap(span_far, n, 1)
-    chunks = [(prior_far, None), (span_far, part), (prior_core, None), (span_core, 2 * part)]
+    chunks = [(prior_far, None), (span_far, part)]
     state = attention(q, None, chunks, state=state, last=False, **common)
     chunks = [(prior_core_far, None), (span_core_far, 3 * part)]
     heads = attention(q, None, chunks, state=state, last=True, **common)
     peer = lax.ppermute(heads, "head", [(0, 1), (1, 0)])
 
-    all_span = [span, span_far, span_core, span_core_far]
+    all_span = [span, span_far, *span_core, span_core_far]
     new_keys, new_values, partial = pl.pallas_call(
         functools.partial(pages_kernel, len(all_span)),
         out_shape=[jax.ShapeDtypeStruct((1, PAGE, 128), BF16)] * 2

time: 37.3 us -> 36.8 us (0.987)
  waiting for transfers between devices: 6.36 us -> 4.04 us
  starting transfers between devices: 15.2 us -> 16.2 us
  Pallas kernels: 14.7 us -> 15.1 us
    ppermute x1, waiting for transfers between devices: 1.29 us -> 0.01 us  [body(): w_near = lax.ppermute(w_send, 'head', [(0, 1), (1, 0)])]
    ppermute x11 -> x13, waiting for transfers between devices: 3.49 us -> 2.37 us  [swap(): return lax.ppermute(x, 'seq', [(i, i ^ step) for i in range(n)])]
    ppermute x11 -> x13, starting transfers between devices: 12.4 us -> 13.2 us  [swap(): return lax.ppermute(x, 'seq', [(i, i ^ step) for i in range(n)])]
    pallas_call x3 -> x4, Pallas kernels: 6.37 us -> 6.84 us  [attention(): pl.pallas_call(functools.partial(attention_kernel, offsets, join, own is...]
  transfers between devices with their start and end apart: 13 -> 15, of which waited for: 7 -> 5; matrix products, arithmetic and copies ran while one was open for 0% -> 0% of each run, Pallas kernels for 31% -> 33%
where the time goes in v5:
time: 36.8 us; the launch traced here: 36.3 us
  starting transfers between devices  16.2 us (44%)
  Pallas kernels  15.1 us (41%)
  waiting for transfers between devices  4.04 us (11%)
  between operations  0.82 us (2%)
    ppermute x13, starting transfers between devices, swap(): return lax.ppermute(x, 'seq', [(i, i ^ step) for i in range(n)])  13.2 us
    pallas_call x4, Pallas kernels, attention(): pl.pallas_call(functools.partial(attention_kernel, offsets, join, own is...  6.84 us
    pallas_call x1, Pallas kernels, body(): pl.pallas_call(functools.partial(pages_kernel, len(all_span)), out_shape=...  2.56 us
    ppermute x13, waiting for transfers between devices, swap(): return lax.ppermute(x, 'seq', [(i, i ^ step) for i in range(n)])  2.37 us
    pallas_call x1, Pallas kernels, body(): pl.pallas_call(functools.partial(kv_kernel, prior_len), out_shape=[jax.Sh...  2.14 us
    ppermute x1, waiting for transfers between devices, body(): peer = lax.ppermute(heads, 'head', [(0, 1), (1, 0)])  1.67 us
    pallas_call x1, Pallas kernels, body(): pl.pallas_call(functools.partial(mask_kernel, blocks), out_shape=[jax.Sha...  1.63 us
    ppermute x1, starting transfers between devices, body(): peer = lax.ppermute(heads, 'head', [(0, 1), (1, 0)])  1.55 us
  transfers between devices with their start and end apart: 15, of which 5 were waited for; matrix products, arithmetic and copies ran while one was open for 0% of the time, Pallas kernels for 33%

profile of v5, /device:TPU:0, one launch (start us, length us, event | category | flops | bytes accessed | tf_op | source)
XLA Modules:
  0.0 36.3 jit_solution(15813514186870902471)
XLA Ops:
  0.6 2.1 %shard_map.184 = (bf16[128,256]{1,0:T(8,128)(2,1)S(1)}, bf16[128,256]{1,0:T(8,128)(2,1)S(1)}, bf16[128,2048]{1,0:T(8,128)(2,1)S(1)}, f32[128,128]{1,0:T(8,128)S(...) custom-call(s32[32]{0:T(128)} %order.5, s32[16]{0:T(128)} %table.1, bf16[128,2048]{1,0:T(8,128)(2,1)} %hidden.1, ...), custom_call_target="tpu_custom_call" | custom-call | flops 134217728 | bytes 3145728 | tf_op jit(solution)/shard_map/pallas_call | solution.py:481
  2.8 3.0 %collective-permute-start.1 = (bf16[128,256]{1,0:T(8,128)(2,1)S(1)}, bf16[128,256]{1,0:T(8,128)(2,1)S(1)}, u32[]{:S(2)}, u32[]{:S(2)}) collective-permute-start(bf16[128,256]{1,0:T(8,128)(2,1)S(1)} %get-tuple-element.32.refs_1_), channel_id=1, source_target_pairs={{0,4},{2,6},{4,0},{6,2},{8,12},{10,14},{12,8},{14,10},{16,20},{18,... | collective-permute-start | bytes 196616 | tf_op jit(solution)/shard_map/span_step_0/ppermute | solution.py:439
  5.8 2.6 %collective-permute-start = (bf16[128,256]{1,0:T(8,128)(2,1)S(1)}, bf16[128,256]{1,0:T(8,128)(2,1)S(1)}, u32[]{:S(2)}, u32[]{:S(2)}) collective-permute-start(bf16[128,256]{1,0:T(8,128)(2,1)S(1)} %get-tuple-element.31), channel_id=1, source_target_pairs={{0,16},{2,18},{4,20},{6,22},{8,24},{10,26},{12,28},{14,30},{16,0},... | collective-permute-start | bytes 196616 | tf_op jit(solution)/shard_map/prior_step_0/ppermute | solution.py:439
  8.4 1.5 %collective-permute-start.13 = (bf16[256,1024]{1,0:T(8,128)(2,1)S(1)}, bf16[256,1024]{1,0:T(8,128)(2,1)S(1)}, u32[]{:S(2)}, u32[]{:S(2)}) collective-permute-start(bf16[256,1024]{1,0:T(8,128)(2,1)S(1)} %get-tuple-element.54), channel_id=1, source_target_pairs={{0,1},{1,0},{2,3},{3,2},{4,5},{5,4},{6,7},{7,6},{8,9},{9,8},{10,11... | collective-permute-start | bytes 1572872 | tf_op jit(solution)/shard_map/weights_step/ppermute | solution.py:529
  9.9 1.2 %collective-permute-start.3 = (bf16[256,256]{1,0:T(8,128)(2,1)S(1)}, bf16[256,256]{1,0:T(8,128)(2,1)S(1)}, u32[]{:S(2)}, u32[]{:S(2)}) collective-permute-start(bf16[256,256]{1,0:T(8,128)(2,1)S(1)} %constant_dynamic-update-slice_fusion.2), channel_id=1, source_target_pairs={{0,16},{2,18},{4,20},{6,22},{8,24},{10,26},{12,28},{14,30},{16,0},... | collective-permute-start | bytes 393224 | tf_op jit(solution)/shard_map/span_step_1/ppermute | solution.py:439
  11.2 0.1 collective-permute-done
  11.3 3.3 %collective-permute-start.2 = (bf16[256,256]{1,0:T(8,128)(2,1)S(1)}, bf16[256,256]{1,0:T(8,128)(2,1)S(1)}, u32[]{:S(2)}, u32[]{:S(2)}) collective-permute-start(bf16[256,256]{1,0:T(8,128)(2,1)S(1)} %constant_dynamic-update-slice_fusion), channel_id=1, source_target_pairs={{0,8},{2,10},{4,12},{6,14},{8,0},{10,2},{12,4},{14,6},{16,24},{18,... | collective-permute-start | bytes 393224 | tf_op jit(solution)/shard_map/prior_step_1/ppermute | solution.py:439
  14.6 1.6 %shard_map.185 = (f32[128,128]{1,0:T(8,128)S(1)}, f32[2,2048]{1,0:T(2,128)S(1)}, bf16[2048,512]{1,0:T(8,128)(2,1)S(1)}) custom-call(s32[32]{0:T(128)} %order.5, s32[32]{0:T(128)} %live.1, s32[16]{0:T(128)} %constant.7.clone.masks, bf16[2048,512]{1,0:T(8,128)(2,1)} %w_query.1, bf16[128,2048]{1,0:T(8,128)(2,1)S(1)} %get-tuple-element.33.turn.normed), custom_call_target="tpu_custom_call" | custom-call | flops 268435456 | bytes 1048576 | tf_op jit(solution)/shard_map/pallas_call | solution.py:531
  16.2 0.8 %shard_map.186.refs_0_ = bf16[1024,256]{1,0:T(8,128)(2,1)S(1)} custom-call(bf16[128,2048]{1,0:T(8,128)(2,1)S(1)} %get-tuple-element.33.turn.normed, f32[128,128]{1,0:T(8,128)S(1)} %get-tuple-element.34.cosine, f32[128,128]{1,0:T(8,128)S(1)} %get-tuple-element.35.sine, bf16[2048,512]{1,0:T(8,128)(2,1)S(1)} %get-tuple-element.36.w_query, f32[1,64]{1,0:T(1,128)S(1)} %bitcast.3), custom_call_target="tpu_custom_call" | custom-call | flops 268435456 | bytes 4194304 | tf_op jit(solution)/shard_map/pallas_call | solution.py:549
  17.1 1.2 %collective-permute-done.3 = bf16[256,256]{1,0:T(8,128)(2,1)S(1)} collective-permute-done((bf16[256,256]{1,0:T(8,128)(2,1)S(1)}, bf16[256,256]{1,0:T(8,128)(2,1)S(1)}, u32[]{:S(2)}, u32[]{:S(2)}) %collective-permute-start.3) | collective-permute-done | bytes 131104 | tf_op jit(solution)/shard_map/span_step_1/ppermute | solution.py:439
  18.3 0.2 collective-permute-done.2
  18.5 0.4 %collective-permute-start.4 = (bf16[512,256]{1,0:T(8,128)(2,1)S(1)}, bf16[512,256]{1,0:T(8,128)(2,1)S(1)}, u32[]{:S(2)}, u32[]{:S(2)}) collective-permute-start(bf16[512,256]{1,0:T(8,128)(2,1)S(1)} %pad_maximum_fusion.refs_3_), channel_id=1, source_target_pairs={{0,4},{2,6},{4,0},{6,2},{8,12},{10,14},{12,8},{14,10},{16,20},{18,... | collective-permute-start | bytes 786440 | tf_op jit(solution)/shard_map/prior_last/ppermute | solution.py:439
  18.9 0.9 %collective-permute-start.5 = (bf16[512,256]{1,0:T(8,128)(2,1)S(1)}, bf16[512,256]{1,0:T(8,128)(2,1)S(1)}, u32[]{:S(2)}, u32[]{:S(2)}) collective-permute-start(bf16[512,256]{1,0:T(8,128)(2,1)S(1)} %pad_maximum_fusion.1.refs_4_.refs_0_), channel_id=1, source_target_pairs={{0,8},{2,10},{4,12},{6,14},{8,0},{10,2},{12,4},{14,6},{16,24},{18,... | collective-permute-start | bytes 786440 | tf_op jit(solution)/shard_map/span_last/ppermute | solution.py:439
  19.7 0.1 collective-permute-start.8
  19.8 0.5 %collective-permute-start.9 = (bf16[256,256]{1,0:T(8,128)(2,1)S(1)}, bf16[256,256]{1,0:T(8,128)(2,1)S(1)}, u32[]{:S(2)}, u32[]{:S(2)}) collective-permute-start(bf16[256,256]{1,0:T(8,128)(2,1)S(1)} %get-tuple-element.57), channel_id=1, source_target_pairs={{0,2},{2,0},{4,6},{6,4},{8,10},{10,8},{12,14},{14,12},{16,18},{18,... | collective-permute-start | bytes 393224 | tf_op jit(solution)/shard_map/span_core_near/ppermute | solution.py:439
  20.3 0.8 %collective-permute-done.8.refs_3_.refs_2_ = bf16[256,256]{1,0:T(8,128)(2,1)S(1)} collective-permute-done((bf16[256,256]{1,0:T(8,128)(2,1)S(1)}, bf16[256,256]{1,0:T(8,128)(2,1)S(1)}, u32[]{:S(2)}, u32[]{:S(2)}) %collective-permute-start.8) | collective-permute-done | bytes 131104 | tf_op jit(solution)/shard_map/span_core_near/ppermute | solution.py:439
  21.2 0.1 collective-permute-start.6
  21.3 0.0 collective-permute-done.9.refs_4_.refs_3_
  21.3 0.3 collective-permute-start.7
  21.7 0.2 collective-permute-start.14
  21.9 1.6 %shard_map.187 = (f32[1024,128]{1,0:T(8,128)S(1)}, f32[1024,128]{1,0:T(8,128)S(1)}) custom-call(bf16[1024,256]{1,0:T(8,128)(2,1)S(1)} %shard_map.186.refs_0_, bf16[128,256]{1,0:T(8,128)(2,1)S(1)} %get-tuple-element.32.refs_1_, f32[128,128]{1,0:T(8,128)S(1)} %get-tuple-element.39.refs_2_, bf16[512,256]{1,0:T(8,128)(2,1)S(1)} %pad_maximum_fusion.refs_3_, ...), custom_call_target="tpu_custom_call" | custom-call | flops 1000 | bytes 1000 | tf_op jit(solution)/shard_map/pallas_call | solution.py:361
  23.5 1.7 %shard_map.188 = (f32[1024,128]{1,0:T(8,128)S(1)}, f32[1024,128]{1,0:T(8,128)S(1)}) custom-call(bf16[1024,256]{1,0:T(8,128)(2,1)S(1)} %shard_map.186.refs_0_, bf16[256,256]{1,0:T(8,128)(2,1)S(1)} %collective-permute-done.6.refs_1_, bf16[256,256]{1,0:T(8,128)(2,1)S(1)} %collective-permute-done.7.refs_2_, ...), custom_call_target="tpu_custom_call" | custom-call | flops 1000 | bytes 1000 | tf_op jit(solution)/shard_map/pallas_call | solution.py:361
  25.2 0.0 collective-permute-done.5.refs_2_.refs_1_
  25.2 0.4 %collective-permute-start.10 = (bf16[512,256]{1,0:T(8,128)(2,1)S(1)}, bf16[512,256]{1,0:T(8,128)(2,1)S(1)}, u32[]{:S(2)}, u32[]{:S(2)}) collective-permute-start(bf16[512,256]{1,0:T(8,128)(2,1)S(1)} %collective-permute-done.4.refs_1_), channel_id=1, source_target_pairs={{0,2},{2,0},{4,6},{6,4},{8,10},{10,8},{12,14},{14,12},{16,18},{18,... | collective-permute-start | bytes 786440 | tf_op jit(solution)/shard_map/prior_core_far/ppermute | solution.py:439
  25.6 0.2 collective-permute-start.11
  25.8 1.7 %shard_map.189 = (f32[1024,128]{1,0:T(8,128)S(1)}, f32[1024,128]{1,0:T(8,128)S(1)}) custom-call(bf16[1024,256]{1,0:T(8,128)(2,1)S(1)} %shard_map.186.refs_0_, bf16[512,256]{1,0:T(8,128)(2,1)S(1)} %collective-permute-done.4.refs_1_, bf16[512,256]{1,0:T(8,128)(2,1)S(1)} %collective-permute-done.5.refs_2_.refs_1_, ...), custom_call_target="tpu_custom_call" | custom-call | flops 1073741824 | bytes 2621440 | tf_op jit(solution)/shard_map/pallas_call | solution.py:361
  27.5 0.0 copy-start.2
  27.5 1.9 %shard_map.190.mine = bf16[128,512]{1,0:T(8,128)(2,1)S(1)} custom-call(bf16[1024,256]{1,0:T(8,128)(2,1)S(1)} %shard_map.186.refs_0_, bf16[512,256]{1,0:T(8,128)(2,1)S(1)} %collective-permute-done.10.refs_1_, bf16[512,256]{1,0:T(8,128)(2,1)S(1)} %collective-permute-done.11.refs_2_.refs_4_, f32[2,2048]{1,0:T(2,128)S(1)} %get-tuple-element.42.refs_5_.refs_3_, ...), custom_call_target="tpu_custom_call" | custom-call | flops 1073741824 | bytes 2621440 | tf_op jit(solution)/shard_map/pallas_call | solution.py:361
  29.4 1.6 %collective-permute-start.12 = (bf16[128,512]{1,0:T(8,128)(2,1)S(1)}, bf16[128,512]{1,0:T(8,128)(2,1)S(1)}, u32[]{:S(2)}, u32[]{:S(2)}) collective-permute-start(bf16[128,512]{1,0:T(8,128)(2,1)S(1)} %shard_map.190.mine), channel_id=1, source_target_pairs={{0,1},{1,0},{2,3},{3,2},{4,5},{5,4},{6,7},{7,6},{8,9},{9,8},{10,11... | collective-permute-start | bytes 393224 | tf_op jit(solution)/shard_map/ppermute | solution.py:590
  31.0 2.6 %shard_map.191 = (bf16[1,128,128]{2,1,0:T(8,128)(2,1)}, bf16[1,128,128]{2,1,0:T(8,128)(2,1)}, f32[128,1024]{1,0:T(8,128)S(1)}) custom-call(s32[16]{0:T(128)S(1)} %copy-done.1, s32[32]{0:T(128)S(1)} %copy-done, s32[16]{0:T(128)S(1)} %copy-done.2, bf16[128,512]{1,0:T(8,128)(2,1)S(1)} %shard_map.190.mine, bf16[512,2048]{1,0:T(8,128)(2,1)} %w_output.3, ...), custom_call_target="tpu_custom_call" | custom-call | flops 134217728 | bytes 2097152 | tf_op jit(solution)/shard_map/pallas_call | solution.py:593
  33.5 1.7 %collective-permute-done.12.peer = bf16[128,512]{1,0:T(8,128)(2,1)S(1)} collective-permute-done((bf16[128,512]{1,0:T(8,128)(2,1)S(1)}, bf16[128,512]{1,0:T(8,128)(2,1)S(1)}, u32[]{:S(2)}, u32[]{:S(2)}) %collective-permute-start.12) | collective-permute-done | bytes 131104 | tf_op jit(solution)/shard_map/ppermute | solution.py:590
  35.2 1.1 %shard_map.192 = f32[128,1024]{1,0:T(8,128)} custom-call(f32[128,1024]{1,0:T(8,128)S(1)} %get-tuple-element.53.partial, bf16[128,512]{1,0:T(8,128)(2,1)S(1)} %collective-permute-done.12.peer, bf16[256,1024]{1,0:T(8,128)(2,1)S(1)} %collective-permute-done.13.w_near, bf16[256,1024]{1,0:T(8,128)(2,1)S(1)} %collective-permute-done.14.w_far), custom_call_target="tpu_custom_call" | custom-call | flops 134217728 | bytes 2097152 | tf_op jit(solution)/shard_map/pallas_call | solution.py:608
  (23 shorter events, 0.1 us)
Async XLA Ops:
  2.8 13.4 %copy-start.3 = (f32[64]{0:T(128)S(1)}, f32[64]{0:T(128)}, u32[]{:S(2)}) copy-start(f32[64]{0:T(128)} %param.22) | copy-start | bytes 772
  2.8 7.1 %collective-permute-start.1 = (bf16[128,256]{1,0:T(8,128)(2,1)S(1)}, bf16[128,256]{1,0:T(8,128)(2,1)S(1)}, u32[]{:S(2)}, u32[]{:S(2)}) collective-permute-start(bf16[128,256]{1,0:T(8,128)(2,1)S(1)} %get-tuple-element.32.refs_1_), channel_id=1, source_target_pairs={{0,4},{2,6},{4,0},{6,2},{8,12},{10,14},{12,8},{14,10},{16,20},{18,... | collective-permute-start | bytes 196616 | tf_op jit(solution)/shard_map/span_step_0/ppermute | solution.py:439
  5.8 5.5 %collective-permute-start = (bf16[128,256]{1,0:T(8,128)(2,1)S(1)}, bf16[128,256]{1,0:T(8,128)(2,1)S(1)}, u32[]{:S(2)}, u32[]{:S(2)}) collective-permute-start(bf16[128,256]{1,0:T(8,128)(2,1)S(1)} %get-tuple-element.31), channel_id=1, source_target_pairs={{0,16},{2,18},{4,20},{6,22},{8,24},{10,26},{12,28},{14,30},{16,0},... | collective-permute-start | bytes 196616 | tf_op jit(solution)/shard_map/prior_step_0/ppermute | solution.py:439
  8.4 13.3 %collective-permute-start.13 = (bf16[256,1024]{1,0:T(8,128)(2,1)S(1)}, bf16[256,1024]{1,0:T(8,128)(2,1)S(1)}, u32[]{:S(2)}, u32[]{:S(2)}) collective-permute-start(bf16[256,1024]{1,0:T(8,128)(2,1)S(1)} %get-tuple-element.54), channel_id=1, source_target_pairs={{0,1},{1,0},{2,3},{3,2},{4,5},{5,4},{6,7},{7,6},{8,9},{9,8},{10,11... | collective-permute-start | bytes 1572872 | tf_op jit(solution)/shard_map/weights_step/ppermute | solution.py:529
  9.9 8.3 %collective-permute-start.3 = (bf16[256,256]{1,0:T(8,128)(2,1)S(1)}, bf16[256,256]{1,0:T(8,128)(2,1)S(1)}, u32[]{:S(2)}, u32[]{:S(2)}) collective-permute-start(bf16[256,256]{1,0:T(8,128)(2,1)S(1)} %constant_dynamic-update-slice_fusion.2), channel_id=1, source_target_pairs={{0,16},{2,18},{4,20},{6,22},{8,24},{10,26},{12,28},{14,30},{16,0},... | collective-permute-start | bytes 393224 | tf_op jit(solution)/shard_map/span_step_1/ppermute | solution.py:439
  11.3 7.2 %collective-permute-start.2 = (bf16[256,256]{1,0:T(8,128)(2,1)S(1)}, bf16[256,256]{1,0:T(8,128)(2,1)S(1)}, u32[]{:S(2)}, u32[]{:S(2)}) collective-permute-start(bf16[256,256]{1,0:T(8,128)(2,1)S(1)} %constant_dynamic-update-slice_fusion), channel_id=1, source_target_pairs={{0,8},{2,10},{4,12},{6,14},{8,0},{10,2},{12,4},{14,6},{16,24},{18,... | collective-permute-start | bytes 393224 | tf_op jit(solution)/shard_map/prior_step_1/ppermute | solution.py:439
  18.5 6.7 %collective-permute-start.4 = (bf16[512,256]{1,0:T(8,128)(2,1)S(1)}, bf16[512,256]{1,0:T(8,128)(2,1)S(1)}, u32[]{:S(2)}, u32[]{:S(2)}) collective-permute-start(bf16[512,256]{1,0:T(8,128)(2,1)S(1)} %pad_maximum_fusion.refs_3_), channel_id=1, source_target_pairs={{0,4},{2,6},{4,0},{6,2},{8,12},{10,14},{12,8},{14,10},{16,20},{18,... | collective-permute-start | bytes 786440 | tf_op jit(solution)/shard_map/prior_last/ppermute | solution.py:439
  18.9 6.4 %collective-permute-start.5 = (bf16[512,256]{1,0:T(8,128)(2,1)S(1)}, bf16[512,256]{1,0:T(8,128)(2,1)S(1)}, u32[]{:S(2)}, u32[]{:S(2)}) collective-permute-start(bf16[512,256]{1,0:T(8,128)(2,1)S(1)} %pad_maximum_fusion.1.refs_4_.refs_0_), channel_id=1, source_target_pairs={{0,8},{2,10},{4,12},{6,14},{8,0},{10,2},{12,4},{14,6},{16,24},{18,... | collective-permute-start | bytes 786440 | tf_op jit(solution)/shard_map/span_last/ppermute | solution.py:439
  19.7 1.4 %collective-permute-start.8 = (bf16[256,256]{1,0:T(8,128)(2,1)S(1)}, bf16[256,256]{1,0:T(8,128)(2,1)S(1)}, u32[]{:S(2)}, u32[]{:S(2)}) collective-permute-start(bf16[256,256]{1,0:T(8,128)(2,1)S(1)} %get-tuple-element.58), channel_id=1, source_target_pairs={{0,2},{2,0},{4,6},{6,4},{8,10},{10,8},{12,14},{14,12},{16,18},{18,... | collective-permute-start | bytes 393224 | tf_op jit(solution)/shard_map/span_core_near/ppermute | solution.py:439
  19.8 1.5 %collective-permute-start.9 = (bf16[256,256]{1,0:T(8,128)(2,1)S(1)}, bf16[256,256]{1,0:T(8,128)(2,1)S(1)}, u32[]{:S(2)}, u32[]{:S(2)}) collective-permute-start(bf16[256,256]{1,0:T(8,128)(2,1)S(1)} %get-tuple-element.57), channel_id=1, source_target_pairs={{0,2},{2,0},{4,6},{6,4},{8,10},{10,8},{12,14},{14,12},{16,18},{18,... | collective-permute-start | bytes 393224 | tf_op jit(solution)/shard_map/span_core_near/ppermute | solution.py:439
  21.2 2.4 %collective-permute-start.6 = (bf16[256,256]{1,0:T(8,128)(2,1)S(1)}, bf16[256,256]{1,0:T(8,128)(2,1)S(1)}, u32[]{:S(2)}, u32[]{:S(2)}) collective-permute-start(bf16[256,256]{1,0:T(8,128)(2,1)S(1)} %get-tuple-element.60), channel_id=1, source_target_pairs={{0,2},{2,0},{4,6},{6,4},{8,10},{10,8},{12,14},{14,12},{16,18},{18,... | collective-permute-start | bytes 393224 | tf_op jit(solution)/shard_map/prior_core_near/ppermute | solution.py:439
  21.3 2.2 %collective-permute-start.7 = (bf16[256,256]{1,0:T(8,128)(2,1)S(1)}, bf16[256,256]{1,0:T(8,128)(2,1)S(1)}, u32[]{:S(2)}, u32[]{:S(2)}) collective-permute-start(bf16[256,256]{1,0:T(8,128)(2,1)S(1)} %get-tuple-element.59), channel_id=1, source_target_pairs={{0,2},{2,0},{4,6},{6,4},{8,10},{10,8},{12,14},{14,12},{16,18},{18,... | collective-permute-start | bytes 393224 | tf_op jit(solution)/shard_map/prior_core_near/ppermute | solution.py:439
  21.7 13.5 %collective-permute-start.14 = (bf16[256,1024]{1,0:T(8,128)(2,1)S(1)}, bf16[256,1024]{1,0:T(8,128)(2,1)S(1)}, u32[]{:S(2)}, u32[]{:S(2)}) collective-permute-start(bf16[256,1024]{1,0:T(8,128)(2,1)S(1)} %collective-permute-done.13.w_near), channel_id=1, source_target_pairs={{0,2},{2,0},{4,6},{6,4},{8,10},{10,8},{12,14},{14,12},{16,18},{18,... | collective-permute-start | bytes 1572872 | tf_op jit(solution)/shard_map/weights_step/ppermute | solution.py:439
  25.2 2.3 %collective-permute-start.10 = (bf16[512,256]{1,0:T(8,128)(2,1)S(1)}, bf16[512,256]{1,0:T(8,128)(2,1)S(1)}, u32[]{:S(2)}, u32[]{:S(2)}) collective-permute-start(bf16[512,256]{1,0:T(8,128)(2,1)S(1)} %collective-permute-done.4.refs_1_), channel_id=1, source_target_pairs={{0,2},{2,0},{4,6},{6,4},{8,10},{10,8},{12,14},{14,12},{16,18},{18,... | collective-permute-start | bytes 786440 | tf_op jit(solution)/shard_map/prior_core_far/ppermute | solution.py:439
  25.6 1.9 %collective-permute-start.11 = (bf16[512,256]{1,0:T(8,128)(2,1)S(1)}, bf16[512,256]{1,0:T(8,128)(2,1)S(1)}, u32[]{:S(2)}, u32[]{:S(2)}) collective-permute-start(bf16[512,256]{1,0:T(8,128)(2,1)S(1)} %collective-permute-done.5.refs_2_.refs_1_), channel_id=1, source_target_pairs={{0,2},{2,0},{4,6},{6,4},{8,10},{10,8},{12,14},{14,12},{16,18},{18,... | collective-permute-start | bytes 786440 | tf_op jit(solution)/shard_map/span_core_far/ppermute | solution.py:439
  27.5 3.5 %copy-start = (s32[32]{0:T(128)S(1)}, s32[32]{0:T(128)}, u32[]{:S(2)}) copy-start(s32[32]{0:T(128)} %order.5) | copy-start | bytes 388
  27.5 3.5 %copy-start.1 = (s32[16]{0:T(128)S(1)}, s32[16]{0:T(128)}, u32[]{:S(2)}) copy-start(s32[16]{0:T(128)} %dest.1) | copy-start | bytes 196
  27.5 3.5 %copy-start.2 = (s32[16]{0:T(128)S(1)}, s32[16]{0:T(128)}, u32[]{:S(2)}) copy-start(s32[16]{0:T(128)} %constant.8.clone.where) | copy-start | bytes 196
  29.4 5.8 %collective-permute-start.12 = (bf16[128,512]{1,0:T(8,128)(2,1)S(1)}, bf16[128,512]{1,0:T(8,128)(2,1)S(1)}, u32[]{:S(2)}, u32[]{:S(2)}) collective-permute-start(bf16[128,512]{1,0:T(8,128)(2,1)S(1)} %shard_map.190.mine), channel_id=1, source_target_pairs={{0,1},{1,0},{2,3},{3,2},{4,5},{5,4},{6,7},{7,6},{8,9},{9,8},{10,11... | collective-permute-start | bytes 393224 | tf_op jit(solution)/shard_map/ppermute | solution.py:590

commit v6 on v5

--- a/solution.py
+++ b/solution.py
@@ -308,7 +308,12 @@
     if not refs:
         rows = [chunk[...] for chunk in chunks]
         starts = range(0, len(rows), join)
-        pieces = [piece(jnp.concatenate(rows[i : i + join], axis=0), offsets[i]) for i in starts]
+        pieces = []
+        for i in starts:
+            joined = jnp.concatenate(rows[i : i + join], axis=0)
+            halves = offsets[i] if isinstance(offsets[i], tuple) else (offsets[i],)
+            size = joined.shape[0] // len(halves)
+            pieces += [piece(joined[h * size : (h + 1) * size, :], at) for h, at in enumerate(halves)]
         fold(
             q, m_in, acc_in, m_ref, acc_ref, pieces + extra, blocks, part, finish if last else None
         )
@@ -320,16 +325,19 @@
         m_ref[...] = m_in[...]
         acc_ref[...] = acc_in[...]
     for chunk, at in zip(chunks, offsets):
-
-        def visit(c, chunk=chunk, at=at):
-            first_row = pl.multiple_of(c * step, step)
-            copy = pltpu.make_async_copy(chunk.at[pl.ds(first_row, step)], held, sem)
-            copy.start()
-            copy.wait()
-            pieces = [piece(held[...], None if at is None else at + first_row)]
-            fold(q, m_ref, acc_ref, m_ref, acc_ref, pieces, blocks, part)
-
-        pl.loop(0, chunk.shape[0] // step)(visit)
+        halves = at if isinstance(at, tuple) else (at,)
+        size = chunk.shape[0] // len(halves)
+        for i, half in enumerate(halves):
+
+            def visit(c, chunk=chunk, half=half, start=i * size):
+                row = pl.multiple_of(c * step, step)
+                copy = pltpu.make_async_copy(chunk.at[pl.ds(start + row, step)], held, sem)
+                copy.start()
+                copy.wait()
+                pieces = [piece(held[...], None if half is None else half + row)]
+                fold(q, m_ref, acc_ref, m_ref, acc_ref, pieces, blocks, part)
+
+            pl.loop(0, size // step)(visit)
     if last:
         tiles = [acc_ref[t * part : (t + 1) * part, :] for t in range(2 * blocks)]
         for b in range(blocks):
@@ -340,7 +348,7 @@
     arrays, offsets = zip(*chunks)
     rows = sum(c.shape[0] for c in arrays)
     direct = rows <= 2048
-    step = min(1024, *(c.shape[0] for c in arrays))
+    step = min([1024] + [c.shape[0] // 2 for c in arrays])
     first = state is None
     operands = [q, *(own or ()), *arrays, bias, *(state or ())]
     specs = [spec(VMEM)] * len(operands)
@@ -393,11 +401,11 @@
         row = slot * PAGE + (source % 2) * BLOCK
         at = 0
         for chunk in chunks:
-            size = chunk.shape[0]
+            size = min(chunk.shape[0], chunks[0].shape[0])
             inside = (row >= at) & (row < at + size)
 
             @pl.when(inside)
-            def _(chunk=chunk, at=at):
+            def _(chunk=chunk, at=at - (chunk.shape[0] - size)):
                 rows = pl.ds(pl.multiple_of(row - at, BLOCK), BLOCK)
                 to = pl.ds(half * BLOCK, BLOCK)
                 a = pltpu.make_async_copy(chunk.at[rows, :128], keys.at[0, to], sems.at[0])
@@ -579,17 +587,15 @@
     chunks += [(c, 2 * part + i * half) for i, c in enumerate(span_core)]
     state = attention(q, None, chunks, state=state, last=False, join=2, **common)
     prior_far, span_far, *state = lax.optimization_barrier((prior_far, span_far, *state))
-    with jax.named_scope("prior_core_far"):
-        prior_core_far = swap(prior_far, n, 1)
-    with jax.named_scope("span_core_far"):
-        span_core_far = swap(span_far, n, 1)
+    with jax.named_scope("core_far"):
+        far_core = swap(jnp.concatenate([prior_far, span_far], axis=0), n, 1)
     chunks = [(prior_far, None), (span_far, part)]
     state = attention(q, None, chunks, state=state, last=False, **common)
-    chunks = [(prior_core_far, None), (span_core_far, 3 * part)]
+    chunks = [(far_core, (None, 3 * part))]
     heads = attention(q, None, chunks, state=state, last=True, **common)
     peer = lax.ppermute(heads, "head", [(0, 1), (1, 0)])
 
-    all_span = [span, span_far, *span_core, span_core_far]
+    all_span = [span, span_far, *span_core, far_core]
     new_keys, new_values, partial = pl.pallas_call(
         functools.partial(pages_kernel, len(all_span)),
         out_shape=[jax.ShapeDtypeStruct((1, PAGE, 128), BF16)] * 2

time: 36.8 us -> 36.5 us (level)
  starting transfers between devices: 16.2 us -> 15.8 us
    ppermute x13 -> x12, waiting for transfers between devices: 2.37 us -> 2.55 us  [swap(): return lax.ppermute(x, 'seq', [(i, i ^ step) for i in range(n)])]
    ppermute x13 -> x12, starting transfers between devices: 13.2 us -> 13 us  [swap(): return lax.ppermute(x, 'seq', [(i, i ^ step) for i in range(n)])]
  transfers between devices with their start and end apart: 15 -> 14, of which waited for: 5 -> 6; matrix products, arithmetic and copies ran while one was open for 0% -> 0% of each run, Pallas kernels for 33% -> 33%
where the time goes in v6:
time: 36.5 us; the launch traced here: 36.1 us
  starting transfers between devices  15.8 us (43%)
  Pallas kernels  15.1 us (41%)
  waiting for transfers between devices  4.17 us (11%)
  between operations  0.84 us (2%)
    ppermute x12, starting transfers between devices, swap(): return lax.ppermute(x, 'seq', [(i, i ^ step) for i in range(n)])  13 us
    pallas_call x4, Pallas kernels, attention(): pl.pallas_call(functools.partial(attention_kernel, offsets, join, own is...  6.84 us
    pallas_call x1, Pallas kernels, body(): pl.pallas_call(functools.partial(pages_kernel, len(all_span)), out_shape=...  2.56 us
    ppermute x12, waiting for transfers between devices, swap(): return lax.ppermute(x, 'seq', [(i, i ^ step) for i in range(n)])  2.55 us
    pallas_call x1, Pallas kernels, body(): pl.pallas_call(functools.partial(kv_kernel, prior_len), out_shape=[jax.Sh...  2.14 us
    pallas_call x1, Pallas kernels, body(): pl.pallas_call(functools.partial(mask_kernel, blocks), out_shape=[jax.Sha...  1.63 us
    ppermute x1, waiting for transfers between devices, body(): peer = lax.ppermute(heads, 'head', [(0, 1), (1, 0)])  1.61 us
    ppermute x1, starting transfers between devices, body(): w_near = lax.ppermute(w_send, 'head', [(0, 1), (1, 0)])  1.49 us
  transfers between devices with their start and end apart: 14, of which 6 were waited for; matrix products, arithmetic and copies ran while one was open for 0% of the time, Pallas kernels for 33%

profile of v6, /device:TPU:0, one launch (start us, length us, event | category | flops | bytes accessed | tf_op | source)
XLA Modules:
  0.0 36.1 jit_solution(6431494934473417852)
XLA Ops:
  0.6 2.1 %shard_map.184 = (bf16[128,256]{1,0:T(8,128)(2,1)S(1)}, bf16[128,256]{1,0:T(8,128)(2,1)S(1)}, bf16[128,2048]{1,0:T(8,128)(2,1)S(1)}, f32[128,128]{1,0:T(8,128)S(...) custom-call(s32[32]{0:T(128)} %order.5, s32[16]{0:T(128)} %table.1, bf16[128,2048]{1,0:T(8,128)(2,1)} %hidden.1, ...), custom_call_target="tpu_custom_call" | custom-call | flops 134217728 | bytes 3145728 | tf_op jit(solution)/shard_map/pallas_call | solution.py:489
  2.8 3.0 %collective-permute-start.1 = (bf16[128,256]{1,0:T(8,128)(2,1)S(1)}, bf16[128,256]{1,0:T(8,128)(2,1)S(1)}, u32[]{:S(2)}, u32[]{:S(2)}) collective-permute-start(bf16[128,256]{1,0:T(8,128)(2,1)S(1)} %get-tuple-element.32.refs_1_), channel_id=1, source_target_pairs={{0,4},{2,6},{4,0},{6,2},{8,12},{10,14},{12,8},{14,10},{16,20},{18,... | collective-permute-start | bytes 196616 | tf_op jit(solution)/shard_map/span_step_0/ppermute | solution.py:447
  5.8 2.6 %collective-permute-start = (bf16[128,256]{1,0:T(8,128)(2,1)S(1)}, bf16[128,256]{1,0:T(8,128)(2,1)S(1)}, u32[]{:S(2)}, u32[]{:S(2)}) collective-permute-start(bf16[128,256]{1,0:T(8,128)(2,1)S(1)} %get-tuple-element.31), channel_id=1, source_target_pairs={{0,16},{2,18},{4,20},{6,22},{8,24},{10,26},{12,28},{14,30},{16,0},... | collective-permute-start | bytes 196616 | tf_op jit(solution)/shard_map/prior_step_0/ppermute | solution.py:447
  8.4 1.5 %collective-permute-start.12 = (bf16[256,1024]{1,0:T(8,128)(2,1)S(1)}, bf16[256,1024]{1,0:T(8,128)(2,1)S(1)}, u32[]{:S(2)}, u32[]{:S(2)}) collective-permute-start(bf16[256,1024]{1,0:T(8,128)(2,1)S(1)} %get-tuple-element.54), channel_id=1, source_target_pairs={{0,1},{1,0},{2,3},{3,2},{4,5},{5,4},{6,7},{7,6},{8,9},{9,8},{10,11... | collective-permute-start | bytes 1572872 | tf_op jit(solution)/shard_map/weights_step/ppermute | solution.py:537
  9.9 1.2 %collective-permute-start.3 = (bf16[256,256]{1,0:T(8,128)(2,1)S(1)}, bf16[256,256]{1,0:T(8,128)(2,1)S(1)}, u32[]{:S(2)}, u32[]{:S(2)}) collective-permute-start(bf16[256,256]{1,0:T(8,128)(2,1)S(1)} %constant_dynamic-update-slice_fusion.2), channel_id=1, source_target_pairs={{0,16},{2,18},{4,20},{6,22},{8,24},{10,26},{12,28},{14,30},{16,0},... | collective-permute-start | bytes 393224 | tf_op jit(solution)/shard_map/span_step_1/ppermute | solution.py:447
  11.2 0.1 collective-permute-done
  11.3 3.3 %collective-permute-start.2 = (bf16[256,256]{1,0:T(8,128)(2,1)S(1)}, bf16[256,256]{1,0:T(8,128)(2,1)S(1)}, u32[]{:S(2)}, u32[]{:S(2)}) collective-permute-start(bf16[256,256]{1,0:T(8,128)(2,1)S(1)} %constant_dynamic-update-slice_fusion), channel_id=1, source_target_pairs={{0,8},{2,10},{4,12},{6,14},{8,0},{10,2},{12,4},{14,6},{16,24},{18,... | collective-permute-start | bytes 393224 | tf_op jit(solution)/shard_map/prior_step_1/ppermute | solution.py:447
  14.6 1.6 %shard_map.185 = (f32[128,128]{1,0:T(8,128)S(1)}, f32[2,2048]{1,0:T(2,128)S(1)}, bf16[2048,512]{1,0:T(8,128)(2,1)S(1)}) custom-call(s32[32]{0:T(128)} %order.5, s32[32]{0:T(128)} %live.1, s32[16]{0:T(128)} %constant.7.clone.masks, bf16[2048,512]{1,0:T(8,128)(2,1)} %w_query.1, bf16[128,2048]{1,0:T(8,128)(2,1)S(1)} %get-tuple-element.33.turn.normed), custom_call_target="tpu_custom_call" | custom-call | flops 268435456 | bytes 1048576 | tf_op jit(solution)/shard_map/pallas_call | solution.py:539
  16.2 0.8 %shard_map.186.refs_0_ = bf16[1024,256]{1,0:T(8,128)(2,1)S(1)} custom-call(bf16[128,2048]{1,0:T(8,128)(2,1)S(1)} %get-tuple-element.33.turn.normed, f32[128,128]{1,0:T(8,128)S(1)} %get-tuple-element.34.cosine, f32[128,128]{1,0:T(8,128)S(1)} %get-tuple-element.35.sine, bf16[2048,512]{1,0:T(8,128)(2,1)S(1)} %get-tuple-element.36.w_query, f32[1,64]{1,0:T(1,128)S(1)} %bitcast.3), custom_call_target="tpu_custom_call" | custom-call | flops 268435456 | bytes 4194304 | tf_op jit(solution)/shard_map/pallas_call | solution.py:557
  17.1 1.2 %collective-permute-done.3 = bf16[256,256]{1,0:T(8,128)(2,1)S(1)} collective-permute-done((bf16[256,256]{1,0:T(8,128)(2,1)S(1)}, bf16[256,256]{1,0:T(8,128)(2,1)S(1)}, u32[]{:S(2)}, u32[]{:S(2)}) %collective-permute-start.3) | collective-permute-done | bytes 131104 | tf_op jit(solution)/shard_map/span_step_1/ppermute | solution.py:447
  18.3 0.2 collective-permute-done.2
  18.5 0.4 %collective-permute-start.4 = (bf16[512,256]{1,0:T(8,128)(2,1)S(1)}, bf16[512,256]{1,0:T(8,128)(2,1)S(1)}, u32[]{:S(2)}, u32[]{:S(2)}) collective-permute-start(bf16[512,256]{1,0:T(8,128)(2,1)S(1)} %pad_maximum_fusion.1.refs_3_), channel_id=1, source_target_pairs={{0,4},{2,6},{4,0},{6,2},{8,12},{10,14},{12,8},{14,10},{16,20},{18,... | collective-permute-start | bytes 786440 | tf_op jit(solution)/shard_map/prior_last/ppermute | solution.py:447
  18.9 0.9 %collective-permute-start.5 = (bf16[512,256]{1,0:T(8,128)(2,1)S(1)}, bf16[512,256]{1,0:T(8,128)(2,1)S(1)}, u32[]{:S(2)}, u32[]{:S(2)}) collective-permute-start(bf16[512,256]{1,0:T(8,128)(2,1)S(1)} %pad_maximum_fusion.2.refs_4_.refs_0_), channel_id=1, source_target_pairs={{0,8},{2,10},{4,12},{6,14},{8,0},{10,2},{12,4},{14,6},{16,24},{18,... | collective-permute-start | bytes 786440 | tf_op jit(solution)/shard_map/span_last/ppermute | solution.py:447
  19.7 0.1 collective-permute-start.8
  19.8 0.5 %collective-permute-start.9 = (bf16[256,256]{1,0:T(8,128)(2,1)S(1)}, bf16[256,256]{1,0:T(8,128)(2,1)S(1)}, u32[]{:S(2)}, u32[]{:S(2)}) collective-permute-start(bf16[256,256]{1,0:T(8,128)(2,1)S(1)} %get-tuple-element.57), channel_id=1, source_target_pairs={{0,2},{2,0},{4,6},{6,4},{8,10},{10,8},{12,14},{14,12},{16,18},{18,... | collective-permute-start | bytes 393224 | tf_op jit(solution)/shard_map/span_core_near/ppermute | solution.py:447
  20.3 0.8 %collective-permute-done.8.refs_3_.refs_2_ = bf16[256,256]{1,0:T(8,128)(2,1)S(1)} collective-permute-done((bf16[256,256]{1,0:T(8,128)(2,1)S(1)}, bf16[256,256]{1,0:T(8,128)(2,1)S(1)}, u32[]{:S(2)}, u32[]{:S(2)}) %collective-permute-start.8) | collective-permute-done | bytes 131104 | tf_op jit(solution)/shard_map/span_core_near/ppermute | solution.py:447
  21.2 0.1 collective-permute-start.6
  21.3 0.0 collective-permute-done.9.refs_4_.refs_3_
  21.3 0.3 collective-permute-start.7
  21.7 1.6 %shard_map.187 = (f32[1024,128]{1,0:T(8,128)S(1)}, f32[1024,128]{1,0:T(8,128)S(1)}) custom-call(bf16[1024,256]{1,0:T(8,128)(2,1)S(1)} %shard_map.186.refs_0_, bf16[128,256]{1,0:T(8,128)(2,1)S(1)} %get-tuple-element.32.refs_1_, f32[128,128]{1,0:T(8,128)S(1)} %get-tuple-element.39.refs_2_, bf16[512,256]{1,0:T(8,128)(2,1)S(1)} %pad_maximum_fusion.1.refs_3_, ...), custom_call_target="tpu_custom_call" | custom-call | flops 1000 | bytes 1000 | tf_op jit(solution)/shard_map/pallas_call | solution.py:369
  23.3 1.7 %shard_map.188 = (f32[1024,128]{1,0:T(8,128)S(1)}, f32[1024,128]{1,0:T(8,128)S(1)}) custom-call(bf16[1024,256]{1,0:T(8,128)(2,1)S(1)} %shard_map.186.refs_0_, bf16[256,256]{1,0:T(8,128)(2,1)S(1)} %collective-permute-done.6.refs_1_, bf16[256,256]{1,0:T(8,128)(2,1)S(1)} %collective-permute-done.7.refs_2_, ...), custom_call_target="tpu_custom_call" | custom-call | flops 1000 | bytes 1000 | tf_op jit(solution)/shard_map/pallas_call | solution.py:369
  25.0 0.2 collective-permute-done.5.refs_2_.refs_1_
  25.3 0.1 collective-permute-start.10
  25.4 0.5 %collective-permute-start.13 = (bf16[256,1024]{1,0:T(8,128)(2,1)S(1)}, bf16[256,1024]{1,0:T(8,128)(2,1)S(1)}, u32[]{:S(2)}, u32[]{:S(2)}) collective-permute-start(bf16[256,1024]{1,0:T(8,128)(2,1)S(1)} %collective-permute-done.12.w_near), channel_id=1, source_target_pairs={{0,2},{2,0},{4,6},{6,4},{8,10},{10,8},{12,14},{14,12},{16,18},{18,... | collective-permute-start | bytes 1572872 | tf_op jit(solution)/shard_map/weights_step/ppermute | solution.py:447
  25.8 1.7 %shard_map.189 = (f32[1024,128]{1,0:T(8,128)S(1)}, f32[1024,128]{1,0:T(8,128)S(1)}) custom-call(bf16[1024,256]{1,0:T(8,128)(2,1)S(1)} %shard_map.186.refs_0_, bf16[512,256]{1,0:T(8,128)(2,1)S(1)} %collective-permute-done.4.refs_1_, bf16[512,256]{1,0:T(8,128)(2,1)S(1)} %collective-permute-done.5.refs_2_.refs_1_, ...), custom_call_target="tpu_custom_call" | custom-call | flops 1073741824 | bytes 2621440 | tf_op jit(solution)/shard_map/pallas_call | solution.py:369
  27.5 0.0 copy-start
  27.5 0.0 copy-start.2
  27.6 1.9 %shard_map.190.mine = bf16[128,512]{1,0:T(8,128)(2,1)S(1)} custom-call(bf16[1024,256]{1,0:T(8,128)(2,1)S(1)} %shard_map.186.refs_0_, bf16[1024,256]{1,0:T(8,128)(2,1)S(1)} %collective-permute-done.10.refs_1_.refs_4_, f32[2,2048]{1,0:T(2,128)S(1)} %get-tuple-element.42.refs_5_.refs_3_.refs_2_, f32[1024,128]{1,0:T(8,128)S(1)} %get-tuple-element.51.refs_3_, ...), custom_call_target="tpu_custom_call" | custom-call | flops 1073741824 | bytes 2621440 | tf_op jit(solution)/shard_map/pallas_call | solution.py:369
  29.4 1.4 %collective-permute-start.11 = (bf16[128,512]{1,0:T(8,128)(2,1)S(1)}, bf16[128,512]{1,0:T(8,128)(2,1)S(1)}, u32[]{:S(2)}, u32[]{:S(2)}) collective-permute-start(bf16[128,512]{1,0:T(8,128)(2,1)S(1)} %shard_map.190.mine), channel_id=1, source_target_pairs={{0,1},{1,0},{2,3},{3,2},{4,5},{5,4},{6,7},{7,6},{8,9},{9,8},{10,11... | collective-permute-start | bytes 393224 | tf_op jit(solution)/shard_map/ppermute | solution.py:596
  30.8 2.6 %shard_map.191 = (bf16[1,128,128]{2,1,0:T(8,128)(2,1)}, bf16[1,128,128]{2,1,0:T(8,128)(2,1)}, f32[128,1024]{1,0:T(8,128)S(1)}) custom-call(s32[16]{0:T(128)S(1)} %copy-done.1, s32[32]{0:T(128)S(1)} %copy-done, s32[16]{0:T(128)S(1)} %copy-done.2, bf16[128,512]{1,0:T(8,128)(2,1)S(1)} %shard_map.190.mine, bf16[512,2048]{1,0:T(8,128)(2,1)} %w_output.3, ...), custom_call_target="tpu_custom_call" | custom-call | flops 134217728 | bytes 2097152 | tf_op jit(solution)/shard_map/pallas_call | solution.py:599
  33.4 1.6 %collective-permute-done.11.peer = bf16[128,512]{1,0:T(8,128)(2,1)S(1)} collective-permute-done((bf16[128,512]{1,0:T(8,128)(2,1)S(1)}, bf16[128,512]{1,0:T(8,128)(2,1)S(1)}, u32[]{:S(2)}, u32[]{:S(2)}) %collective-permute-start.11) | collective-permute-done | bytes 131104 | tf_op jit(solution)/shard_map/ppermute | solution.py:596
  35.0 1.1 %shard_map.192 = f32[128,1024]{1,0:T(8,128)} custom-call(f32[128,1024]{1,0:T(8,128)S(1)} %get-tuple-element.53.partial, bf16[128,512]{1,0:T(8,128)(2,1)S(1)} %collective-permute-done.11.peer, bf16[256,1024]{1,0:T(8,128)(2,1)S(1)} %collective-permute-done.12.w_near, bf16[256,1024]{1,0:T(8,128)(2,1)S(1)} %collective-permute-done.13.w_far), custom_call_target="tpu_custom_call" | custom-call | flops 134217728 | bytes 2097152 | tf_op jit(solution)/shard_map/pallas_call | solution.py:614
  (22 shorter events, 0.2 us)
Async XLA Ops:
  2.8 13.4 %copy-start.3 = (f32[64]{0:T(128)S(1)}, f32[64]{0:T(128)}, u32[]{:S(2)}) copy-start(f32[64]{0:T(128)} %param.22) | copy-start | bytes 772
  2.8 7.1 %collective-permute-start.1 = (bf16[128,256]{1,0:T(8,128)(2,1)S(1)}, bf16[128,256]{1,0:T(8,128)(2,1)S(1)}, u32[]{:S(2)}, u32[]{:S(2)}) collective-permute-start(bf16[128,256]{1,0:T(8,128)(2,1)S(1)} %get-tuple-element.32.refs_1_), channel_id=1, source_target_pairs={{0,4},{2,6},{4,0},{6,2},{8,12},{10,14},{12,8},{14,10},{16,20},{18,... | collective-permute-start | bytes 196616 | tf_op jit(solution)/shard_map/span_step_0/ppermute | solution.py:447
  5.8 5.5 %collective-permute-start = (bf16[128,256]{1,0:T(8,128)(2,1)S(1)}, bf16[128,256]{1,0:T(8,128)(2,1)S(1)}, u32[]{:S(2)}, u32[]{:S(2)}) collective-permute-start(bf16[128,256]{1,0:T(8,128)(2,1)S(1)} %get-tuple-element.31), channel_id=1, source_target_pairs={{0,16},{2,18},{4,20},{6,22},{8,24},{10,26},{12,28},{14,30},{16,0},... | collective-permute-start | bytes 196616 | tf_op jit(solution)/shard_map/prior_step_0/ppermute | solution.py:447
  8.4 16.9 %collective-permute-start.12 = (bf16[256,1024]{1,0:T(8,128)(2,1)S(1)}, bf16[256,1024]{1,0:T(8,128)(2,1)S(1)}, u32[]{:S(2)}, u32[]{:S(2)}) collective-permute-start(bf16[256,1024]{1,0:T(8,128)(2,1)S(1)} %get-tuple-element.54), channel_id=1, source_target_pairs={{0,1},{1,0},{2,3},{3,2},{4,5},{5,4},{6,7},{7,6},{8,9},{9,8},{10,11... | collective-permute-start | bytes 1572872 | tf_op jit(solution)/shard_map/weights_step/ppermute | solution.py:537
  9.9 8.3 %collective-permute-start.3 = (bf16[256,256]{1,0:T(8,128)(2,1)S(1)}, bf16[256,256]{1,0:T(8,128)(2,1)S(1)}, u32[]{:S(2)}, u32[]{:S(2)}) collective-permute-start(bf16[256,256]{1,0:T(8,128)(2,1)S(1)} %constant_dynamic-update-slice_fusion.2), channel_id=1, source_target_pairs={{0,16},{2,18},{4,20},{6,22},{8,24},{10,26},{12,28},{14,30},{16,0},... | collective-permute-start | bytes 393224 | tf_op jit(solution)/shard_map/span_step_1/ppermute | solution.py:447
  11.3 7.2 %collective-permute-start.2 = (bf16[256,256]{1,0:T(8,128)(2,1)S(1)}, bf16[256,256]{1,0:T(8,128)(2,1)S(1)}, u32[]{:S(2)}, u32[]{:S(2)}) collective-permute-start(bf16[256,256]{1,0:T(8,128)(2,1)S(1)} %constant_dynamic-update-slice_fusion), channel_id=1, source_target_pairs={{0,8},{2,10},{4,12},{6,14},{8,0},{10,2},{12,4},{14,6},{16,24},{18,... | collective-permute-start | bytes 393224 | tf_op jit(solution)/shard_map/prior_step_1/ppermute | solution.py:447
  18.5 6.5 %collective-permute-start.4 = (bf16[512,256]{1,0:T(8,128)(2,1)S(1)}, bf16[512,256]{1,0:T(8,128)(2,1)S(1)}, u32[]{:S(2)}, u32[]{:S(2)}) collective-permute-start(bf16[512,256]{1,0:T(8,128)(2,1)S(1)} %pad_maximum_fusion.1.refs_3_), channel_id=1, source_target_pairs={{0,4},{2,6},{4,0},{6,2},{8,12},{10,14},{12,8},{14,10},{16,20},{18,... | collective-permute-start | bytes 786440 | tf_op jit(solution)/shard_map/prior_last/ppermute | solution.py:447
  18.9 6.4 %collective-permute-start.5 = (bf16[512,256]{1,0:T(8,128)(2,1)S(1)}, bf16[512,256]{1,0:T(8,128)(2,1)S(1)}, u32[]{:S(2)}, u32[]{:S(2)}) collective-permute-start(bf16[512,256]{1,0:T(8,128)(2,1)S(1)} %pad_maximum_fusion.2.refs_4_.refs_0_), channel_id=1, source_target_pairs={{0,8},{2,10},{4,12},{6,14},{8,0},{10,2},{12,4},{14,6},{16,24},{18,... | collective-permute-start | bytes 786440 | tf_op jit(solution)/shard_map/span_last/ppermute | solution.py:447
  19.7 1.4 %collective-permute-start.8 = (bf16[256,256]{1,0:T(8,128)(2,1)S(1)}, bf16[256,256]{1,0:T(8,128)(2,1)S(1)}, u32[]{:S(2)}, u32[]{:S(2)}) collective-permute-start(bf16[256,256]{1,0:T(8,128)(2,1)S(1)} %get-tuple-element.58), channel_id=1, source_target_pairs={{0,2},{2,0},{4,6},{6,4},{8,10},{10,8},{12,14},{14,12},{16,18},{18,... | collective-permute-start | bytes 393224 | tf_op jit(solution)/shard_map/span_core_near/ppermute | solution.py:447
  19.8 1.5 %collective-permute-start.9 = (bf16[256,256]{1,0:T(8,128)(2,1)S(1)}, bf16[256,256]{1,0:T(8,128)(2,1)S(1)}, u32[]{:S(2)}, u32[]{:S(2)}) collective-permute-start(bf16[256,256]{1,0:T(8,128)(2,1)S(1)} %get-tuple-element.57), channel_id=1, source_target_pairs={{0,2},{2,0},{4,6},{6,4},{8,10},{10,8},{12,14},{14,12},{16,18},{18,... | collective-permute-start | bytes 393224 | tf_op jit(solution)/shard_map/span_core_near/ppermute | solution.py:447
  21.2 2.2 %collective-permute-start.6 = (bf16[256,256]{1,0:T(8,128)(2,1)S(1)}, bf16[256,256]{1,0:T(8,128)(2,1)S(1)}, u32[]{:S(2)}, u32[]{:S(2)}) collective-permute-start(bf16[256,256]{1,0:T(8,128)(2,1)S(1)} %get-tuple-element.60), channel_id=1, source_target_pairs={{0,2},{2,0},{4,6},{6,4},{8,10},{10,8},{12,14},{14,12},{16,18},{18,... | collective-permute-start | bytes 393224 | tf_op jit(solution)/shard_map/prior_core_near/ppermute | solution.py:447
  21.3 2.0 %collective-permute-start.7 = (bf16[256,256]{1,0:T(8,128)(2,1)S(1)}, bf16[256,256]{1,0:T(8,128)(2,1)S(1)}, u32[]{:S(2)}, u32[]{:S(2)}) collective-permute-start(bf16[256,256]{1,0:T(8,128)(2,1)S(1)} %get-tuple-element.59), channel_id=1, source_target_pairs={{0,2},{2,0},{4,6},{6,4},{8,10},{10,8},{12,14},{14,12},{16,18},{18,... | collective-permute-start | bytes 393224 | tf_op jit(solution)/shard_map/prior_core_near/ppermute | solution.py:447
  25.3 2.3 %collective-permute-start.10 = (bf16[1024,256]{1,0:T(8,128)(2,1)S(1)}, bf16[1024,256]{1,0:T(8,128)(2,1)S(1)}, u32[]{:S(2)}, u32[]{:S(2)}) collective-permute-start(bf16[1024,256]{1,0:T(8,128)(2,1)S(1)} %pad_maximum_fusion), channel_id=1, source_target_pairs={{0,2},{2,0},{4,6},{6,4},{8,10},{10,8},{12,14},{14,12},{16,18},{18,... | collective-permute-start | bytes 1572872 | tf_op jit(solution)/shard_map/core_far/ppermute | solution.py:447
  25.4 8.0 %collective-permute-start.13 = (bf16[256,1024]{1,0:T(8,128)(2,1)S(1)}, bf16[256,1024]{1,0:T(8,128)(2,1)S(1)}, u32[]{:S(2)}, u32[]{:S(2)}) collective-permute-start(bf16[256,1024]{1,0:T(8,128)(2,1)S(1)} %collective-permute-done.12.w_near), channel_id=1, source_target_pairs={{0,2},{2,0},{4,6},{6,4},{8,10},{10,8},{12,14},{14,12},{16,18},{18,... | collective-permute-start | bytes 1572872 | tf_op jit(solution)/shard_map/weights_step/ppermute | solution.py:447
  27.5 3.3 %copy-start = (s32[32]{0:T(128)S(1)}, s32[32]{0:T(128)}, u32[]{:S(2)}) copy-start(s32[32]{0:T(128)} %order.5) | copy-start | bytes 388
  27.5 3.3 %copy-start.1 = (s32[16]{0:T(128)S(1)}, s32[16]{0:T(128)}, u32[]{:S(2)}) copy-start(s32[16]{0:T(128)} %dest.1) | copy-start | bytes 196
  27.5 3.3 %copy-start.2 = (s32[16]{0:T(128)S(1)}, s32[16]{0:T(128)}, u32[]{:S(2)}) copy-start(s32[16]{0:T(128)} %constant.8.clone.where) | copy-start | bytes 196
  29.4 5.6 %collective-permute-start.11 = (bf16[128,512]{1,0:T(8,128)(2,1)S(1)}, bf16[128,512]{1,0:T(8,128)(2,1)S(1)}, u32[]{:S(2)}, u32[]{:S(2)}) collective-permute-start(bf16[128,512]{1,0:T(8,128)(2,1)S(1)} %shard_map.190.mine), channel_id=1, source_target_pairs={{0,1},{1,0},{2,3},{3,2},{4,5},{5,4},{6,7},{7,6},{8,9},{9,8},{10,11... | collective-permute-start | bytes 393224 | tf_op jit(solution)/shard_map/ppermute | solution.py:596

commit v7 on v6

--- a/solution.py
+++ b/solution.py
@@ -134,18 +134,39 @@
     return pl.ds(pl.multiple_of(x * ref.shape[1], ref.shape[1]), ref.shape[1])
 
 
-def query_kernel(normed, cosine, sine, w_query, query_gain, q_out):
+def query_kernel(
+    normed, cosine, sine, w_query, query_gain, order, live, masks,
+    q_out, own_bias, span_bias, w_query_v, query_gain_v, order_s, live_s, masks_s, sems, tile_sems,
+):
+    bring = []
+    for t in range(w_query.shape[1] // 256):
+        at = slice(t * 256, (t + 1) * 256)
+        bring.append(
+            pltpu.make_async_copy(w_query.at[:, at], w_query_v.at[:, at], tile_sems.at[t])
+        )
+    pairs = [(order, order_s), (live, live_s), (masks, masks_s), (query_gain, query_gain_v)]
+    copies = [pltpu.make_async_copy(a, b, sems.at[i]) for i, (a, b) in enumerate(pairs)]
+    for copy in copies + bring:
+        copy.start()
+    for copy in copies:
+        copy.wait()
+    fill_masks(normed.shape[0] // BLOCK, order_s, live_s, masks_s, own_bias, span_bias)
     rows = normed.shape[0]
     blocks = rows // BLOCK
     tiles = w_query.shape[1] // 128
     per_kv = tiles // 2
     group = 2 * per_kv
-    queries = jnp.dot(normed[...], w_query[...], preferred_element_type=F32)
-    gain = twice(query_gain)
+    gain = twice(query_gain_v)
     left = lanes_of((rows, 128)) < 64
     for t in range(tiles):
         kv_head, u = divmod(t, per_kv)
-        x = norm_and_rotate(queries[:, t * 128 : (t + 1) * 128], gain, cosine[...], sine[...])
+        if t % 2 == 0:
+            bring[t // 2].wait()
+            two = jnp.dot(
+                normed[...], w_query_v[:, t * 128 : (t + 2) * 128], preferred_element_type=F32
+            )
+        x = two[:, t % 2 * 128 : (t % 2 + 1) * 128]
+        x = norm_and_rotate(x, gain, cosine[...], sine[...])
         x = x * (64**-0.5 * LOG2E)
         turned = pltpu.roll(x, 64, 1)
         pair = (x, turned) if kv_head == 0 else (turned, x)
@@ -159,18 +180,7 @@
                 q_out[at : at + BLOCK, :] = both[b * BLOCK : (b + 1) * BLOCK, :]
 
 
-def mask_kernel(
-    blocks, order, live, masks, w_query, turn,
-    own_bias, span_bias, w_query_out, order_s, live_s, masks_s, sems,
-):
-    pairs = [(order, order_s), (live, live_s), (masks, masks_s)]
-    bring = pltpu.make_async_copy(w_query, w_query_out, sems.at[3])
-    bring.start()
-    copies = [pltpu.make_async_copy(a, b, sems.at[i]) for i, (a, b) in enumerate(pairs)]
-    for copy in copies:
-        copy.start()
-    for copy in copies:
-        copy.wait()
+def fill_masks(blocks, order_s, live_s, masks_s, own_bias, span_bias):
     me = lax.axis_index("seq")
     logical = [order_s[me * blocks + b] for b in range(blocks)]
     key_at = lanes_of((BLOCK, blocks * BLOCK))
@@ -187,7 +197,7 @@
             bias = jnp.where(here, jnp.where(alive, 0.0, MASKED), bias)
         own_bias[b * BLOCK : (b + 1) * BLOCK, :] = bias
 
-    count = masks.shape[0]
+    count = masks_s.shape[0]
     lane = lanes_of((1, PAGE))
 
     def visit(i, carry):
@@ -203,7 +213,6 @@
         return carry
 
     lax.fori_loop(0, count, visit, 0, unroll=count <= 16)
-    bring.wait()
 
 
 class Piece:
@@ -536,32 +545,32 @@
     with jax.named_scope("weights_step"):
         w_near = lax.ppermute(w_send, "head", [(0, 1), (1, 0)])
         w_far = swap(w_near, n, 1)
-    own_bias, span_bias, w_query = pl.pallas_call(
-        functools.partial(mask_kernel, blocks),
+    q, own_bias, span_bias = pl.pallas_call(
+        query_kernel,
         out_shape=[
+            jax.ShapeDtypeStruct((2 * blocks * group * BLOCK, 256), BF16),
             jax.ShapeDtypeStruct((rows, rows), F32),
             jax.ShapeDtypeStruct((blocks, n * PAGE), F32),
-            jax.ShapeDtypeStruct(w_query.shape, BF16),
         ],
-        in_specs=[spec(pltpu.HBM)] * 4 + [spec(pl.ANY)],
+        in_specs=[spec(VMEM)] * 3 + [spec(pltpu.HBM)] * 5,
         out_specs=[spec(VMEM)] * 3,
         scratch_shapes=[
+            VMEM(w_query.shape, BF16),
+            VMEM((1, head_dim), F32),
             SMEM(span_order.shape, jnp.int32),
             SMEM(key_live.shape, jnp.int32),
             SMEM((masks.size,), jnp.int32),
             pltpu.SemaphoreType.DMA((4,)),
+            pltpu.SemaphoreType.DMA((w_query.shape[1] // 256,)),
         ],
         compiler_params=params(),
-        cost_estimate=cost(1 << 28, 1 << 20),
-    )(*in_hbm(span_order, key_live, jnp.asarray(masks), w_query), normed)
-    q = pl.pallas_call(
-        query_kernel,
-        out_shape=jax.ShapeDtypeStruct((2 * blocks * group * BLOCK, 256), BF16),
-        in_specs=[spec(VMEM)] * 5,
-        out_specs=spec(VMEM),
-        compiler_params=params(),
         cost_estimate=cost(2 * rows * width * 512, 4 << 20),
-    )(normed, cosine, sine, w_query, query_gain.reshape(1, -1))
+    )(
+        normed,
+        cosine,
+        sine,
+        *in_hbm(w_query, query_gain.reshape(1, -1), span_order, key_live, jnp.asarray(masks)),
+    )
     for i, step in enumerate(steps[1:-1], 1):
         with jax.named_scope(f"prior_step_{i}"):
             prior = grow(prior, n, step)

time: 36.5 us -> 36.5 us (level)
    pallas_call x2 -> x1, Pallas kernels: 2.47 us -> 2.66 us  [body(): pl.pallas_call(query_kernel, out_shape=[jax.ShapeDtypeStruct((2 * blocks...]
where the time goes in v7:
time: 36.5 us; the launch traced here: 36.1 us
  starting transfers between devices  15.9 us (44%)
  Pallas kernels  15.3 us (42%)
  waiting for transfers between devices  3.92 us (11%)
  between operations  0.8 us (2%)
    ppermute x12, starting transfers between devices, swap(): return lax.ppermute(x, 'seq', [(i, i ^ step) for i in range(n)])  13 us
    pallas_call x4, Pallas kernels, attention(): pl.pallas_call(functools.partial(attention_kernel, offsets, join, own is...  6.87 us
    pallas_call x1, Pallas kernels, body(): pl.pallas_call(query_kernel, out_shape=[jax.ShapeDtypeStruct((2 * blocks...  2.66 us
    pallas_call x1, Pallas kernels, body(): pl.pallas_call(functools.partial(pages_kernel, len(all_span)), out_shape=...  2.56 us
    ppermute x12, waiting for transfers between devices, swap(): return lax.ppermute(x, 'seq', [(i, i ^ step) for i in range(n)])  2.34 us
    pallas_call x1, Pallas kernels, body(): pl.pallas_call(functools.partial(kv_kernel, prior_len), out_shape=[jax.Sh...  2.14 us
    ppermute x1, waiting for transfers between devices, body(): peer = lax.ppermute(heads, 'head', [(0, 1), (1, 0)])  1.58 us
    ppermute x1, starting transfers between devices, body(): w_near = lax.ppermute(w_send, 'head', [(0, 1), (1, 0)])  1.49 us
  transfers between devices with their start and end apart: 14, of which 6 were waited for; matrix products, arithmetic and copies ran while one was open for 0% of the time, Pallas kernels for 33%

profile of v7, /device:TPU:0, one launch (start us, length us, event | category | flops | bytes accessed | tf_op | source)
XLA Modules:
  0.0 36.1 jit_solution(3557256927861506035)
XLA Ops:
  0.6 2.1 %shard_map.184 = (bf16[128,256]{1,0:T(8,128)(2,1)S(1)}, bf16[128,256]{1,0:T(8,128)(2,1)S(1)}, bf16[128,2048]{1,0:T(8,128)(2,1)S(1)}, f32[128,128]{1,0:T(8,128)S(...) custom-call(s32[32]{0:T(128)} %order.5, s32[16]{0:T(128)} %table.1, bf16[128,2048]{1,0:T(8,128)(2,1)} %hidden.1, ...), custom_call_target="tpu_custom_call" | custom-call | flops 134217728 | bytes 3145728 | tf_op jit(solution)/shard_map/pallas_call | solution.py:498
  2.8 3.0 %collective-permute-start.1 = (bf16[128,256]{1,0:T(8,128)(2,1)S(1)}, bf16[128,256]{1,0:T(8,128)(2,1)S(1)}, u32[]{:S(2)}, u32[]{:S(2)}) collective-permute-start(bf16[128,256]{1,0:T(8,128)(2,1)S(1)} %get-tuple-element.32.refs_1_), channel_id=1, source_target_pairs={{0,4},{2,6},{4,0},{6,2},{8,12},{10,14},{12,8},{14,10},{16,20},{18,... | collective-permute-start | bytes 196616 | tf_op jit(solution)/shard_map/span_step_0/ppermute | solution.py:456
  5.8 2.6 %collective-permute-start = (bf16[128,256]{1,0:T(8,128)(2,1)S(1)}, bf16[128,256]{1,0:T(8,128)(2,1)S(1)}, u32[]{:S(2)}, u32[]{:S(2)}) collective-permute-start(bf16[128,256]{1,0:T(8,128)(2,1)S(1)} %get-tuple-element.31), channel_id=1, source_target_pairs={{0,16},{2,18},{4,20},{6,22},{8,24},{10,26},{12,28},{14,30},{16,0},... | collective-permute-start | bytes 196616 | tf_op jit(solution)/shard_map/prior_step_0/ppermute | solution.py:456
  8.4 1.5 %collective-permute-start.12 = (bf16[256,1024]{1,0:T(8,128)(2,1)S(1)}, bf16[256,1024]{1,0:T(8,128)(2,1)S(1)}, u32[]{:S(2)}, u32[]{:S(2)}) collective-permute-start(bf16[256,1024]{1,0:T(8,128)(2,1)S(1)} %get-tuple-element.54), channel_id=1, source_target_pairs={{0,1},{1,0},{2,3},{3,2},{4,5},{5,4},{6,7},{7,6},{8,9},{9,8},{10,11... | collective-permute-start | bytes 1572872 | tf_op jit(solution)/shard_map/weights_step/ppermute | solution.py:546
  9.9 1.2 %collective-permute-start.3 = (bf16[256,256]{1,0:T(8,128)(2,1)S(1)}, bf16[256,256]{1,0:T(8,128)(2,1)S(1)}, u32[]{:S(2)}, u32[]{:S(2)}) collective-permute-start(bf16[256,256]{1,0:T(8,128)(2,1)S(1)} %constant_dynamic-update-slice_fusion.2), channel_id=1, source_target_pairs={{0,16},{2,18},{4,20},{6,22},{8,24},{10,26},{12,28},{14,30},{16,0},... | collective-permute-start | bytes 393224 | tf_op jit(solution)/shard_map/span_step_1/ppermute | solution.py:456
  11.2 0.1 collective-permute-done
  11.3 3.3 %collective-permute-start.2 = (bf16[256,256]{1,0:T(8,128)(2,1)S(1)}, bf16[256,256]{1,0:T(8,128)(2,1)S(1)}, u32[]{:S(2)}, u32[]{:S(2)}) collective-permute-start(bf16[256,256]{1,0:T(8,128)(2,1)S(1)} %constant_dynamic-update-slice_fusion), channel_id=1, source_target_pairs={{0,8},{2,10},{4,12},{6,14},{8,0},{10,2},{12,4},{14,6},{16,24},{18,... | collective-permute-start | bytes 393224 | tf_op jit(solution)/shard_map/prior_step_1/ppermute | solution.py:456
  14.6 2.7 %shard_map.185 = (bf16[1024,256]{1,0:T(8,128)(2,1)S(1)}, f32[128,128]{1,0:T(8,128)S(1)}, f32[2,2048]{1,0:T(2,128)S(1)}) custom-call(bf16[128,2048]{1,0:T(8,128)(2,1)S(1)} %get-tuple-element.33.normed, f32[128,128]{1,0:T(8,128)S(1)} %get-tuple-element.34.cosine, f32[128,128]{1,0:T(8,128)S(1)} %get-tuple-element.35.sine, bf16[2048,512]{1,0:T(8,128)(2,1)} %w_query.1, ...), custom_call_target="tpu_custom_call" | custom-call | flops 268435456 | bytes 4194304 | tf_op jit(solution)/shard_map/pallas_call | solution.py:548
  17.2 1.0 %collective-permute-done.3 = bf16[256,256]{1,0:T(8,128)(2,1)S(1)} collective-permute-done((bf16[256,256]{1,0:T(8,128)(2,1)S(1)}, bf16[256,256]{1,0:T(8,128)(2,1)S(1)}, u32[]{:S(2)}, u32[]{:S(2)}) %collective-permute-start.3) | collective-permute-done | bytes 131104 | tf_op jit(solution)/shard_map/span_step_1/ppermute | solution.py:456
  18.3 0.2 collective-permute-done.2
  18.5 0.4 %collective-permute-start.4 = (bf16[512,256]{1,0:T(8,128)(2,1)S(1)}, bf16[512,256]{1,0:T(8,128)(2,1)S(1)}, u32[]{:S(2)}, u32[]{:S(2)}) collective-permute-start(bf16[512,256]{1,0:T(8,128)(2,1)S(1)} %pad_maximum_fusion.1.refs_3_), channel_id=1, source_target_pairs={{0,4},{2,6},{4,0},{6,2},{8,12},{10,14},{12,8},{14,10},{16,20},{18,... | collective-permute-start | bytes 786440 | tf_op jit(solution)/shard_map/prior_last/ppermute | solution.py:456
  18.8 0.9 %collective-permute-start.5 = (bf16[512,256]{1,0:T(8,128)(2,1)S(1)}, bf16[512,256]{1,0:T(8,128)(2,1)S(1)}, u32[]{:S(2)}, u32[]{:S(2)}) collective-permute-start(bf16[512,256]{1,0:T(8,128)(2,1)S(1)} %pad_maximum_fusion.2.refs_4_.refs_0_), channel_id=1, source_target_pairs={{0,8},{2,10},{4,12},{6,14},{8,0},{10,2},{12,4},{14,6},{16,24},{18,... | collective-permute-start | bytes 786440 | tf_op jit(solution)/shard_map/span_last/ppermute | solution.py:456
  19.7 0.1 collective-permute-start.8
  19.8 0.5 %collective-permute-start.9 = (bf16[256,256]{1,0:T(8,128)(2,1)S(1)}, bf16[256,256]{1,0:T(8,128)(2,1)S(1)}, u32[]{:S(2)}, u32[]{:S(2)}) collective-permute-start(bf16[256,256]{1,0:T(8,128)(2,1)S(1)} %get-tuple-element.57), channel_id=1, source_target_pairs={{0,2},{2,0},{4,6},{6,4},{8,10},{10,8},{12,14},{14,12},{16,18},{18,... | collective-permute-start | bytes 393224 | tf_op jit(solution)/shard_map/span_core_near/ppermute | solution.py:456
  20.3 0.8 %collective-permute-done.8.refs_3_.refs_2_ = bf16[256,256]{1,0:T(8,128)(2,1)S(1)} collective-permute-done((bf16[256,256]{1,0:T(8,128)(2,1)S(1)}, bf16[256,256]{1,0:T(8,128)(2,1)S(1)}, u32[]{:S(2)}, u32[]{:S(2)}) %collective-permute-start.8) | collective-permute-done | bytes 131104 | tf_op jit(solution)/shard_map/span_core_near/ppermute | solution.py:456
  21.1 0.1 collective-permute-start.6
  21.3 0.0 collective-permute-done.9.refs_4_.refs_3_
  21.3 0.3 collective-permute-start.7
  21.7 1.7 %shard_map.186 = (f32[1024,128]{1,0:T(8,128)S(1)}, f32[1024,128]{1,0:T(8,128)S(1)}) custom-call(bf16[1024,256]{1,0:T(8,128)(2,1)S(1)} %get-tuple-element.36.refs_0_, bf16[128,256]{1,0:T(8,128)(2,1)S(1)} %get-tuple-element.32.refs_1_, f32[128,128]{1,0:T(8,128)S(1)} %get-tuple-element.39.refs_2_, bf16[512,256]{1,0:T(8,128)(2,1)S(1)} %pad_maximum_fusion.1.refs_3_, ...), custom_call_target="tpu_custom_call" | custom-call | flops 1000 | bytes 1000 | tf_op jit(solution)/shard_map/pallas_call | solution.py:378
  23.3 1.7 %shard_map.187 = (f32[1024,128]{1,0:T(8,128)S(1)}, f32[1024,128]{1,0:T(8,128)S(1)}) custom-call(bf16[1024,256]{1,0:T(8,128)(2,1)S(1)} %get-tuple-element.36.refs_0_, bf16[256,256]{1,0:T(8,128)(2,1)S(1)} %collective-permute-done.6.refs_1_, bf16[256,256]{1,0:T(8,128)(2,1)S(1)} %collective-permute-done.7.refs_2_, ...), custom_call_target="tpu_custom_call" | custom-call | flops 1000 | bytes 1000 | tf_op jit(solution)/shard_map/pallas_call | solution.py:378
  25.0 0.2 collective-permute-done.5.refs_2_.refs_1_
  25.3 0.1 collective-permute-start.10
  25.4 0.5 %collective-permute-start.13 = (bf16[256,1024]{1,0:T(8,128)(2,1)S(1)}, bf16[256,1024]{1,0:T(8,128)(2,1)S(1)}, u32[]{:S(2)}, u32[]{:S(2)}) collective-permute-start(bf16[256,1024]{1,0:T(8,128)(2,1)S(1)} %collective-permute-done.12.w_near), channel_id=1, source_target_pairs={{0,2},{2,0},{4,6},{6,4},{8,10},{10,8},{12,14},{14,12},{16,18},{18,... | collective-permute-start | bytes 1572872 | tf_op jit(solution)/shard_map/weights_step/ppermute | solution.py:456
  25.8 1.7 %shard_map.188 = (f32[1024,128]{1,0:T(8,128)S(1)}, f32[1024,128]{1,0:T(8,128)S(1)}) custom-call(bf16[1024,256]{1,0:T(8,128)(2,1)S(1)} %get-tuple-element.36.refs_0_, bf16[512,256]{1,0:T(8,128)(2,1)S(1)} %collective-permute-done.4.refs_1_, bf16[512,256]{1,0:T(8,128)(2,1)S(1)} %collective-permute-done.5.refs_2_.refs_1_, ...), custom_call_target="tpu_custom_call" | custom-call | flops 1073741824 | bytes 2621440 | tf_op jit(solution)/shard_map/pallas_call | solution.py:378
  27.5 0.0 copy-start
  27.5 0.0 copy-start.1
  27.5 0.0 copy-start.2
  27.6 1.9 %shard_map.189.mine = bf16[128,512]{1,0:T(8,128)(2,1)S(1)} custom-call(bf16[1024,256]{1,0:T(8,128)(2,1)S(1)} %get-tuple-element.36.refs_0_, bf16[1024,256]{1,0:T(8,128)(2,1)S(1)} %collective-permute-done.10.refs_1_.refs_4_, f32[2,2048]{1,0:T(2,128)S(1)} %get-tuple-element.42.refs_5_.refs_3_.refs_2_, f32[1024,128]{1,0:T(8,128)S(1)} %get-tuple-element.51.refs_3_, ...), custom_call_target="tpu_custom_call" | custom-call | flops 1073741824 | bytes 2621440 | tf_op jit(solution)/shard_map/pallas_call | solution.py:378
  29.4 1.4 %collective-permute-start.11 = (bf16[128,512]{1,0:T(8,128)(2,1)S(1)}, bf16[128,512]{1,0:T(8,128)(2,1)S(1)}, u32[]{:S(2)}, u32[]{:S(2)}) collective-permute-start(bf16[128,512]{1,0:T(8,128)(2,1)S(1)} %shard_map.189.mine), channel_id=1, source_target_pairs={{0,1},{1,0},{2,3},{3,2},{4,5},{5,4},{6,7},{7,6},{8,9},{9,8},{10,11... | collective-permute-start | bytes 393224 | tf_op jit(solution)/shard_map/ppermute | solution.py:605
  30.8 2.6 %shard_map.190 = (bf16[1,128,128]{2,1,0:T(8,128)(2,1)}, bf16[1,128,128]{2,1,0:T(8,128)(2,1)}, f32[128,1024]{1,0:T(8,128)S(1)}) custom-call(s32[16]{0:T(128)S(1)} %copy-done.1, s32[32]{0:T(128)S(1)} %copy-done, s32[16]{0:T(128)S(1)} %copy-done.2, bf16[128,512]{1,0:T(8,128)(2,1)S(1)} %shard_map.189.mine, bf16[512,2048]{1,0:T(8,128)(2,1)} %w_output.3, ...), custom_call_target="tpu_custom_call" | custom-call | flops 134217728 | bytes 2097152 | tf_op jit(solution)/shard_map/pallas_call | solution.py:608
  33.4 1.6 %collective-permute-done.11.peer = bf16[128,512]{1,0:T(8,128)(2,1)S(1)} collective-permute-done((bf16[128,512]{1,0:T(8,128)(2,1)S(1)}, bf16[128,512]{1,0:T(8,128)(2,1)S(1)}, u32[]{:S(2)}, u32[]{:S(2)}) %collective-permute-start.11) | collective-permute-done | bytes 131104 | tf_op jit(solution)/shard_map/ppermute | solution.py:605
  35.0 1.1 %shard_map.191 = f32[128,1024]{1,0:T(8,128)} custom-call(f32[128,1024]{1,0:T(8,128)S(1)} %get-tuple-element.53.partial, bf16[128,512]{1,0:T(8,128)(2,1)S(1)} %collective-permute-done.11.peer, bf16[256,1024]{1,0:T(8,128)(2,1)S(1)} %collective-permute-done.12.w_near, bf16[256,1024]{1,0:T(8,128)(2,1)S(1)} %collective-permute-done.13.w_far), custom_call_target="tpu_custom_call" | custom-call | flops 134217728 | bytes 2097152 | tf_op jit(solution)/shard_map/pallas_call | solution.py:623
  (19 shorter events, 0.2 us)
Async XLA Ops:
  2.8 7.1 %collective-permute-start.1 = (bf16[128,256]{1,0:T(8,128)(2,1)S(1)}, bf16[128,256]{1,0:T(8,128)(2,1)S(1)}, u32[]{:S(2)}, u32[]{:S(2)}) collective-permute-start(bf16[128,256]{1,0:T(8,128)(2,1)S(1)} %get-tuple-element.32.refs_1_), channel_id=1, source_target_pairs={{0,4},{2,6},{4,0},{6,2},{8,12},{10,14},{12,8},{14,10},{16,20},{18,... | collective-permute-start | bytes 196616 | tf_op jit(solution)/shard_map/span_step_0/ppermute | solution.py:456
  5.8 5.5 %collective-permute-start = (bf16[128,256]{1,0:T(8,128)(2,1)S(1)}, bf16[128,256]{1,0:T(8,128)(2,1)S(1)}, u32[]{:S(2)}, u32[]{:S(2)}) collective-permute-start(bf16[128,256]{1,0:T(8,128)(2,1)S(1)} %get-tuple-element.31), channel_id=1, source_target_pairs={{0,16},{2,18},{4,20},{6,22},{8,24},{10,26},{12,28},{14,30},{16,0},... | collective-permute-start | bytes 196616 | tf_op jit(solution)/shard_map/prior_step_0/ppermute | solution.py:456
  8.4 16.9 %collective-permute-start.12 = (bf16[256,1024]{1,0:T(8,128)(2,1)S(1)}, bf16[256,1024]{1,0:T(8,128)(2,1)S(1)}, u32[]{:S(2)}, u32[]{:S(2)}) collective-permute-start(bf16[256,1024]{1,0:T(8,128)(2,1)S(1)} %get-tuple-element.54), channel_id=1, source_target_pairs={{0,1},{1,0},{2,3},{3,2},{4,5},{5,4},{6,7},{7,6},{8,9},{9,8},{10,11... | collective-permute-start | bytes 1572872 | tf_op jit(solution)/shard_map/weights_step/ppermute | solution.py:546
  9.9 8.3 %collective-permute-start.3 = (bf16[256,256]{1,0:T(8,128)(2,1)S(1)}, bf16[256,256]{1,0:T(8,128)(2,1)S(1)}, u32[]{:S(2)}, u32[]{:S(2)}) collective-permute-start(bf16[256,256]{1,0:T(8,128)(2,1)S(1)} %constant_dynamic-update-slice_fusion.2), channel_id=1, source_target_pairs={{0,16},{2,18},{4,20},{6,22},{8,24},{10,26},{12,28},{14,30},{16,0},... | collective-permute-start | bytes 393224 | tf_op jit(solution)/shard_map/span_step_1/ppermute | solution.py:456
  11.3 7.2 %collective-permute-start.2 = (bf16[256,256]{1,0:T(8,128)(2,1)S(1)}, bf16[256,256]{1,0:T(8,128)(2,1)S(1)}, u32[]{:S(2)}, u32[]{:S(2)}) collective-permute-start(bf16[256,256]{1,0:T(8,128)(2,1)S(1)} %constant_dynamic-update-slice_fusion), channel_id=1, source_target_pairs={{0,8},{2,10},{4,12},{6,14},{8,0},{10,2},{12,4},{14,6},{16,24},{18,... | collective-permute-start | bytes 393224 | tf_op jit(solution)/shard_map/prior_step_1/ppermute | solution.py:456
  18.5 6.6 %collective-permute-start.4 = (bf16[512,256]{1,0:T(8,128)(2,1)S(1)}, bf16[512,256]{1,0:T(8,128)(2,1)S(1)}, u32[]{:S(2)}, u32[]{:S(2)}) collective-permute-start(bf16[512,256]{1,0:T(8,128)(2,1)S(1)} %pad_maximum_fusion.1.refs_3_), channel_id=1, source_target_pairs={{0,4},{2,6},{4,0},{6,2},{8,12},{10,14},{12,8},{14,10},{16,20},{18,... | collective-permute-start | bytes 786440 | tf_op jit(solution)/shard_map/prior_last/ppermute | solution.py:456
  18.8 6.4 %collective-permute-start.5 = (bf16[512,256]{1,0:T(8,128)(2,1)S(1)}, bf16[512,256]{1,0:T(8,128)(2,1)S(1)}, u32[]{:S(2)}, u32[]{:S(2)}) collective-permute-start(bf16[512,256]{1,0:T(8,128)(2,1)S(1)} %pad_maximum_fusion.2.refs_4_.refs_0_), channel_id=1, source_target_pairs={{0,8},{2,10},{4,12},{6,14},{8,0},{10,2},{12,4},{14,6},{16,24},{18,... | collective-permute-start | bytes 786440 | tf_op jit(solution)/shard_map/span_last/ppermute | solution.py:456
  19.7 1.4 %collective-permute-start.8 = (bf16[256,256]{1,0:T(8,128)(2,1)S(1)}, bf16[256,256]{1,0:T(8,128)(2,1)S(1)}, u32[]{:S(2)}, u32[]{:S(2)}) collective-permute-start(bf16[256,256]{1,0:T(8,128)(2,1)S(1)} %get-tuple-element.58), channel_id=1, source_target_pairs={{0,2},{2,0},{4,6},{6,4},{8,10},{10,8},{12,14},{14,12},{16,18},{18,... | collective-permute-start | bytes 393224 | tf_op jit(solution)/shard_map/span_core_near/ppermute | solution.py:456
  19.8 1.5 %collective-permute-start.9 = (bf16[256,256]{1,0:T(8,128)(2,1)S(1)}, bf16[256,256]{1,0:T(8,128)(2,1)S(1)}, u32[]{:S(2)}, u32[]{:S(2)}) collective-permute-start(bf16[256,256]{1,0:T(8,128)(2,1)S(1)} %get-tuple-element.57), channel_id=1, source_target_pairs={{0,2},{2,0},{4,6},{6,4},{8,10},{10,8},{12,14},{14,12},{16,18},{18,... | collective-permute-start | bytes 393224 | tf_op jit(solution)/shard_map/span_core_near/ppermute | solution.py:456
  21.1 2.2 %collective-permute-start.6 = (bf16[256,256]{1,0:T(8,128)(2,1)S(1)}, bf16[256,256]{1,0:T(8,128)(2,1)S(1)}, u32[]{:S(2)}, u32[]{:S(2)}) collective-permute-start(bf16[256,256]{1,0:T(8,128)(2,1)S(1)} %get-tuple-element.60), channel_id=1, source_target_pairs={{0,2},{2,0},{4,6},{6,4},{8,10},{10,8},{12,14},{14,12},{16,18},{18,... | collective-permute-start | bytes 393224 | tf_op jit(solution)/shard_map/prior_core_near/ppermute | solution.py:456
  21.3 2.0 %collective-permute-start.7 = (bf16[256,256]{1,0:T(8,128)(2,1)S(1)}, bf16[256,256]{1,0:T(8,128)(2,1)S(1)}, u32[]{:S(2)}, u32[]{:S(2)}) collective-permute-start(bf16[256,256]{1,0:T(8,128)(2,1)S(1)} %get-tuple-element.59), channel_id=1, source_target_pairs={{0,2},{2,0},{4,6},{6,4},{8,10},{10,8},{12,14},{14,12},{16,18},{18,... | collective-permute-start | bytes 393224 | tf_op jit(solution)/shard_map/prior_core_near/ppermute | solution.py:456
  25.3 2.3 %collective-permute-start.10 = (bf16[1024,256]{1,0:T(8,128)(2,1)S(1)}, bf16[1024,256]{1,0:T(8,128)(2,1)S(1)}, u32[]{:S(2)}, u32[]{:S(2)}) collective-permute-start(bf16[1024,256]{1,0:T(8,128)(2,1)S(1)} %pad_maximum_fusion), channel_id=1, source_target_pairs={{0,2},{2,0},{4,6},{6,4},{8,10},{10,8},{12,14},{14,12},{16,18},{18,... | collective-permute-start | bytes 1572872 | tf_op jit(solution)/shard_map/core_far/ppermute | solution.py:456
  25.4 8.0 %collective-permute-start.13 = (bf16[256,1024]{1,0:T(8,128)(2,1)S(1)}, bf16[256,1024]{1,0:T(8,128)(2,1)S(1)}, u32[]{:S(2)}, u32[]{:S(2)}) collective-permute-start(bf16[256,1024]{1,0:T(8,128)(2,1)S(1)} %collective-permute-done.12.w_near), channel_id=1, source_target_pairs={{0,2},{2,0},{4,6},{6,4},{8,10},{10,8},{12,14},{14,12},{16,18},{18,... | collective-permute-start | bytes 1572872 | tf_op jit(solution)/shard_map/weights_step/ppermute | solution.py:456
  27.5 3.3 %copy-start = (s32[32]{0:T(128)S(1)}, s32[32]{0:T(128)}, u32[]{:S(2)}) copy-start(s32[32]{0:T(128)} %order.5) | copy-start | bytes 388
  27.5 3.3 %copy-start.1 = (s32[16]{0:T(128)S(1)}, s32[16]{0:T(128)}, u32[]{:S(2)}) copy-start(s32[16]{0:T(128)} %dest.1) | copy-start | bytes 196
  27.5 3.3 %copy-start.2 = (s32[16]{0:T(128)S(1)}, s32[16]{0:T(128)}, u32[]{:S(2)}) copy-start(s32[16]{0:T(128)} %constant.8.clone.where) | copy-start | bytes 196
  29.4 5.6 %collective-permute-start.11 = (bf16[128,512]{1,0:T(8,128)(2,1)S(1)}, bf16[128,512]{1,0:T(8,128)(2,1)S(1)}, u32[]{:S(2)}, u32[]{:S(2)}) collective-permute-start(bf16[128,512]{1,0:T(8,128)(2,1)S(1)} %shard_map.189.mine), channel_id=1, source_target_pairs={{0,1},{1,0},{2,3},{3,2},{4,5},{5,4},{6,7},{7,6},{8,9},{9,8},{10,11... | collective-permute-start | bytes 393224 | tf_op jit(solution)/shard_map/ppermute | solution.py:605
